TPU v7x, 128 devices: a whole 4x4x4 slice. The times are simulated.
128 devices in a mesh: rep: 32 (over y, x, z_lo), grp: 4 (over z_hi, core).
Axes of the slice: x: 4, y: 4, z: 4 (z_hi: 2, z_lo: 2; z = z_hi * 2 + z_lo), core: 2. Of those that a mesh axis runs over, the one named last changes fastest.
Arguments:
- block_input: bfloat16 [32, 1024, 1088], P('rep', 'grp'), may hold values from -6 to 6
- segment_ids: int32 [32, 1024], P('rep'), may hold values from 0 to 2, as said below
- attn_gain: bfloat16 [1088], P('grp'), may hold values from 0.5 to 1.5
- attn_shift: bfloat16 [1088], P('grp'), may hold values from -1.75 to 1.75
- w_qkv: bfloat16 [1088, 3264], P('grp'), may hold values from -0.1875 to 0.1875
- bias_query: bfloat16 [1088], P('grp'), may hold values from -1.75 to 1.75
- bias_value: bfloat16 [1088], P('grp'), may hold values from -1.75 to 1.75
- w_out: bfloat16 [1088, 1088], P('grp'), may hold values from -0.5 to 0.5
- bias_out: bfloat16 [1088], P('grp'), may hold values from -1.75 to 1.75
- mlp_gain: bfloat16 [1088], P('grp'), may hold values from 0.5 to 1.5
- mlp_shift: bfloat16 [1088], P('grp'), may hold values from -1.75 to 1.75
- w_up: bfloat16 [1088, 4352], P('grp'), may hold values from -0.1875 to 0.1875
- bias_up: bfloat16 [4352], P('grp'), may hold values from -1.75 to 1.75
- w_down: bfloat16 [4352, 1088], P('grp'), may hold values from -0.09375 to 0.09375
- bias_down: bfloat16 [1088], P('grp'), may hold values from -1.75 to 1.75
- cotangent: bfloat16 [32, 1024, 1088], P('rep', 'grp'), may hold values from -6 to 6
Outputs:
- block_output: float32 [32, 1024, 1088], P('rep', 'grp')
- grad_input: float32 [32, 1024, 1088], P('rep', 'grp')
- grad_attn_gain: float32 [1088], P('grp')
- grad_attn_shift: float32 [1088], P('grp')
- grad_w_qkv: float32 [1088, 3264], P('grp')
- grad_bias_query: float32 [1088], P('grp')
- grad_bias_value: float32 [1088], P('grp')
- grad_w_out: float32 [1088, 1088], P('grp')
- grad_bias_out: float32 [1088], P('grp')
- grad_mlp_gain: float32 [1088], P('grp')
- grad_mlp_shift: float32 [1088], P('grp')
- grad_w_up: float32 [1088, 4352], P('grp')
- grad_bias_up: float32 [4352], P('grp')
- grad_w_down: float32 [4352, 1088], P('grp')
- grad_bias_down: float32 [1088], P('grp')
Inputs may be any that keep to these rules, and one draw needn't show every extreme that they name: `segment_ids`: in each row the first document holds fewer than 128 tokens, the second runs until fewer than 128 tokens remain, and the third holds the rest; numbers never fall along a row.
All inputs are finite; a program needn't handle non-finite values.
Results may differ from a plain program's by a relative error of at most 0.015.
Values may be sent and summed in bfloat16 or wider, within the bound.
No kernel may reach another device: no remote copies, remote signals or barrier semaphores. Data moves between devices by JAX's collectives and lax.ppermute only.
A program may use at most 192 MiB of HBM per device.

v0:
```python
import functools

import jax
import jax.numpy as jnp
from jax import lax
from jax.experimental import pallas as pl
from jax.experimental.pallas import tpu as pltpu
from jax.sharding import Mesh
from jax.sharding import PartitionSpec as P

D = 1088
HEADS = 17
HEAD = 64
QUART = 272
SLICE = 68
PAD = 72
VECTOR = 204
AXES = ("y", "x", "zl", "zh", "c")
BF = jnp.bfloat16
F32 = jnp.float32


def layer_norm(values, gain, shift):
    centre = values - jnp.mean(values, axis=-1, keepdims=True)
    spread = jnp.mean(centre * centre, axis=-1, keepdims=True)
    return centre * lax.rsqrt(spread + 1e-05) * gain + shift


def exact_gelu(values):
    return jax.nn.gelu(values, approximate=False)


def swap_core(x):
    return lax.ppermute(x, "c", [(0, 1), (1, 0)])


def swap_half(x):
    return lax.ppermute(x, "zh", [(0, 1), (1, 0)])


def swap_near(x):
    return lax.ppermute(x, "zl", [(0, 1), (1, 0)])


def swap_far(x):
    return lax.ppermute(x, ("zl", "zh"), [(0, 3), (3, 0), (1, 2), (2, 1)])


def depth_sum(values, zh):
    mine = jnp.where(zh == 0, values[0], values[1]).astype(F32)
    other = jnp.where(zh == 0, values[1], values[0])
    near = (mine + swap_far(other).astype(F32)).astype(BF)
    return (near.astype(F32) + swap_near(near).astype(F32)).astype(BF)


def assemble_kernel(spots, *refs):
    *parts, out, sems = refs
    rows = out.shape[0] // 4
    rank = lax.axis_index("zh") * 2 + lax.axis_index("c")
    quarter = lax.axis_index("y") % 2 * 2 + lax.axis_index("x") % 2
    copies = []
    for ref, (flip, start, turn, size) in zip(parts, spots):
        at = jnp.bitwise_xor(rank, flip) * rows + start
        if turn is not None:
            at = at + jnp.bitwise_xor(quarter, turn) * size
        copy = pltpu.make_async_copy(
            ref.at[pl.ds(0, size)],
            out.at[pl.ds(pl.multiple_of(at, 16), size)],
            sems.at[len(copies)],
        )
        copy.start()
        copies.append(copy)
    for copy in copies:
        copy.wait()


def assemble(rows, parts, spots):
    columns = parts[0].shape[1]
    return pl.pallas_call(
        functools.partial(assemble_kernel, spots),
        out_shape=jax.ShapeDtypeStruct((rows * 4, columns), BF),
        in_specs=[pl.BlockSpec(memory_space=pltpu.VMEM)] * len(parts),
        out_specs=pl.BlockSpec(memory_space=pl.ANY),
        scratch_shapes=[pltpu.SemaphoreType.DMA((len(parts),))],
        compiler_params=pltpu.CompilerParams(vmem_limit_bytes=24 * 2**20),
        cost_estimate=pl.CostEstimate(
            flops=0, bytes_accessed=rows * columns * 16, transcendentals=0
        ),
    )(*parts)


def dot_nt(left, right):
    return lax.dot_general(left, right, (((1,), (1,)), ((), ())), preferred_element_type=F32)


def dot_tn(left, right):
    return lax.dot_general(left, right, (((0,), (0,)), ((), ())), preferred_element_type=F32)


def attend_forward_kernel(q_ref, k_ref, v_ref, mask_ref, mixed_ref, total_ref):
    mask = mask_ref[...]
    queries, keys, values = q_ref[...], k_ref[...], v_ref[...]
    mixed, totals = [], []
    for head in range(2):
        lanes = slice(head * HEAD, (head + 1) * HEAD)
        scores = dot_nt(queries[:, lanes], keys[:, lanes]) * 0.125 + mask
        highest = jnp.max(scores, axis=1, keepdims=True)
        powers = jnp.exp(scores - highest)
        total = jnp.sum(powers, axis=1, keepdims=True)
        probs = (powers * (1.0 / total)).astype(BF)
        value = jnp.dot(probs, values[:, lanes], preferred_element_type=F32)
        mixed.append(value)
        totals.append(jnp.broadcast_to(highest + jnp.log(total), value.shape))
    mixed_ref[...] = jnp.concatenate(mixed, axis=1).astype(BF)
    total_ref[...] = jnp.concatenate(totals, axis=1)


def attend_backward_kernel(
    q_ref, k_ref, v_ref, mask_ref, total_ref, d_mixed_ref, dq_ref, keep_ref, send_ref
):
    mask = mask_ref[...]
    queries, keys, values = q_ref[...], k_ref[...], v_ref[...]
    totals, d_mixed = total_ref[...], d_mixed_ref[...]
    d_query, d_key, d_value = [], [], []
    for head in range(2):
        lanes = slice(head * HEAD, (head + 1) * HEAD)
        query, key, upstream = queries[:, lanes], keys[:, lanes], d_mixed[:, lanes]
        scores = dot_nt(query, key) * 0.125 + mask
        probs = jnp.exp(scores - totals[:, lanes][:, :1])
        weighted = probs * dot_nt(upstream, values[:, lanes])
        centred = jnp.sum(weighted, axis=1, keepdims=True)
        d_scores = (weighted - probs * centred).astype(BF)
        d_query.append(jnp.dot(d_scores, key, preferred_element_type=F32) * 0.125)
        d_key.append(dot_tn(d_scores, query) * 0.125)
        d_value.append(dot_tn(probs.astype(BF), upstream))
    dq_ref[...] = jnp.concatenate(d_query, axis=1).astype(BF)
    rows = dq_ref.shape[0]
    for at, parts in enumerate((d_key, d_value)):
        whole = jnp.concatenate(parts, axis=1).astype(BF)
        keep_ref[0, at] = whole[:rows]
        send_ref[0, at] = whole[rows : 2 * rows]
        keep_ref[1, at] = whole[2 * rows : 3 * rows]
        send_ref[1, at] = whole[3 * rows :]


def pair_spec(rows):
    return pl.BlockSpec((rows, 2 * HEAD), lambda at: (0, at))


def attend_forward(queries, keys, values, mask):
    rows, length = mask.shape
    return pl.pallas_call(
        attend_forward_kernel,
        grid=((HEADS + 1) // 2,),
        out_shape=(
            jax.ShapeDtypeStruct((rows, D), BF),
            jax.ShapeDtypeStruct((rows, D), F32),
        ),
        in_specs=[
            pair_spec(rows),
            pair_spec(length),
            pair_spec(length),
            pl.BlockSpec(mask.shape, lambda at: (0, 0)),
        ],
        out_specs=(pair_spec(rows), pair_spec(rows)),
        compiler_params=pltpu.CompilerParams(vmem_limit_bytes=32 * 2**20),
        cost_estimate=pl.CostEstimate(
            flops=4 * rows * length * D,
            bytes_accessed=24 * rows * D,
            transcendentals=HEADS * rows * length,
        ),
    )(queries, keys, values, mask)


def attend_backward(queries, keys, values, mask, totals, d_mixed):
    rows, length = mask.shape
    both = jax.ShapeDtypeStruct((2, 2, rows, D), BF)
    both_spec = pl.BlockSpec((2, 2, rows, 2 * HEAD), lambda at: (0, 0, 0, at))
    return pl.pallas_call(
        attend_backward_kernel,
        grid=((HEADS + 1) // 2,),
        out_shape=(jax.ShapeDtypeStruct((rows, D), BF), both, both),
        in_specs=[
            pair_spec(rows),
            pair_spec(length),
            pair_spec(length),
            pl.BlockSpec(mask.shape, lambda at: (0, 0)),
            pair_spec(rows),
            pair_spec(rows),
        ],
        out_specs=(pair_spec(rows), both_spec, both_spec),
        compiler_params=pltpu.CompilerParams(vmem_limit_bytes=32 * 2**20),
        cost_estimate=pl.CostEstimate(
            flops=10 * rows * length * D,
            bytes_accessed=48 * rows * D,
            transcendentals=HEADS * rows * length,
        ),
    )(queries, keys, values, mask, totals, d_mixed)


def weight_grad_kernel(left_ref, right_ref, out_ref):
    left = left_ref[0]
    pieces = left.shape[1] // SLICE
    empty = jnp.zeros((PAD - SLICE, D), BF)
    for at in range(right_ref.shape[1] // D):
        product = lax.dot_general(
            left,
            right_ref[:, at * D : (at + 1) * D],
            (((0,), (0,)), ((), ())),
            preferred_element_type=F32,
        )
        for piece in range(pieces):
            part = product[piece * SLICE : (piece + 1) * SLICE].astype(BF)
            out_ref[at * pieces + piece, 0] = jnp.concatenate([part, empty])


def weight_grad(left, right):
    _, tokens, width = left.shape
    pieces = right.shape[1] // D * (width // SLICE)
    return pl.pallas_call(
        weight_grad_kernel,
        grid=(2,),
        out_shape=jax.ShapeDtypeStruct((pieces, 2, PAD, D), BF),
        in_specs=[
            pl.BlockSpec((1, tokens, width), lambda at: (at, 0, 0)),
            pl.BlockSpec(right.shape, lambda at: (0, 0)),
        ],
        out_specs=pl.BlockSpec((pieces, 1, PAD, D), lambda at: (0, at, 0, 0)),
        compiler_params=pltpu.CompilerParams(vmem_limit_bytes=48 * 2**20),
        cost_estimate=pl.CostEstimate(
            flops=4 * tokens * width * right.shape[1],
            bytes_accessed=2 * left.size + 2 * right.size + 2 * pieces * 2 * PAD * D,
            transcendentals=0,
        ),
    )(left, right)


def unpack_kernel(in_ref, out_ref):
    count, across = out_ref.shape[0] // SLICE, out_ref.shape[1] // D
    for at in range(across):
        for piece in range(count):
            part = in_ref[at * count + piece].astype(F32)[:SLICE]
            out_ref[piece * SLICE : (piece + 1) * SLICE, at * D : (at + 1) * D] = part


def unpack(pieces, rows):
    columns = pieces.shape[0] * SLICE // rows * D
    return pl.pallas_call(
        unpack_kernel,
        out_shape=jax.ShapeDtypeStruct((rows, columns), F32),
        in_specs=[pl.BlockSpec(memory_space=pltpu.VMEM)],
        out_specs=pl.BlockSpec(memory_space=pltpu.VMEM),
        compiler_params=pltpu.CompilerParams(vmem_limit_bytes=24 * 2**20),
        cost_estimate=pl.CostEstimate(
            flops=0, bytes_accessed=pieces.size * 6, transcendentals=0
        ),
    )(pieces)


def gather_direct(shard):
    far = swap_far(shard)
    return shard, swap_core(shard), far, swap_core(far)


def swap_pair(x, axis):
    return lax.ppermute(x, axis, [(0, 1), (1, 0), (2, 3), (3, 2)])


def gather_quarters(shard):
    across, down = lax.axis_index("x") % 2, lax.axis_index("y") % 2
    quarter = down * 2 + across
    main = shard[:256].reshape(4, 64, shard.shape[1])
    piece = lax.dynamic_index_in_dim(main, quarter, 0, keepdims=False)
    got = swap_far(jnp.concatenate([piece, shard[256:]]))
    mine, rest = got[:64], got[64:]
    by_x, by_y = swap_pair(mine, "x"), swap_pair(mine, "y")
    last = jnp.concatenate([swap_pair(by_y[:32], "x"), swap_pair(by_x[32:], "y")])
    pieces = [mine, by_x, by_y, last]
    return pieces + [rest], [swap_core(piece) for piece in pieces] + [swap_core(rest)]


def gather_spread(shard, spot):
    unit = shard.shape[0] // 17
    main = shard[: 16 * unit].reshape(16, unit, shard.shape[1])
    tail = shard[16 * unit :]
    piece = lax.dynamic_index_in_dim(main, spot, 0, keepdims=False)
    got = swap_far(jnp.concatenate([piece, tail]))
    far = lax.all_gather(got[:unit], ("y", "x"), axis=0, tiled=True)
    rest = got[unit:]
    rows, main = shard.shape[0], 16 * unit
    return assemble(
        rows,
        (shard, swap_core(shard), far, rest, swap_core(far), swap_core(rest)),
        (
            (0, 0, None, rows),
            (1, 0, None, rows),
            (2, 0, None, main),
            (2, main, None, unit),
            (3, 0, None, main),
            (3, main, None, unit),
        ),
    )


def body(
    block_input,
    segment_ids,
    attn_gain,
    attn_shift,
    w_qkv,
    bias_query,
    bias_value,
    w_out,
    bias_out,
    mlp_gain,
    mlp_shift,
    w_up,
    bias_up,
    w_down,
    bias_down,
    cotangent,
):
    core, zh = lax.axis_index("c"), lax.axis_index("zh")
    rank = zh * 2 + core
    spot = lax.axis_index("y") * 4 + lax.axis_index("x")
    small = jnp.concatenate(
        [
            attn_gain,
            attn_shift,
            bias_query,
            bias_value,
            bias_out,
            mlp_gain,
            mlp_shift,
            bias_up,
            bias_down,
        ]
    )
    small = jnp.pad(small[None], ((0, 15), (0, 0)))
    rows = block_input.shape[1]
    own_tokens = block_input[0]
    with_small = jnp.concatenate([w_qkv, small])
    far_parts, across_parts = gather_quarters(with_small)
    beside = swap_core(with_small)
    half_tokens = swap_half(own_tokens)
    tokens = [own_tokens, swap_core(own_tokens), half_tokens, swap_core(half_tokens)]
    turns = [(0, 0, 64), (0, 1, 64), (0, 2, 64), (0, 3, 64), (256, None, 16)]
    full_qkv = assemble(
        QUART,
        (with_small, beside, *far_parts, *across_parts),
        ((0, 0, None, QUART), (1, 0, None, QUART))
        + tuple((2, *turn) for turn in turns)
        + tuple((3, *turn) for turn in turns),
    )
    smalls = [
        value.astype(F32) for value in (small[0], beside[QUART], far_parts[4][16], across_parts[4][16])
    ]
    full_out = assemble(
        QUART, gather_direct(w_out), tuple((flip, 0, None, QUART) for flip in range(4))
    )
    full_up = gather_spread(w_up, spot)
    full_down = gather_spread(w_down, spot)

    ordered = []
    for index in range(4):
        value = smalls[index]
        for at in range(1, 4):
            value = jnp.where(rank == at, smalls[index ^ at], value)
        ordered.append(value)
    ordered = jnp.stack(ordered)

    def vector(start, size):
        return ordered[:, start : start + size].reshape(-1)

    gain_one, shift_one, query_bias, value_bias, out_bias, gain_two, shift_two = (
        vector(QUART * index, QUART) for index in range(7)
    )
    up_bias = vector(7 * QUART, D)
    down_bias = vector(11 * QUART, QUART)

    segments = segment_ids[0]
    upstream = cotangent[0]

    hidden_in = own_tokens.astype(F32)
    normed_parts = [
        layer_norm(part.astype(F32), gain_one, shift_one).astype(BF) for part in tokens
    ]
    normed = normed_parts[0]
    normed_all = jnp.concatenate(normed_parts)
    queries = (
        jnp.dot(normed, full_qkv[:, :D], preferred_element_type=F32) + query_bias
    ).astype(BF)
    keys = jnp.dot(normed_all, full_qkv[:, D : 2 * D], preferred_element_type=F32).astype(BF)
    values = jnp.dot(normed_all, full_qkv[:, 2 * D :], preferred_element_type=F32)
    values = (values + value_bias).astype(BF)
    query_places = rank * rows + jnp.arange(rows)
    starts = [jnp.bitwise_xor(rank, flip) * rows for flip in range(4)]
    key_places = jnp.concatenate([start + jnp.arange(rows) for start in starts])
    key_segments = jnp.concatenate(
        [lax.dynamic_slice_in_dim(segments, start, rows) for start in starts]
    )
    allowed = (key_segments[:rows, None] == key_segments[None, :]) & (
        query_places[:, None] >= key_places[None, :]
    )
    mask = jnp.where(allowed, 0.0, -1e30).astype(F32)
    mixed, log_total = attend_forward(queries, keys, values, mask)
    middle = hidden_in + jnp.dot(mixed, full_out, preferred_element_type=F32) + out_bias
    normed_two = layer_norm(middle, gain_two, shift_two).astype(BF)
    upper = jnp.dot(normed_two, full_up, preferred_element_type=F32) + up_bias
    activated = exact_gelu(upper).astype(BF)
    block_output = middle + jnp.dot(activated, full_down, preferred_element_type=F32) + down_bias

    def paired(value):
        return jnp.concatenate([value, swap_core(value)])

    def paired_columns(value):
        width = value.shape[1] // 4
        blocks = [value[:, at * width : (at + 1) * width] for at in range(4)]
        even, odd = jnp.stack([blocks[0], blocks[2]]), jnp.stack([blocks[1], blocks[3]])
        mine = jnp.where(core == 0, even, odd)
        other = jnp.where(core == 0, odd, even)
        return jnp.concatenate([mine, swap_core(other)], axis=1)

    def across(value):
        rest = value.shape[2]
        value = lax.psum_scatter(
            value.reshape(32 * rest, D), ("y", "x"), scatter_dimension=0, tiled=True
        )
        return value.reshape(2, rest, D)

    upstream_wide = upstream.astype(F32)
    upstream_pair = paired(upstream)
    grad_down_bias = jnp.sum(upstream_wide, axis=0)
    down_part = across(weight_grad(paired_columns(activated), upstream_pair))

    d_activated = jnp.dot(upstream, full_down.T, preferred_element_type=F32)
    gelu_back = jax.vjp(exact_gelu, upper)[1]
    d_upper = gelu_back(d_activated)[0].astype(BF)
    grad_up_bias = jnp.sum(d_upper.astype(F32), axis=0)
    grad_up = weight_grad(paired_columns(normed_two), paired(d_upper))
    down_part, grad_up = lax.optimization_barrier((down_part, grad_up))
    up_part = across(grad_up)

    d_normed_two = jnp.dot(d_upper, full_up.T, preferred_element_type=F32)
    norm_two_back = jax.vjp(layer_norm, middle, gain_two, shift_two)[1]
    d_middle_part, grad_gain_two, grad_shift_two = norm_two_back(d_normed_two)
    d_middle = upstream_wide + d_middle_part
    d_attended = d_middle.astype(BF)
    grad_out_bias = jnp.sum(d_attended.astype(F32), axis=0)
    grad_out = weight_grad(paired_columns(mixed), paired(d_attended))

    d_mixed = jnp.dot(d_attended, full_out.T, preferred_element_type=F32).astype(BF)
    d_queries, d_both, d_beside = attend_backward(
        queries, keys, values, mask, log_total, d_mixed
    )
    d_beside = swap_core(d_beside)
    d_half = swap_half((d_both[1].astype(F32) + d_beside[1].astype(F32)).astype(BF))
    d_both = d_both[0].astype(F32) + d_beside[0].astype(F32) + d_half.astype(F32)
    d_both = d_both.astype(BF)
    d_project = jnp.concatenate([d_queries, d_both[0], d_both[1]], axis=1)
    grad_query_bias = jnp.sum(d_queries.astype(F32), axis=0)
    grad_value_bias = jnp.sum(d_both[1].astype(F32), axis=0)
    grad_qkv = weight_grad(paired_columns(normed), paired(d_project))

    d_normed = jnp.dot(d_project, full_qkv.T, preferred_element_type=F32)
    norm_one_back = jax.vjp(layer_norm, hidden_in, gain_one, shift_one)[1]
    d_input_part, grad_gain_one, grad_shift_one = norm_one_back(d_normed)
    grad_input = d_middle + d_input_part

    vectors = jnp.concatenate(
        [
            value.reshape(4, -1)
            for value in (
                grad_gain_one,
                grad_shift_one,
                grad_query_bias,
                grad_value_bias,
                grad_out_bias,
                grad_gain_two,
                grad_shift_two,
                grad_down_bias,
                grad_up_bias,
            )
        ],
        axis=1,
    )
    even, odd = vectors[0::2], vectors[1::2]
    mine = jnp.where(core == 0, even, odd)
    other = jnp.where(core == 0, odd, even)
    mine = (mine + swap_core(other.astype(BF)).astype(F32)).astype(BF)
    mine = mine.reshape(2, 16, VECTOR).transpose(1, 0, 2)[:, :, None]

    grad_attn = jnp.concatenate([grad_qkv, grad_out])
    grad_attn = lax.dynamic_update_slice(grad_attn, mine, (0, 0, SLICE, 0))
    up_part, grad_attn = lax.optimization_barrier((up_part, grad_attn))
    early = depth_sum(jnp.concatenate([down_part, up_part], axis=1), zh)
    attn_part = depth_sum(lax.optimization_barrier(across(grad_attn)), zh)
    parts = lax.all_gather(
        jnp.concatenate([early, attn_part]).reshape(3, PAD, D), ("y", "x"), axis=0, tiled=False
    ).reshape(16, 3, PAD, D)
    grad_down = unpack(parts[:, 0], D)
    grad_up = unpack(parts[:, 1], QUART)
    grad_qkv = unpack(parts[:12, 2], QUART)
    grad_out = unpack(parts[12:, 2], QUART)
    vectors = parts[:, 2, SLICE, :VECTOR].reshape(-1).astype(F32)

    def owned(start, size):
        return vectors[start : start + size]

    return (
        block_output[None],
        grad_input[None],
        owned(0, QUART),
        owned(QUART, QUART),
        grad_qkv,
        owned(2 * QUART, QUART),
        owned(3 * QUART, QUART),
        grad_out,
        owned(4 * QUART, QUART),
        owned(5 * QUART, QUART),
        owned(6 * QUART, QUART),
        grad_up,
        owned(8 * QUART, D),
        grad_down,
        owned(7 * QUART, QUART),
    )


def solution(mesh):
    grid = Mesh(mesh.devices.reshape(4, 4, 2, 2, 2), AXES)
    rep, grp = ("y", "x", "zl"), ("zh", "c")
    tokens = P(rep, grp, None)
    vector, matrix = P(grp), P(grp, None)
    params = (
        vector,
        vector,
        matrix,
        vector,
        vector,
        matrix,
        vector,
        vector,
        vector,
        matrix,
        vector,
        matrix,
        vector,
    )
    return jax.shard_map(
        body,
        mesh=grid,
        in_specs=(tokens, P(rep, None)) + params + (tokens,),
        out_specs=(tokens, tokens) + params,
        check_vma=False,
    )
```

profile of v0, /device:TPU:0, one launch (start us, length us, event | category | flops | bytes accessed | tf_op | source)
XLA Modules:
  0.0 574.8 jit_solution(4941239245155786617)
XLA Ops:
  8.9 4.2 collective-permute-start.18
  13.1 6.7 %collective-permute-done.18 = bf16[32,4352]{1,0:T(8,128)(2,1)S(1)} collective-permute-done((bf16[32,4352]{1,0:T(8,128)(2,1)S(1)}, bf16[32,4352]{1,0:T(8,128)(2,1)S(1)}, u32[]{:S(2)}, u32[]{:S(2)}) %collective-permute-start.18) | collective-permute-done | bytes 278560 | tf_op jit(solution)/shard_map/ppermute | solution.py:46
  24.0 2.9 fusion.15.refs_0_
  36.6 20.3 %collective-permute-done.22 = bf16[128,1088]{1,0:T(8,128)(2,1)S(1)} collective-permute-done((bf16[128,1088]{1,0:T(8,128)(2,1)}, bf16[128,1088]{1,0:T(8,128)(2,1)S(1)}, u32[]{:S(2)}, u32[]{:S(2)}) %collective-permute-start.22) | collective-permute-done | bytes 278560 | tf_op jit(solution)/shard_map/ppermute | solution.py:46
  57.0 2.9 collective-permute-start
  66.1 8.8 %collective-permute-done = bf16[96,3264]{1,0:T(8,128)(2,1)} collective-permute-done((bf16[96,3264]{1,0:T(8,128)(2,1)}, bf16[96,3264]{1,0:T(8,128)(2,1)}, u32[]{:S(2)}, u32[]{:S(2)}) %collective-permute-start) | collective-permute-done | bytes 626720 | tf_op jit(solution)/shard_map/ppermute | solution.py:46
  81.4 7.5 %collective-permute-done.4.refs_4_ = bf16[64,3264]{1,0:T(8,128)(2,1)S(1)} collective-permute-done((bf16[64,3264]{1,0:T(8,128)(2,1)S(1)}, bf16[64,3264]{1,0:T(8,128)(2,1)S(1)}, u32[]{:S(2)}, u32[]{:S(2)}) %collective-permute-start.4) | collective-permute-done | bytes 417824 | tf_op jit(solution)/shard_map/ppermute | solution.py:266
  93.5 2.1 copy.101
  98.9 2.5 shard_map.273
  105.9 9.0 %collective-permute-done.6 = bf16[32,3264]{1,0:T(8,128)(2,1)S(1)} collective-permute-done((bf16[32,3264]{1,0:T(8,128)(2,1)S(1)}, bf16[32,3264]{1,0:T(8,128)(2,1)S(1)}, u32[]{:S(2)}, u32[]{:S(2)}) %collective-permute-start.6) | collective-permute-done | bytes 208928 | tf_op jit(solution)/shard_map/ppermute | solution.py:266
  119.5 2.6 fusion.42
  122.9 5.9 %shard_map.271 = bf16[1088,3264]{1,0:T(8,128)(2,1)S(1)} custom-call(bf16[288,3264]{1,0:T(8,128)(2,1)} %fusion.15.refs_0_, bf16[288,3264]{1,0:T(8,128)(2,1)} %collective-permute-done.2.refs_1_, bf16[64,3264]{1,0:T(8,128)(2,1)S(1)} %slice.298.refs_2_, bf16[64,3264]{1,0:T(8,128)(2,1)} %collective-permute-done.3.refs_3_, ...), custom_call_target="tpu_custom_call" | custom-call | bytes 14204928 | tf_op jit(solution)/shard_map/pallas_call | solution.py:79
  128.8 6.4 %add_convert_fusion.v_ref = bf16[1024,1088]{1,0:T(8,128)(2,1)} fusion(bf16[1088,3264]{1,0:T(8,128)(2,1)S(1)} %shard_map.271, f32[1088]{0:T(1024)S(1)} %add.268, bf16[256,1088]{1,0:T(8,128)(2,1)S(1)} %get-tuple-element.160, bf16[256,1088]{1,0:T(8,128)(2,1)S(1)} %get-tuple-element.159, bf16[256,1088]{1,0:T(8,128)(2,1)S(1)} %get-tuple-element.158, ...), kind=kOutput, calls=%fused_computation.4 | convolution fusion | flops 2435448832 | bytes 7102464 | tf_op jit(solution)/shard_map/dot_general | solution.py:394
  135.2 1.8 fusion.10.q_ref
  138.5 6.4 %convolution_convert_fusion.k_ref = bf16[1024,1088]{1,0:T(8,128)(2,1)S(1)} fusion(bf16[1088,3264]{1,0:T(8,128)(2,1)} %copy-done.6, bf16[256,1088]{1,0:T(8,128)(2,1)} %copy-done.60, bf16[256,1088]{1,0:T(8,128)(2,1)} %copy-done.59, bf16[256,1088]{1,0:T(8,128)(2,1)} %copy-done.58, bf16[256,1088]{1,0:T(8,128)(2,1)} %copy-done.54), kind=kOutput, calls=%fused_computation.25 | convolution fusion | flops 2434334720 | bytes 7094272 | tf_op jit(solution)/shard_map/dot_general | solution.py:393
  144.9 15.1 %shard_map.272 = (bf16[256,1088]{1,0:T(8,128)(2,1)S(1)}, f32[256,1088]{1,0:T(8,128)S(1)}) custom-call(bf16[256,1088]{1,0:T(8,128)(2,1)S(1)} %copy-done.31, bf16[1024,1088]{1,0:T(8,128)(2,1)S(1)} %convolution_convert_fusion.k_ref, bf16[1024,1088]{1,0:T(8,128)(2,1)S(1)} %copy-done.25, f32[256,1024]{1,0:T(8,128)S(1)} %copy-done.19), custom_call_target="tpu_custom_call" | custom-call | flops 1140850688 | bytes 6684672 | tf_op jit(solution)/shard_map/pallas_call | solution.py:152
  165.7 3.8 shard_map.274
  169.6 14.6 %multiply_convert_fusion = (bf16[256,4352]{1,0:T(8,128)(2,1)S(1)}, f32[256,4352]{1,0:T(8,128)}, f32[256,4352]{1,0:T(8,128)}) fusion(f32[4352]{0:T(1024)S(1)} %add.293, bf16[256,1088]{1,0:T(8,128)(2,1)S(1)} %add_convert_fusion.3, bf16[1088,4352]{1,0:T(8,128)(2,1)S(1)} %shard_map.274), kind=kOutput, calls=%fused_computation.9 | convolution fusion | flops 2497839104 | bytes 21185536 | tf_op jit(solution)/shard_map/dot_general | solution.py:409
  193.2 2.4 copy.118
  197.1 4.9 shard_map.277
  203.8 4.3 copy.105
  209.5 3.5 collective-permute-done.29
  214.0 4.2 copy.106.refs_4_
  221.6 3.4 shard_map.275
  225.0 3.8 copy-done
  228.8 13.1 %convert_reduce_fusion = (f32[4352]{0:T(1024)S(1)}, bf16[256,4352]{1,0:T(8,128)(2,1)}) fusion(f32[256,4352]{1,0:T(8,128)} %get-tuple-element.102, f32[256,4352]{1,0:T(8,128)} %get-tuple-element.168, bf16[4352,1088]{1,0:T(8,128)(2,1)} %copy-done, bf16[1,256,1088]{1,2,0:T(8,128)(2,1)} %param.31), kind=kOutput, calls=%fused_computation.7 | convolution fusion | flops 2442129152 | bytes 21185536 | tf_op jit(solution)/shard_map/dot_general | solution.py:436
  242.8 5.3 fusion.66
  261.4 21.5 %shard_map.276 = (bf16[256,1088]{1,0:T(8,128)(2,1)S(1)}, bf16[2,2,256,1088]{3,2,1,0:T(8,128)(2,1)S(1)}, bf16[2,2,256,1088]{3,2,1,0:T(8,128)(2,1)S(1)}) custom-call(bf16[256,1088]{1,0:T(8,128)(2,1)S(1)} %copy-done.32, bf16[1024,1088]{1,0:T(8,128)(2,1)S(1)} %copy-done.28, bf16[1024,1088]{1,0:T(8,128)(2,1)S(1)} %copy-done.26, f32[256,1024]{1,0:T(8,128)S(1)} %copy-done.20, ...), custom_call_target="tpu_custom_call" | custom-call | flops 2852126720 | bytes 13369344 | tf_op jit(solution)/shard_map/pallas_call | solution.py:179
  285.1 4.6 copy.111
  289.8 2.6 pad_maximum_fusion.1.right_ref
  292.4 4.8 shard_map.278
  300.1 2.7 fusion.59
  304.2 2.6 fusion.45
  306.8 2.5 copy.114
  311.9 2.0 pad_maximum_fusion.10.left_ref
  314.6 2.1 copy.124
  317.9 2.4 copy.138
  320.2 17.5 %collective-permute-done.26 = bf16[2,256,1088]{1,2,0:T(8,128)(2,1)} collective-permute-done((bf16[2,256,1088]{1,2,0:T(8,128)(2,1)}, bf16[2,256,1088]{1,2,0:T(8,128)(2,1)}, u32[]{:S(2)}, u32[]{:S(2)}) %collective-permute-start.26) | collective-permute-done | bytes 1114144 | tf_op jit(solution)/shard_map/ppermute | solution.py:38
  337.7 2.4 copy.115
  340.1 2.4 fusion.14
  343.8 2.2 slice_bitcast_fusion.8
  346.0 3.7 concatenate.110
  349.7 6.7 %fusion.65 = (f32[1088]{0:T(1024)S(1)}, f32[256,1088]{0,1:T(8,128)}) fusion(bf16[256,3264]{1,0:T(8,128)(2,1)} %concatenate.110, bf16[1088,3264]{1,0:T(8,128)(2,1)} %copy-done.6), kind=kOutput, calls=%fused_computation.215 | convolution fusion | flops 1818508288 | bytes 9892096 | tf_op jit(solution)/shard_map/dot_general | solution.py:465
  356.5 2.7 copy.116
  362.4 3.8 copy.121
  370.1 3.8 copy.122
  373.9 1.8 pad_maximum_fusion.2.right_ref
  375.7 3.9 shard_map.279
  379.6 5.1 pad_maximum_fusion
  384.7 2.1 dynamic_update_slice.3
  387.9 2.5 collective-permute-start.36
  390.4 78.0 %reduce-scatter.14.cloned.1.call-done = bf16[144,1088]{1,0:T(8,128)(2,1)} async-done(((bf16[2304,1088]{1,0:T(8,128)(2,1)}), bf16[144,1088]{1,0:T(8,128)(2,1)}) %reduce-scatter.14.cloned.1.call-update) | async-done | bytes 313360
  469.4 3.0 collective-permute-start.38
  472.8 3.3 collective-permute-done.38
  477.8 4.4 collective-permute-done.37
  485.0 8.7 %fusion.9 = f32[1,256,1088]{2,1,0:T(8,128)} fusion(f32[256,1088]{1,0:T(8,128)S(1)} %copy-done.39, bf16[256,4352]{1,0:T(8,128)(2,1)} %copy-done.56, bf16[4352,1088]{1,0:T(8,128)(2,1)} %copy-done, f32[1088]{0:T(1024)S(1)} %add.297), kind=kOutput, calls=%fused_computation.32 | convolution fusion | flops 2424864768 | bytes 13930752 | tf_op jit(solution)/shard_map/dot_general | solution.py:411
  493.7 2.8 copy.128
  497.2 2.2 add_bitcast_fusion
  499.5 2.6 copy.129
  502.1 49.8 %all-gather.8.cloned.1.call-done = bf16[16,3,72,1088]{3,2,0,1:T(8,128)(2,1)} async-done(((bf16[1,3,72,1088]{3,2,0,1:T(8,128)(2,1)}), bf16[16,3,72,1088]{3,2,0,1:T(8,128)(2,1)}) %all-gather.8.cloned.1.call-update) | async-done | bytes 7520272 | tf_op jit(solution)/shard_map/all_gather | solution.py:498
  556.5 1.9 slice_bitcast_fusion.2.in_ref
  558.4 2.2 shard_map.281
  562.1 2.6 shard_map.284
  564.7 2.8 shard_map.283
  (427 shorter events, 117.6 us)
Async XLA Ops:
  7.2 130.7 %all-gather.4.cloned.1.call-start = ((), (), s32[]{:S(2)}) async-start(), calls=%async_computation.3 | async-start | bytes 2367488 | tf_op jit(solution)/shard_map/all_gather | solution.py:288
  7.3 16.5 %copy-start.75 = (bf16[1088]{0:T(1024)(128)(2,1)S(1)}, bf16[1088]{0:T(1024)(128)(2,1)}, u32[]{:S(2)}) copy-start(bf16[1088]{0:T(1024)(128)(2,1)} %param.28) | copy-start | bytes 6532
  7.3 16.5 %copy-start.87 = (bf16[272]{0:T(512)(128)(2,1)S(1)}, bf16[272]{0:T(512)(128)(2,1)}, u32[]{:S(2)}) copy-start(bf16[272]{0:T(512)(128)(2,1)} %param.18) | copy-start | bytes 1636
  7.3 16.5 %copy-start.88 = (bf16[272]{0:T(512)(128)(2,1)S(1)}, bf16[272]{0:T(512)(128)(2,1)}, u32[]{:S(2)}) copy-start(bf16[272]{0:T(512)(128)(2,1)} %param.19) | copy-start | bytes 1636
  7.3 16.5 %copy-start.89 = (bf16[272]{0:T(512)(128)(2,1)S(1)}, bf16[272]{0:T(512)(128)(2,1)}, u32[]{:S(2)}) copy-start(bf16[272]{0:T(512)(128)(2,1)} %param.21) | copy-start | bytes 1636
  7.3 16.5 %copy-start.90 = (bf16[272]{0:T(512)(128)(2,1)S(1)}, bf16[272]{0:T(512)(128)(2,1)}, u32[]{:S(2)}) copy-start(bf16[272]{0:T(512)(128)(2,1)} %param.22) | copy-start | bytes 1636
  7.3 16.5 %copy-start.91 = (bf16[272]{0:T(512)(128)(2,1)S(1)}, bf16[272]{0:T(512)(128)(2,1)}, u32[]{:S(2)}) copy-start(bf16[272]{0:T(512)(128)(2,1)} %param.24) | copy-start | bytes 1636
  7.3 16.5 %copy-start.92 = (bf16[272]{0:T(512)(128)(2,1)S(1)}, bf16[272]{0:T(512)(128)(2,1)}, u32[]{:S(2)}) copy-start(bf16[272]{0:T(512)(128)(2,1)} %param.25) | copy-start | bytes 1636
  7.3 16.5 %copy-start.93 = (bf16[272]{0:T(512)(128)(2,1)S(1)}, bf16[272]{0:T(512)(128)(2,1)}, u32[]{:S(2)}) copy-start(bf16[272]{0:T(512)(128)(2,1)} %param.26) | copy-start | bytes 1636
  7.3 16.5 %copy-start.94 = (bf16[272]{0:T(512)(128)(2,1)S(1)}, bf16[272]{0:T(512)(128)(2,1)}, u32[]{:S(2)}) copy-start(bf16[272]{0:T(512)(128)(2,1)} %param.30) | copy-start | bytes 1636
  8.9 10.9 %collective-permute-start.18 = (bf16[32,4352]{1,0:T(8,128)(2,1)S(1)}, bf16[32,4352]{1,0:T(8,128)(2,1)S(1)}, u32[]{:S(2)}, u32[]{:S(2)}) collective-permute-start(bf16[32,4352]{1,0:T(8,128)(2,1)S(1)} %pad_maximum_fusion.23), channel_id=1, source_target_pairs={{0,6},{6,0},{2,4},{4,2},{1,7},{7,1},{3,5},{5,3},{8,14},{14,8},{10,... | collective-permute-start | bytes 835592 | tf_op jit(solution)/shard_map/ppermute | solution.py:46
  20.5 183.3 %all-gather.6.cloned.1.call-start = ((), (), s32[]{:S(2)}) async-start(), calls=%async_computation.4 | async-start | bytes 2506752 | tf_op jit(solution)/shard_map/all_gather | solution.py:288
  20.6 40.1 %collective-permute-start.11 = (bf16[256,1088]{0,1:T(8,128)(2,1)S(1)}, bf16[256,1088]{0,1:T(8,128)(2,1)}, u32[]{:S(2)}, u32[]{:S(2)}) collective-permute-start(bf16[256,1088]{0,1:T(8,128)(2,1)S(1)} %bitcast.145), channel_id=1, source_target_pairs={{0,1},{1,0},{2,3},{3,2},{4,5},{5,4},{6,7},{7,6},{8,9},{9,8},{10,11... | collective-permute-start | bytes 1671176 | tf_op jit(solution)/shard_map/ppermute | solution.py:34
  20.7 42.1 %collective-permute-start.12 = (bf16[256,1088]{0,1:T(8,128)(2,1)S(1)}, bf16[256,1088]{0,1:T(8,128)(2,1)}, u32[]{:S(2)}, u32[]{:S(2)}) collective-permute-start(bf16[256,1088]{0,1:T(8,128)(2,1)S(1)} %bitcast.146), channel_id=1, source_target_pairs={{0,2},{2,0},{1,3},{3,1},{4,6},{6,4},{5,7},{7,5},{8,10},{10,8},{9,1... | collective-permute-start | bytes 1671176 | tf_op jit(solution)/shard_map/ppermute | solution.py:38
  22.3 67.2 %collective-permute-start.15 = (bf16[272,1088]{1,0:T(8,128)(2,1)}, bf16[272,1088]{1,0:T(8,128)(2,1)}, u32[]{:S(2)}, u32[]{:S(2)}) collective-permute-start(bf16[272,1088]{1,0:T(8,128)(2,1)} %refs_0_.3), channel_id=1, source_target_pairs={{0,6},{6,0},{2,4},{4,2},{1,7},{7,1},{3,5},{5,3},{8,14},{14,8},{10,... | collective-permute-start | bytes 1775624 | tf_op jit(solution)/shard_map/ppermute | solution.py:46
  26.9 89.2 %collective-permute-start.2 = (bf16[288,3264]{1,0:T(8,128)(2,1)}, bf16[288,3264]{1,0:T(8,128)(2,1)}, u32[]{:S(2)}, u32[]{:S(2)}) collective-permute-start(bf16[288,3264]{1,0:T(8,128)(2,1)} %fusion.15.refs_0_), channel_id=1, source_target_pairs={{0,1},{1,0},{2,3},{3,2},{4,5},{5,4},{6,7},{7,6},{8,9},{9,8},{10,11... | collective-permute-start | bytes 5640200 | tf_op jit(solution)/shard_map/ppermute | solution.py:34
  29.4 27.6 %collective-permute-start.22 = (bf16[128,1088]{1,0:T(8,128)(2,1)}, bf16[128,1088]{1,0:T(8,128)(2,1)S(1)}, u32[]{:S(2)}, u32[]{:S(2)}) collective-permute-start(bf16[128,1088]{1,0:T(8,128)(2,1)} %pad_maximum_fusion.22), channel_id=1, source_target_pairs={{0,6},{6,0},{2,4},{4,2},{1,7},{7,1},{3,5},{5,3},{8,14},{14,8},{10,... | collective-permute-start | bytes 835592 | tf_op jit(solution)/shard_map/ppermute | solution.py:46
  32.9 86.6 %copy-start.67 = (f32[256]{0:T(256)}, f32[256]{0:T(256)S(1)}, u32[]{:S(2)}) copy-start(f32[256]{0:T(256)S(1)} %broadcast_multiply_fusion.4) | copy-start | bytes 3076
  35.3 84.1 %copy-start.73 = (f32[256]{0:T(256)}, f32[256]{0:T(256)S(1)}, u32[]{:S(2)}) copy-start(f32[256]{0:T(256)S(1)} %fusion.50) | copy-start | bytes 3076
  57.0 18.0 %collective-permute-start = (bf16[96,3264]{1,0:T(8,128)(2,1)}, bf16[96,3264]{1,0:T(8,128)(2,1)}, u32[]{:S(2)}, u32[]{:S(2)}) collective-permute-start(bf16[96,3264]{1,0:T(8,128)(2,1)} %pad_maximum_fusion.12), channel_id=1, source_target_pairs={{0,6},{6,0},{2,4},{4,2},{1,7},{7,1},{3,5},{5,3},{8,14},{14,8},{10,... | collective-permute-start | bytes 1880072 | tf_op jit(solution)/shard_map/ppermute | solution.py:46
  60.6 236.7 %reduce-scatter.10.cloned.1.call-start = ((), (), s32[]{:S(2)}) async-start(), calls=%async_computation.6 | async-start | bytes 5640192
  62.8 26.8 %copy-start.3 = (bf16[272,4352]{1,0:T(8,128)(2,1)S(1)}, bf16[272,4352]{1,0:T(8,128)(2,1)}, u32[]{:S(2)}) copy-start(bf16[272,4352]{1,0:T(8,128)(2,1)} %refs_0_.4) | copy-start | bytes 7102468
  64.4 27.9 %collective-permute-start.13 = (bf16[256,1088]{0,1:T(8,128)(2,1)}, bf16[256,1088]{0,1:T(8,128)(2,1)}, u32[]{:S(2)}, u32[]{:S(2)}) collective-permute-start(bf16[256,1088]{0,1:T(8,128)(2,1)} %collective-permute-done.12), channel_id=1, source_target_pairs={{0,1},{1,0},{2,3},{3,2},{4,5},{5,4},{6,7},{7,6},{8,9},{9,8},{10,11... | collective-permute-start | bytes 1671176 | tf_op jit(solution)/shard_map/ppermute | solution.py:34
  65.2 25.5 %copy-start.80 = (f32[256]{0:T(256)}, f32[256]{0:T(256)S(1)}, u32[]{:S(2)}) copy-start(f32[256]{0:T(256)S(1)} %broadcast_multiply_fusion.3) | copy-start | bytes 3076
  76.0 12.9 %collective-permute-start.4 = (bf16[64,3264]{1,0:T(8,128)(2,1)S(1)}, bf16[64,3264]{1,0:T(8,128)(2,1)S(1)}, u32[]{:S(2)}, u32[]{:S(2)}) collective-permute-start(bf16[64,3264]{1,0:T(8,128)(2,1)S(1)} %slice.298.refs_2_), channel_id=1, source_target_pairs={{0,32},{32,0},{64,96},{96,64},{1,33},{33,1},{65,97},{97,65},{2,34}... | collective-permute-start | bytes 1253384 | tf_op jit(solution)/shard_map/ppermute | solution.py:266
  77.6 13.1 %collective-permute-start.3 = (bf16[64,3264]{1,0:T(8,128)(2,1)S(1)}, bf16[64,3264]{1,0:T(8,128)(2,1)}, u32[]{:S(2)}, u32[]{:S(2)}) collective-permute-start(bf16[64,3264]{1,0:T(8,128)(2,1)S(1)} %slice.298.refs_2_), channel_id=1, source_target_pairs={{0,8},{8,0},{16,24},{24,16},{1,9},{9,1},{17,25},{25,17},{2,10},{10... | collective-permute-start | bytes 1253384 | tf_op jit(solution)/shard_map/ppermute | solution.py:266
  88.9 9.4 %collective-permute-start.14 = (bf16[272,1088]{1,0:T(8,128)(2,1)}, bf16[272,1088]{1,0:T(8,128)(2,1)}, u32[]{:S(2)}, u32[]{:S(2)}) collective-permute-start(bf16[272,1088]{1,0:T(8,128)(2,1)} %refs_0_.3), channel_id=1, source_target_pairs={{0,1},{1,0},{2,3},{3,2},{4,5},{5,4},{6,7},{7,6},{8,9},{9,8},{10,11... | collective-permute-start | bytes 1775624 | tf_op jit(solution)/shard_map/ppermute | solution.py:34
  89.6 74.5 %collective-permute-start.17 = (bf16[272,4352]{1,0:T(8,128)(2,1)S(1)}, bf16[272,4352]{1,0:T(8,128)(2,1)}, u32[]{:S(2)}, u32[]{:S(2)}) collective-permute-start(bf16[272,4352]{1,0:T(8,128)(2,1)S(1)} %copy-done.3), channel_id=1, source_target_pairs={{0,1},{1,0},{2,3},{3,2},{4,5},{5,4},{6,7},{7,6},{8,9},{9,8},{10,11... | collective-permute-start | bytes 7102472 | tf_op jit(solution)/shard_map/ppermute | solution.py:34
  90.8 7.8 %collective-permute-start.16 = (bf16[272,1088]{1,0:T(8,128)(2,1)}, bf16[272,1088]{1,0:T(8,128)(2,1)}, u32[]{:S(2)}, u32[]{:S(2)}) collective-permute-start(bf16[272,1088]{1,0:T(8,128)(2,1)} %collective-permute-done.15.refs_2_), channel_id=1, source_target_pairs={{0,1},{1,0},{2,3},{3,2},{4,5},{5,4},{6,7},{7,6},{8,9},{9,8},{10,11... | collective-permute-start | bytes 1775624 | tf_op jit(solution)/shard_map/ppermute | solution.py:34
  92.4 10.4 %collective-permute-start.5 = (bf16[32,3264]{1,0:T(8,128)(2,1)}, bf16[32,3264]{1,0:T(8,128)(2,1)}, u32[]{:S(2)}, u32[]{:S(2)}) collective-permute-start(bf16[32,3264]{1,0:T(8,128)(2,1)} %slice.299), channel_id=1, source_target_pairs={{0,8},{8,0},{16,24},{24,16},{1,9},{9,1},{17,25},{25,17},{2,10},{10... | collective-permute-start | bytes 626696 | tf_op jit(solution)/shard_map/ppermute | solution.py:266
  98.2 18.0 %copy-start.66 = (bf16[1,3264]{1,0:T(2,128)(2,1)S(1)}, bf16[1,3264]{1,0:T(2,128)(2,1)}, u32[]{:S(2)}) copy-start(bf16[1,3264]{1,0:T(2,128)(2,1)} %concatenate.103) | copy-start | bytes 19588
  98.2 21.2 %copy-start.81 = (f32[256]{0:T(256)S(1)}, f32[256]{0:T(256)}, u32[]{:S(2)}) copy-start(f32[256]{0:T(256)} %copy-done.80) | copy-start | bytes 3076
  98.2 21.2 %copy-start.86 = (f32[256]{0:T(256)S(1)}, f32[256]{0:T(256)}, u32[]{:S(2)}) copy-start(f32[256]{0:T(256)} %add_rsqrt_fusion.2) | copy-start | bytes 3076
  98.3 23.9 %collective-permute-start.7 = (bf16[64,3264]{1,0:T(8,128)(2,1)S(1)}, bf16[64,3264]{1,0:T(8,128)(2,1)}, u32[]{:S(2)}, u32[]{:S(2)}) collective-permute-start(bf16[64,3264]{1,0:T(8,128)(2,1)S(1)} %slice.298.refs_2_), channel_id=1, source_target_pairs={{0,1},{1,0},{2,3},{3,2},{4,5},{5,4},{6,7},{7,6},{8,9},{9,8},{10,11... | collective-permute-start | bytes 1253384 | tf_op jit(solution)/shard_map/ppermute | solution.py:34
  98.5 17.1 %collective-permute-start.1 = (bf16[32,3264]{1,0:T(8,128)(2,1)S(1)}, bf16[32,3264]{1,0:T(8,128)(2,1)S(1)}, u32[]{:S(2)}, u32[]{:S(2)}) collective-permute-start(bf16[32,3264]{1,0:T(8,128)(2,1)S(1)} %slice.292.refs_6_), channel_id=1, source_target_pairs={{0,1},{1,0},{2,3},{3,2},{4,5},{5,4},{6,7},{7,6},{8,9},{9,8},{10,11... | collective-permute-start | bytes 626696 | tf_op jit(solution)/shard_map/ppermute | solution.py:34
  102.8 12.1 %collective-permute-start.6 = (bf16[32,3264]{1,0:T(8,128)(2,1)S(1)}, bf16[32,3264]{1,0:T(8,128)(2,1)S(1)}, u32[]{:S(2)}, u32[]{:S(2)}) collective-permute-start(bf16[32,3264]{1,0:T(8,128)(2,1)S(1)} %copy-done.65), channel_id=1, source_target_pairs={{0,32},{32,0},{64,96},{96,64},{1,33},{33,1},{65,97},{97,65},{2,34}... | collective-permute-start | bytes 626696 | tf_op jit(solution)/shard_map/ppermute | solution.py:266
  114.9 7.9 %collective-permute-start.9 = (bf16[64,3264]{1,0:T(8,128)(2,1)S(1)}, bf16[64,3264]{1,0:T(8,128)(2,1)}, u32[]{:S(2)}, u32[]{:S(2)}) collective-permute-start(bf16[64,3264]{1,0:T(8,128)(2,1)S(1)} %collective-permute-done.4.refs_4_), channel_id=1, source_target_pairs={{0,1},{1,0},{2,3},{3,2},{4,5},{5,4},{6,7},{7,6},{8,9},{9,8},{10,11... | collective-permute-start | bytes 1253384 | tf_op jit(solution)/shard_map/ppermute | solution.py:34
  115.6 7.3 %collective-permute-start.8 = (bf16[64,3264]{1,0:T(8,128)(2,1)}, bf16[64,3264]{1,0:T(8,128)(2,1)}, u32[]{:S(2)}, u32[]{:S(2)}) collective-permute-start(bf16[64,3264]{1,0:T(8,128)(2,1)} %collective-permute-done.3.refs_3_), channel_id=1, source_target_pairs={{0,1},{1,0},{2,3},{3,2},{4,5},{5,4},{6,7},{7,6},{8,9},{9,8},{10,11... | collective-permute-start | bytes 1253384 | tf_op jit(solution)/shard_map/ppermute | solution.py:34
  116.1 6.7 %collective-permute-start.10 = (bf16[64,3264]{1,0:T(8,128)(2,1)}, bf16[64,3264]{1,0:T(8,128)(2,1)}, u32[]{:S(2)}, u32[]{:S(2)}) collective-permute-start(bf16[64,3264]{1,0:T(8,128)(2,1)} %constant_dynamic-update-slice_fusion.refs_5_), channel_id=1, source_target_pairs={{0,1},{1,0},{2,3},{3,2},{4,5},{5,4},{6,7},{7,6},{8,9},{9,8},{10,11... | collective-permute-start | bytes 1253384 | tf_op jit(solution)/shard_map/ppermute | solution.py:34
  122.1 41.9 %collective-permute-start.20 = (bf16[16,4352]{1,0:T(8,128)(2,1)}, bf16[16,4352]{1,0:T(8,128)(2,1)}, u32[]{:S(2)}, u32[]{:S(2)}) collective-permute-start(bf16[16,4352]{1,0:T(8,128)(2,1)} %get-tuple-element.140.refs_3_), channel_id=1, source_target_pairs={{0,1},{1,0},{2,3},{3,2},{4,5},{5,4},{6,7},{7,6},{8,9},{9,8},{10,11... | collective-permute-start | bytes 417800 | tf_op jit(solution)/shard_map/ppermute | solution.py:34
  137.9 26.1 %collective-permute-start.19 = (bf16[256,4352]{1,0:T(8,128)(2,1)}, bf16[256,4352]{1,0:T(8,128)(2,1)}, u32[]{:S(2)}, u32[]{:S(2)}) collective-permute-start(bf16[256,4352]{1,0:T(8,128)(2,1)} %all-gather.4.cloned.1.call-done.refs_2_), channel_id=1, source_target_pairs={{0,1},{1,0},{2,3},{3,2},{4,5},{5,4},{6,7},{7,6},{8,9},{9,8},{10,11... | collective-permute-start | bytes 6684680 | tf_op jit(solution)/shard_map/ppermute | solution.py:34
  187.2 6.0 %collective-permute-start.27 = (bf16[2,256,1088]{1,2,0:T(8,128)(2,1)}, bf16[2,256,1088]{1,2,0:T(8,128)(2,1)}, u32[]{:S(2)}, u32[]{:S(2)}) collective-permute-start(bf16[2,256,1088]{1,2,0:T(8,128)(2,1)} %copy.117), channel_id=1, source_target_pairs={{0,1},{1,0},{2,3},{3,2},{4,5},{5,4},{6,7},{7,6},{8,9},{9,8},{10,11... | collective-permute-start | bytes 3342344 | tf_op jit(solution)/shard_map/ppermute | solution.py:34
  187.2 3.8 collective-permute-start.28
  202.0 184.8 %reduce-scatter.12.cloned.1.call-start = ((), (), s32[]{:S(2)}) async-start(), calls=%async_computation.7 | async-start | bytes 5640192
  203.7 14.5 %collective-permute-start.21 = (bf16[1088,1088]{1,0:T(8,128)(2,1)S(1)}, bf16[1088,1088]{1,0:T(8,128)(2,1)}, u32[]{:S(2)}, u32[]{:S(2)}) collective-permute-start(bf16[1088,1088]{1,0:T(8,128)(2,1)S(1)} %copy-done.1), channel_id=1, source_target_pairs={{0,1},{1,0},{2,3},{3,2},{4,5},{5,4},{6,7},{7,6},{8,9},{9,8},{10,11... | collective-permute-start | bytes 7102472 | tf_op jit(solution)/shard_map/ppermute | solution.py:34
  208.1 5.9 %collective-permute-start.23 = (bf16[1024,1088]{0,1:T(8,128)(2,1)}, bf16[1024,1088]{0,1:T(8,128)(2,1)}, u32[]{:S(2)}, u32[]{:S(2)}) collective-permute-start(bf16[1024,1088]{0,1:T(8,128)(2,1)} %copy.105), channel_id=1, source_target_pairs={{0,1},{1,0},{2,3},{3,2},{4,5},{5,4},{6,7},{7,6},{8,9},{9,8},{10,11... | collective-permute-start | bytes 6684680 | tf_op jit(solution)/shard_map/ppermute | solution.py:34
  208.9 4.1 collective-permute-start.29
  209.1 9.0 %collective-permute-start.24 = (bf16[64,1088]{1,0:T(8,128)(2,1)S(1)}, bf16[64,1088]{1,0:T(8,128)(2,1)S(1)}, u32[]{:S(2)}, u32[]{:S(2)}) collective-permute-start(bf16[64,1088]{1,0:T(8,128)(2,1)S(1)} %copy-done.21), channel_id=1, source_target_pairs={{0,1},{1,0},{2,3},{3,2},{4,5},{5,4},{6,7},{7,6},{8,9},{9,8},{10,11... | collective-permute-start | bytes 417800 | tf_op jit(solution)/shard_map/ppermute | solution.py:34
  221.6 21.2 %slice-start.2 = ((s8[9469952]{0:T(1024)(128)(4,1)}), s8[4194304]{0:T(1024)(128)(4,1)S(1)}, s32[]{:S(2)}) async-start(s8[9469952]{0:T(1024)(128)(4,1)} %bitcast.134), calls=%async_computation.11 | async-start | bytes 8388608
  241.9 47.9 %collective-permute-start.30 = (bf16[256,4352]{1,0:T(8,128)(2,1)}, bf16[256,4352]{1,0:T(8,128)(2,1)}, u32[]{:S(2)}, u32[]{:S(2)}) collective-permute-start(bf16[256,4352]{1,0:T(8,128)(2,1)} %get-tuple-element.174), channel_id=1, source_target_pairs={{0,1},{1,0},{2,3},{3,2},{4,5},{5,4},{6,7},{7,6},{8,9},{9,8},{10,11... | collective-permute-start | bytes 6684680 | tf_op jit(solution)/shard_map/ppermute | solution.py:34
  285.1 19.1 %copy-start.12 = (bf16[2,2,256,1088]{3,2,1,0:T(8,128)(2,1)}, bf16[2,2,256,1088]{3,2,1,0:T(8,128)(2,1)S(1)}, u32[]{:S(2)}) copy-start(bf16[2,2,256,1088]{3,2,1,0:T(8,128)(2,1)S(1)} %get-tuple-element.27) | copy-start | bytes 6684676
  289.7 10.4 %collective-permute-start.25 = (bf16[2,2,256,1088]{2,3,1,0:T(8,128)(2,1)}, bf16[2,2,256,1088]{2,3,1,0:T(8,128)(2,1)}, u32[]{:S(2)}, u32[]{:S(2)}) collective-permute-start(bf16[2,2,256,1088]{2,3,1,0:T(8,128)(2,1)} %copy.111), channel_id=1, source_target_pairs={{0,1},{1,0},{2,3},{3,2},{4,5},{5,4},{6,7},{7,6},{8,9},{9,8},{10,11... | collective-permute-start | bytes 6684680 | tf_op jit(solution)/shard_map/ppermute | solution.py:34
  297.3 171.1 %reduce-scatter.14.cloned.1.call-start = ((), (), s32[]{:S(2)}) async-start(), calls=%async_computation.8 | async-start | bytes 5640192
  299.7 12.2 %collective-permute-start.31 = (bf16[2,256,272]{2,1,0:T(8,128)(2,1)}, bf16[2,256,272]{2,1,0:T(8,128)(2,1)}, u32[]{:S(2)}, u32[]{:S(2)}) collective-permute-start(bf16[2,256,272]{2,1,0:T(8,128)(2,1)} %get-tuple-element.120), channel_id=1, source_target_pairs={{0,1},{1,0},{2,3},{3,2},{4,5},{5,4},{6,7},{7,6},{8,9},{9,8},{10,11... | collective-permute-start | bytes 835592 | tf_op jit(solution)/shard_map/ppermute | solution.py:34
  309.3 28.4 %collective-permute-start.26 = (bf16[2,256,1088]{1,2,0:T(8,128)(2,1)}, bf16[2,256,1088]{1,2,0:T(8,128)(2,1)}, u32[]{:S(2)}, u32[]{:S(2)}) collective-permute-start(bf16[2,256,1088]{1,2,0:T(8,128)(2,1)} %copy.114), channel_id=1, source_target_pairs={{0,2},{2,0},{1,3},{3,1},{4,6},{6,4},{5,7},{7,5},{8,10},{10,8},{9,1... | collective-permute-start | bytes 3342344 | tf_op jit(solution)/shard_map/ppermute | solution.py:38
  310.9 3.7 collective-permute-start.34
  311.1 2.8 collective-permute-start.33
  366.2 3.9 collective-permute-start.32
  366.2 3.2 collective-permute-start.35
  386.8 165.2 %all-gather.8.cloned.1.call-start = ((), (), s32[]{:S(2)}) async-start(), calls=%async_computation.5 | async-start | bytes 8460288 | tf_op jit(solution)/shard_map/all_gather | solution.py:498
  387.9 84.6 %collective-permute-start.36 = (bf16[144,1088]{1,0:T(8,128)(2,1)S(1)}, bf16[144,1088]{1,0:T(8,128)(2,1)S(1)}, u32[]{:S(2)}, u32[]{:S(2)}) collective-permute-start(bf16[144,1088]{1,0:T(8,128)(2,1)S(1)} %select_bitcast_fusion), channel_id=1, source_target_pairs={{0,6},{6,0},{2,4},{4,2},{1,7},{7,1},{3,5},{5,3},{8,14},{14,8},{10,... | collective-permute-start | bytes 940040 | tf_op jit(solution)/shard_map/ppermute | solution.py:46
  469.4 6.6 %collective-permute-start.38 = (bf16[72,1088]{1,0:T(8,128)(2,1)S(1)}, bf16[72,1088]{1,0:T(8,128)(2,1)S(1)}, u32[]{:S(2)}, u32[]{:S(2)}) collective-permute-start(bf16[72,1088]{1,0:T(8,128)(2,1)S(1)} %select_bitcast_fusion.1), channel_id=1, source_target_pairs={{0,6},{6,0},{2,4},{4,2},{1,7},{7,1},{3,5},{5,3},{8,14},{14,8},{10,... | collective-permute-start | bytes 470024 | tf_op jit(solution)/shard_map/ppermute | solution.py:46
  472.6 9.6 %collective-permute-start.37 = (bf16[144,1088]{1,0:T(8,128)(2,1)S(1)}, bf16[144,1088]{1,0:T(8,128)(2,1)S(1)}, u32[]{:S(2)}, u32[]{:S(2)}) collective-permute-start(bf16[144,1088]{1,0:T(8,128)(2,1)S(1)} %fusion.47), channel_id=1, source_target_pairs={{0,4},{4,0},{1,5},{5,1},{2,6},{6,2},{3,7},{7,3},{8,12},{12,8},{9,1... | collective-permute-start | bytes 940040 | tf_op jit(solution)/shard_map/ppermute | solution.py:42
  477.1 6.9 %collective-permute-start.39 = (bf16[72,1088]{1,0:T(8,128)(2,1)S(1)}, bf16[72,1088]{1,0:T(8,128)(2,1)S(1)}, u32[]{:S(2)}, u32[]{:S(2)}) collective-permute-start(bf16[72,1088]{1,0:T(8,128)(2,1)S(1)} %fusion.48), channel_id=1, source_target_pairs={{0,4},{4,0},{1,5},{5,1},{2,6},{6,2},{3,7},{7,3},{8,12},{12,8},{9,1... | collective-permute-start | bytes 470024 | tf_op jit(solution)/shard_map/ppermute | solution.py:42
  (86 other events, 370.9 us)
Sparse Core Ops, SparseCore 0:
  20.6 46.6 all-gather.3
  69.5 47.5 all-gather.5
  202.1 81.2 reduce-scatter.9
  297.4 81.5 reduce-scatter.11
  386.9 81.4 reduce-scatter.13
  485.0 66.8 all-gather.7
where the time goes:
time: 586 us; the launch traced here: 575 us
  waiting for transfers between devices  215 us (37%)
  local copies, waits for them, and re-layouts  120 us (20%)
  Pallas kernels  75.7 us (13%)
  matrix products  65 us (11%)
  other arithmetic  51.1 us (9%)
  starting transfers between devices  32.2 us (5%)
  between operations  16 us (3%)
    unnamed x9, waiting for transfers between devices  78.1 us
    all_gather x1, waiting for transfers between devices, body(): lax.all_gather(jnp.concatenate([early, attn_part]).reshape(3, PAD, D), ('...  49.8 us
    unnamed x206, local copies, waits for them, and re-layouts  43.1 us
    ppermute x6, waiting for transfers between devices, swap_far(): return lax.ppermute(x, ('zl', 'zh'), [(0, 3), (3, 0), (1, 2), (2, 1)])  39.1 us
    pallas_call x1, Pallas kernels, attend_backward(): pl.pallas_call(attend_backward_kernel, grid=((HEADS + 1) // 2,), out_shap...  21.5 us
    ppermute x2, waiting for transfers between devices, swap_half(): return lax.ppermute(x, 'zh', [(0, 1), (1, 0)])  17.5 us
    ppermute x4, waiting for transfers between devices, swap_pair(): return lax.ppermute(x, axis, [(0, 1), (1, 0), (2, 3), (3, 2)])  17.2 us
    ppermute x7, local copies, waits for them, and re-layouts, swap_core(): return lax.ppermute(x, 'c', [(0, 1), (1, 0)])  17 us
  transfers between devices with their start and end apart: 46, of which 16 were waited for; matrix products, arithmetic and copies ran while one was open for 34% of the time, Pallas kernels for 12%

commit v1 on v0

--- a/solution.py
+++ b/solution.py
@@ -4,6 +4,7 @@
 import jax.numpy as jnp
 from jax import lax
 from jax.experimental import pallas as pl
+from jax.experimental.layout import Layout, with_layout_constraint
 from jax.experimental.pallas import tpu as pltpu
 from jax.sharding import Mesh
 from jax.sharding import PartitionSpec as P
@@ -30,27 +31,99 @@
     return jax.nn.gelu(values, approximate=False)
 
 
+def rows_major(x):
+    return with_layout_constraint(x, Layout(major_to_minor=tuple(range(x.ndim))))
+
+
+def permute(x, axis, pairs):
+    shape = x.shape
+    if shape[-2] % 128 == 0 and shape[-1] % 128 != 0:
+        x = x.reshape(-1, 64, shape[-1])
+    return rows_major(lax.ppermute(rows_major(x), axis, pairs)).reshape(shape)
+
+
+def rotate(x, axis, step):
+    return permute(x, axis, [(at, (at + step) % 4) for at in range(4)])
+
+
 def swap_core(x):
-    return lax.ppermute(x, "c", [(0, 1), (1, 0)])
+    return permute(x, "c", [(0, 1), (1, 0)])
 
 
 def swap_half(x):
-    return lax.ppermute(x, "zh", [(0, 1), (1, 0)])
+    return permute(x, "zh", [(0, 1), (1, 0)])
 
 
 def swap_near(x):
-    return lax.ppermute(x, "zl", [(0, 1), (1, 0)])
+    return permute(x, "zl", [(0, 1), (1, 0)])
 
 
 def swap_far(x):
-    return lax.ppermute(x, ("zl", "zh"), [(0, 3), (3, 0), (1, 2), (2, 1)])
+    return permute(x, ("zl", "zh"), [(0, 3), (3, 0), (1, 2), (2, 1)])
+
+
+def swap_pair(x, axis):
+    return permute(x, axis, [(0, 1), (1, 0), (2, 3), (3, 2)])
+
+
+def after_kernel(x_ref, done_ref, out_ref):
+    pass
+
+
+def after(x, done):
+    done = done.reshape((-1,) + done.shape[-2:])[0, :16, :128]
+    return pl.pallas_call(
+        after_kernel,
+        out_shape=jax.ShapeDtypeStruct(x.shape, x.dtype),
+        in_specs=[pl.BlockSpec(memory_space=pl.ANY)] * 2,
+        out_specs=pl.BlockSpec(memory_space=pl.ANY),
+        input_output_aliases={0: 0},
+    )(x, done)
+
+
+def pick(values, index, dim):
+    start = [0] * values.ndim
+    start[dim] = index
+    size = list(values.shape)
+    size[dim] = 1
+    part = lax.dynamic_slice(values, start, size, allow_negative_indices=False)
+    return part.reshape(size[:dim] + size[dim + 1 :])
+
+
+def natural(parts, place):
+    found = []
+    for index in range(4):
+        value = parts[index]
+        for at in range(1, 4):
+            value = jnp.where(place == at, parts[(index - at) % 4], value)
+        found.append(value)
+    return jnp.stack(found)
+
+
+def ring_scatter(values, axis, dim):
+    place = lax.axis_index(axis)
+
+    def part(step):
+        return pick(values, (place + step) & 3, dim)
+
+    got = [rotate(part(step), axis, step) for step in (2, 1, 3)]
+    total = part(0).astype(F32)
+    for value in got:
+        total = total + value.astype(F32)
+    return total.astype(BF)
+
+
+def ring_gather(piece, axis):
+    far, behind, ahead = (rotate(piece, axis, step) for step in (2, 1, 3))
+    return natural([piece, ahead, far, behind], lax.axis_index(axis))
 
 
 def depth_sum(values, zh):
-    mine = jnp.where(zh == 0, values[0], values[1]).astype(F32)
+    mine = jnp.where(zh == 0, values[0], values[1])
     other = jnp.where(zh == 0, values[1], values[0])
-    near = (mine + swap_far(other).astype(F32)).astype(BF)
-    return (near.astype(F32) + swap_near(near).astype(F32)).astype(BF)
+    far, half, near = swap_far(other), swap_half(other), swap_near(mine)
+    total = mine.astype(F32) + near.astype(F32) + far.astype(F32) + half.astype(F32)
+    return total.astype(BF)
 
 
 def assemble_kernel(spots, *refs):
@@ -59,12 +132,12 @@
     rank = lax.axis_index("zh") * 2 + lax.axis_index("c")
     quarter = lax.axis_index("y") % 2 * 2 + lax.axis_index("x") % 2
     copies = []
-    for ref, (flip, start, turn, size) in zip(parts, spots):
+    for which, row, flip, start, turn, size in spots:
         at = jnp.bitwise_xor(rank, flip) * rows + start
         if turn is not None:
             at = at + jnp.bitwise_xor(quarter, turn) * size
         copy = pltpu.make_async_copy(
-            ref.at[pl.ds(0, size)],
+            parts[which].at[pl.ds(row, size)],
             out.at[pl.ds(pl.multiple_of(at, 16), size)],
             sems.at[len(copies)],
         )
@@ -81,7 +154,7 @@
         out_shape=jax.ShapeDtypeStruct((rows * 4, columns), BF),
         in_specs=[pl.BlockSpec(memory_space=pltpu.VMEM)] * len(parts),
         out_specs=pl.BlockSpec(memory_space=pl.ANY),
-        scratch_shapes=[pltpu.SemaphoreType.DMA((len(parts),))],
+        scratch_shapes=[pltpu.SemaphoreType.DMA((len(spots),))],
         compiler_params=pltpu.CompilerParams(vmem_limit_bytes=24 * 2**20),
         cost_estimate=pl.CostEstimate(
             flops=0, bytes_accessed=rows * columns * 16, transcendentals=0
@@ -198,41 +271,42 @@
     )(queries, keys, values, mask, totals, d_mixed)
 
 
-def weight_grad_kernel(left_ref, right_ref, out_ref):
+def weight_grad_kernel(left_ref, right_ref, *refs):
+    out_ref = refs[-1]
     left = left_ref[0]
     pieces = left.shape[1] // SLICE
     empty = jnp.zeros((PAD - SLICE, D), BF)
     for at in range(right_ref.shape[1] // D):
-        product = lax.dot_general(
-            left,
-            right_ref[:, at * D : (at + 1) * D],
-            (((0,), (0,)), ((), ())),
-            preferred_element_type=F32,
-        )
+        product = dot_tn(left, right_ref[:, at * D : (at + 1) * D])
         for piece in range(pieces):
             part = product[piece * SLICE : (piece + 1) * SLICE].astype(BF)
-            out_ref[at * pieces + piece, 0] = jnp.concatenate([part, empty])
-
-
-def weight_grad(left, right):
+            out_ref[at * pieces + piece, 0, 0] = jnp.concatenate([part, empty])
+
+
+def weight_grad(left, right, slots, first, slot, buffer=None):
     _, tokens, width = left.shape
     pieces = right.shape[1] // D * (width // SLICE)
+    in_specs = [
+        pl.BlockSpec((1, tokens, width), lambda at: (at, 0, 0)),
+        pl.BlockSpec(right.shape, lambda at: (0, 0)),
+    ]
+    more = () if buffer is None else (buffer,)
     return pl.pallas_call(
         weight_grad_kernel,
         grid=(2,),
-        out_shape=jax.ShapeDtypeStruct((pieces, 2, PAD, D), BF),
-        in_specs=[
-            pl.BlockSpec((1, tokens, width), lambda at: (at, 0, 0)),
-            pl.BlockSpec(right.shape, lambda at: (0, 0)),
-        ],
-        out_specs=pl.BlockSpec((pieces, 1, PAD, D), lambda at: (0, at, 0, 0)),
+        out_shape=jax.ShapeDtypeStruct((16, slots, 2, PAD, D), BF),
+        in_specs=in_specs + [pl.BlockSpec(memory_space=pl.ANY)] * len(more),
+        out_specs=pl.BlockSpec(
+            (pieces, 1, 1, PAD, D), lambda at: (first // pieces, slot, at, 0, 0)
+        ),
+        input_output_aliases={2: 0} if more else {},
         compiler_params=pltpu.CompilerParams(vmem_limit_bytes=48 * 2**20),
         cost_estimate=pl.CostEstimate(
             flops=4 * tokens * width * right.shape[1],
             bytes_accessed=2 * left.size + 2 * right.size + 2 * pieces * 2 * PAD * D,
             transcendentals=0,
         ),
-    )(left, right)
+    )(left, right, *more)
 
 
 def unpack_kernel(in_ref, out_ref):
@@ -262,42 +336,40 @@
     return shard, swap_core(shard), far, swap_core(far)
 
 
-def swap_pair(x, axis):
-    return lax.ppermute(x, axis, [(0, 1), (1, 0), (2, 3), (3, 2)])
-
-
 def gather_quarters(shard):
-    across, down = lax.axis_index("x") % 2, lax.axis_index("y") % 2
+    across, down = lax.axis_index("x") & 1, lax.axis_index("y") & 1
     quarter = down * 2 + across
     main = shard[:256].reshape(4, 64, shard.shape[1])
-    piece = lax.dynamic_index_in_dim(main, quarter, 0, keepdims=False)
+    piece = pick(main, quarter, 0)
     got = swap_far(jnp.concatenate([piece, shard[256:]]))
-    mine, rest = got[:64], got[64:]
+    mine = got[:64]
     by_x, by_y = swap_pair(mine, "x"), swap_pair(mine, "y")
-    last = jnp.concatenate([swap_pair(by_y[:32], "x"), swap_pair(by_x[32:], "y")])
-    pieces = [mine, by_x, by_y, last]
-    return pieces + [rest], [swap_core(piece) for piece in pieces] + [swap_core(rest)]
-
-
-def gather_spread(shard, spot):
+    last_x, last_y = swap_pair(by_y[:32], "x"), swap_pair(by_x[32:], "y")
+    return got, jnp.concatenate([got, by_x, by_y, last_x, last_y])
+
+
+def far_piece(shard, spot, done):
     unit = shard.shape[0] // 17
     main = shard[: 16 * unit].reshape(16, unit, shard.shape[1])
-    tail = shard[16 * unit :]
-    piece = lax.dynamic_index_in_dim(main, spot, 0, keepdims=False)
-    got = swap_far(jnp.concatenate([piece, tail]))
-    far = lax.all_gather(got[:unit], ("y", "x"), axis=0, tiled=True)
+    piece = pick(main, spot, 0)
+    return swap_far(after(jnp.concatenate([piece, shard[16 * unit :]]), done))
+
+
+def gather_spread(shard, got):
+    unit = shard.shape[0] // 17
+    far = rows_major(lax.all_gather(got[:unit], ("y", "x"), axis=0, tiled=True))
     rest = got[unit:]
     rows, main = shard.shape[0], 16 * unit
     return assemble(
         rows,
         (shard, swap_core(shard), far, rest, swap_core(far), swap_core(rest)),
         (
-            (0, 0, None, rows),
-            (1, 0, None, rows),
-            (2, 0, None, main),
-            (2, main, None, unit),
-            (3, 0, None, main),
-            (3, main, None, unit),
+            (0, 0, 0, 0, None, rows),
+            (1, 0, 1, 0, None, rows),
+            (2, 0, 2, 0, None, main),
+            (3, 0, 2, main, None, unit),
+            (4, 0, 3, 0, None, main),
+            (5, 0, 3, main, None, unit),
         ),
     )
 
@@ -340,26 +412,30 @@
     rows = block_input.shape[1]
     own_tokens = block_input[0]
     with_small = jnp.concatenate([w_qkv, small])
-    far_parts, across_parts = gather_quarters(with_small)
     beside = swap_core(with_small)
-    half_tokens = swap_half(own_tokens)
+    got_qkv, far_parts = gather_quarters(with_small)
+    across_parts = swap_core(far_parts)
+    half_tokens = swap_half(after(own_tokens, got_qkv))
     tokens = [own_tokens, swap_core(own_tokens), half_tokens, swap_core(half_tokens)]
-    turns = [(0, 0, 64), (0, 1, 64), (0, 2, 64), (0, 3, 64), (256, None, 16)]
+    got_up = far_piece(w_up, spot, got_qkv)
+    got_down = far_piece(w_down, spot, got_up)
+    out_parts = gather_direct(after(w_out, got_down))
+    full_up = gather_spread(w_up, got_up)
+    full_down = gather_spread(w_down, got_down)
+    turns = ((0, 0, 0, 64), (96, 0, 1, 64), (160, 0, 2, 64), (224, 0, 3, 64), (64, 256, None, 16))
     full_qkv = assemble(
         QUART,
-        (with_small, beside, *far_parts, *across_parts),
-        ((0, 0, None, QUART), (1, 0, None, QUART))
-        + tuple((2, *turn) for turn in turns)
-        + tuple((3, *turn) for turn in turns),
+        (with_small, beside, far_parts, across_parts),
+        ((0, 0, 0, 0, None, QUART), (1, 0, 1, 0, None, QUART))
+        + tuple((2, row, 2, *turn) for row, *turn in turns)
+        + tuple((3, row, 3, *turn) for row, *turn in turns),
     )
     smalls = [
-        value.astype(F32) for value in (small[0], beside[QUART], far_parts[4][16], across_parts[4][16])
+        value.astype(F32) for value in (small[0], beside[QUART], far_parts[80], across_parts[80])
     ]
     full_out = assemble(
-        QUART, gather_direct(w_out), tuple((flip, 0, None, QUART) for flip in range(4))
-    )
-    full_up = gather_spread(w_up, spot)
-    full_down = gather_spread(w_down, spot)
+        QUART, out_parts, tuple((flip, 0, flip, 0, None, QUART) for flip in range(4))
+    )
 
     ordered = []
     for index in range(4):
@@ -397,7 +473,10 @@
     starts = [jnp.bitwise_xor(rank, flip) * rows for flip in range(4)]
     key_places = jnp.concatenate([start + jnp.arange(rows) for start in starts])
     key_segments = jnp.concatenate(
-        [lax.dynamic_slice_in_dim(segments, start, rows) for start in starts]
+        [
+            lax.dynamic_slice(segments, (start,), (rows,), allow_negative_indices=False)
+            for start in starts
+        ]
     )
     allowed = (key_segments[:rows, None] == key_segments[None, :]) & (
         query_places[:, None] >= key_places[None, :]
@@ -421,25 +500,21 @@
         other = jnp.where(core == 0, odd, even)
         return jnp.concatenate([mine, swap_core(other)], axis=1)
 
-    def across(value):
-        rest = value.shape[2]
-        value = lax.psum_scatter(
-            value.reshape(32 * rest, D), ("y", "x"), scatter_dimension=0, tiled=True
-        )
-        return value.reshape(2, rest, D)
-
     upstream_wide = upstream.astype(F32)
     upstream_pair = paired(upstream)
     grad_down_bias = jnp.sum(upstream_wide, axis=0)
-    down_part = across(weight_grad(paired_columns(activated), upstream_pair))
+    activated_pair = paired_columns(activated)
 
     d_activated = jnp.dot(upstream, full_down.T, preferred_element_type=F32)
     gelu_back = jax.vjp(exact_gelu, upper)[1]
     d_upper = gelu_back(d_activated)[0].astype(BF)
     grad_up_bias = jnp.sum(d_upper.astype(F32), axis=0)
-    grad_up = weight_grad(paired_columns(normed_two), paired(d_upper))
-    down_part, grad_up = lax.optimization_barrier((down_part, grad_up))
-    up_part = across(grad_up)
+    normed_two_pair, d_upper_pair = paired_columns(normed_two), paired(d_upper)
+    grad_mlp = weight_grad(activated_pair, upstream_pair, 2, 0, 0)
+    grad_mlp = weight_grad(normed_two_pair, d_upper_pair, 2, 0, 1, grad_mlp)
+    mlp_part = lax.psum_scatter(
+        grad_mlp.reshape(64 * PAD, D), ("y", "x"), scatter_dimension=0, tiled=True
+    ).reshape(2, 2, PAD, D)
 
     d_normed_two = jnp.dot(d_upper, full_up.T, preferred_element_type=F32)
     norm_two_back = jax.vjp(layer_norm, middle, gain_two, shift_two)[1]
@@ -447,11 +522,12 @@
     d_middle = upstream_wide + d_middle_part
     d_attended = d_middle.astype(BF)
     grad_out_bias = jnp.sum(d_attended.astype(F32), axis=0)
-    grad_out = weight_grad(paired_columns(mixed), paired(d_attended))
+    mixed_pair, d_attended_pair = paired_columns(mixed), paired(d_attended)
+    normed_pair = paired_columns(normed)
 
     d_mixed = jnp.dot(d_attended, full_out.T, preferred_element_type=F32).astype(BF)
     d_queries, d_both, d_beside = attend_backward(
-        queries, keys, values, mask, log_total, d_mixed
+        queries, keys, values, mask, log_total, after(d_mixed, grad_mlp)
     )
     d_beside = swap_core(d_beside)
     d_half = swap_half((d_both[1].astype(F32) + d_beside[1].astype(F32)).astype(BF))
@@ -460,7 +536,8 @@
     d_project = jnp.concatenate([d_queries, d_both[0], d_both[1]], axis=1)
     grad_query_bias = jnp.sum(d_queries.astype(F32), axis=0)
     grad_value_bias = jnp.sum(d_both[1].astype(F32), axis=0)
-    grad_qkv = weight_grad(paired_columns(normed), paired(d_project))
+    grad_attn = weight_grad(mixed_pair, d_attended_pair, 1, 12, 0)
+    grad_attn = weight_grad(normed_pair, paired(d_project), 1, 0, 0, grad_attn)
 
     d_normed = jnp.dot(d_project, full_qkv.T, preferred_element_type=F32)
     norm_one_back = jax.vjp(layer_norm, hidden_in, gain_one, shift_one)[1]
@@ -490,19 +567,23 @@
     mine = (mine + swap_core(other.astype(BF)).astype(F32)).astype(BF)
     mine = mine.reshape(2, 16, VECTOR).transpose(1, 0, 2)[:, :, None]
 
-    grad_attn = jnp.concatenate([grad_qkv, grad_out])
-    grad_attn = lax.dynamic_update_slice(grad_attn, mine, (0, 0, SLICE, 0))
-    up_part, grad_attn = lax.optimization_barrier((up_part, grad_attn))
-    early = depth_sum(jnp.concatenate([down_part, up_part], axis=1), zh)
-    attn_part = depth_sum(lax.optimization_barrier(across(grad_attn)), zh)
-    parts = lax.all_gather(
-        jnp.concatenate([early, attn_part]).reshape(3, PAD, D), ("y", "x"), axis=0, tiled=False
-    ).reshape(16, 3, PAD, D)
+    grad_attn = lax.dynamic_update_slice(grad_attn[:, 0], mine, (0, 0, SLICE, 0))
+    grad_attn = after(grad_attn, mlp_part)
+    one = ring_scatter(grad_attn[:, 0].reshape(4, 4, PAD, D), "x", 1)
+    two = ring_scatter(grad_attn[:, 1].reshape(4, 4, PAD, D), "y", 0)
+    one, two = ring_scatter(one, "y", 0), ring_scatter(two, "x", 0)
+    attn_part = depth_sum(jnp.stack([one, two]), zh)
+    one, two = ring_gather(attn_part[:40], "x"), ring_gather(attn_part[40:], "y")
+    one, two = ring_gather(one, "y"), ring_gather(two, "x")
+    attn = jnp.concatenate([one, two.transpose(1, 0, 2, 3)], axis=2).reshape(16, PAD, D)
+    grad_qkv = unpack(attn[:12], QUART)
+    grad_out = unpack(attn[12:], QUART)
+    vectors = attn[:, SLICE, :VECTOR].reshape(-1).astype(F32)
+
+    early = depth_sum(mlp_part.transpose(1, 0, 2, 3).reshape(2, 2 * PAD, D), zh)
+    parts = lax.all_gather(early, ("y", "x"), axis=0, tiled=True).reshape(16, 2, PAD, D)
     grad_down = unpack(parts[:, 0], D)
     grad_up = unpack(parts[:, 1], QUART)
-    grad_qkv = unpack(parts[:12, 2], QUART)
-    grad_out = unpack(parts[12:, 2], QUART)
-    vectors = parts[:, 2, SLICE, :VECTOR].reshape(-1).astype(F32)
 
     def owned(start, size):
         return vectors[start : start + size]

time: 586 us -> 495 us (0.84)
  waiting for transfers between devices: 215 us -> 117 us
  starting transfers between devices: 32.2 us -> 65.9 us
  local copies, waits for them, and re-layouts: 120 us -> 89.9 us
    unnamed x9 -> x4, waiting for transfers between devices: 78.1 us -> 0.07 us
    all_gather x3, waiting for transfers between devices: 49.8 us -> 0.01 us  [the longest x2 0.01 us: gather_spread(): far = rows_major(lax.all_gather(got[:unit], ('y', 'x'), axis=0, tiled=True))]
    ppermute x40 -> x62, starting transfers between devices: 32 us -> 65.5 us  [permute(): return rows_major(lax.ppermute(rows_major(x), axis, pairs)).reshape(shape)]
    ppermute x40 -> x62, waiting for transfers between devices: 86.8 us -> 117 us  [permute(): return rows_major(lax.ppermute(rows_major(x), axis, pairs)).reshape(shape)]
    ppermute x9 -> x0, local copies, waits for them, and re-layouts: 20.9 us -> none  [the longest x7 17 us: swap_core(): return lax.ppermute(x, 'c', [(0, 1), (1, 0)])]
    unnamed x206 -> x148, local copies, waits for them, and re-layouts: 43.1 us -> 30.6 us
    slice x12 -> x16, local copies, waits for them, and re-layouts: 7.48 us -> 12.2 us  [the longest x3 3.14 us: far_piece(): main = shard[:16 * unit].reshape(16, unit, shard.shape[1])]
  transfers between devices with their start and end apart: 46 -> 66, of which waited for: 16 -> 31; matrix products, arithmetic and copies ran while one was open for 34% -> 34% of each run, Pallas kernels for 12% -> 13%
where the time goes in v1:
time: 495 us; the launch traced here: 486 us
  waiting for transfers between devices  117 us (24%)
  local copies, waits for them, and re-layouts  89.9 us (18%)
  Pallas kernels  78.1 us (16%)
  matrix products  69.7 us (14%)
  starting transfers between devices  65.9 us (13%)
  other arithmetic  50.5 us (10%)
  between operations  15.3 us (3%)
    ppermute x62, waiting for transfers between devices, permute(): return rows_major(lax.ppermute(rows_major(x), axis, pairs)).reshape(shape)  117 us
    ppermute x62, starting transfers between devices, permute(): return rows_major(lax.ppermute(rows_major(x), axis, pairs)).reshape(shape)  65.5 us
    unnamed x148, local copies, waits for them, and re-layouts  30.6 us
    pallas_call x1, Pallas kernels, attend_backward(): pl.pallas_call(attend_backward_kernel, grid=((HEADS + 1) // 2,), out_shap...  21.5 us
    pallas_call x4, Pallas kernels, assemble(): pl.pallas_call(functools.partial(assemble_kernel, spots), out_shape=jax.S...  17.1 us
    pallas_call x4, Pallas kernels, weight_grad(): pl.pallas_call(weight_grad_kernel, grid=(2,), out_shape=jax.ShapeDtypeStr...  15.8 us
    dot_general x1, matrix products, body(): d_activated = jnp.dot(upstream, full_down.T, preferred_element_type=F32)  15.2 us
    pallas_call x1, Pallas kernels, attend_forward(): pl.pallas_call(attend_forward_kernel, grid=((HEADS + 1) // 2,), out_shape...  15 us
  transfers between devices with their start and end apart: 66, of which 31 were waited for; matrix products, arithmetic and copies ran while one was open for 34% of the time, Pallas kernels for 13%

profile of v1, /device:TPU:0, one launch (start us, length us, event | category | flops | bytes accessed | tf_op | source)
XLA Modules:
  0.0 486.3 jit_solution(3830766230615750761)
XLA Ops:
  7.3 2.1 copy.126.x_ref
  17.1 4.1 collective-permute-start
  22.4 3.1 slice.270
  32.4 3.7 collective-permute-done
  37.4 3.0 collective-permute-start.10
  41.8 5.1 %collective-permute-done.10 = bf16[32,4352]{1,0:T(8,128)(2,1)S(1)} collective-permute-done((bf16[32,4352]{1,0:T(8,128)(2,1)}, bf16[32,4352]{1,0:T(8,128)(2,1)S(1)}, u32[]{:S(2)}, u32[]{:S(2)}) %collective-permute-start.10) | collective-permute-done | bytes 278560 | tf_op jit(solution)/shard_map/ppermute | solution.py:42
  54.5 5.9 %collective-permute-done.2 = bf16[64,3264]{1,0:T(8,128)(2,1)S(1)} collective-permute-done((bf16[64,3264]{1,0:T(8,128)(2,1)S(1)}, bf16[64,3264]{1,0:T(8,128)(2,1)S(1)}, u32[]{:S(2)}, u32[]{:S(2)}) %collective-permute-start.2) | collective-permute-done | bytes 417824 | tf_op jit(solution)/shard_map/ppermute | solution.py:42
  60.4 2.3 collective-permute-start.11
  64.9 2.2 collective-permute-done.8
  70.1 2.9 collective-permute-done.4
  76.4 2.5 collective-permute-start.13
  82.0 12.0 %collective-permute-done.13.refs_2_ = bf16[272,1088]{1,0:T(8,128)(2,1)} collective-permute-done((bf16[272,1088]{1,0:T(8,128)(2,1)}, bf16[272,1088]{1,0:T(8,128)(2,1)}, u32[]{:S(2)}, u32[]{:S(2)}) %collective-permute-start.13) | collective-permute-done | bytes 591904 | tf_op jit(solution)/shard_map/ppermute | solution.py:42
  96.5 2.2 shard_map.277
  102.8 6.5 %shard_map.271 = bf16[1088,3264]{1,0:T(8,128)(2,1)S(1)} custom-call(bf16[288,3264]{1,0:T(8,128)(2,1)} %fusion.16.refs_0_, bf16[288,3264]{1,0:T(8,128)(2,1)} %collective-permute-done.6.refs_1_, bf16[288,3264]{1,0:T(8,128)(2,1)} %constant_dynamic-update-slice_fusion.refs_2_, bf16[288,3264]{1,0:T(8,128)(2,1)} %collective-permute-done.5.refs_3_), custom_call_target="tpu_custom_call" | custom-call | bytes 14204928 | tf_op jit(solution)/shard_map/pallas_call | solution.py:152
  109.3 3.7 fusion.45
  113.0 6.4 %add_convert_fusion.v_ref = bf16[1024,1088]{1,0:T(8,128)(2,1)} fusion(bf16[1088,3264]{1,0:T(8,128)(2,1)S(1)} %shard_map.271, f32[1088]{0:T(1024)S(1)} %add.298, bf16[256,1088]{1,0:T(8,128)(2,1)S(1)} %get-tuple-element.170, bf16[256,1088]{1,0:T(8,128)(2,1)S(1)} %get-tuple-element.169, bf16[256,1088]{1,0:T(8,128)(2,1)S(1)} %get-tuple-element.168, ...), kind=kOutput, calls=%fused_computation.3 | convolution fusion | flops 2435448832 | bytes 7102464 | tf_op jit(solution)/shard_map/dot_general | solution.py:470
  121.8 6.3 %convolution_convert_fusion.k_ref = bf16[1024,1088]{1,0:T(8,128)(2,1)S(1)} fusion(bf16[1088,3264]{1,0:T(8,128)(2,1)} %copy-done.3, bf16[256,1088]{1,0:T(8,128)(2,1)} %copy-done.51, bf16[256,1088]{1,0:T(8,128)(2,1)} %copy-done.50, bf16[256,1088]{1,0:T(8,128)(2,1)} %copy-done.49, bf16[256,1088]{1,0:T(8,128)(2,1)} %copy-done.41), kind=kOutput, calls=%fused_computation.24 | convolution fusion | flops 2434334720 | bytes 7094272 | tf_op jit(solution)/shard_map/dot_general | solution.py:469
  128.1 15.0 %shard_map.273 = (bf16[256,1088]{1,0:T(8,128)(2,1)S(1)}, f32[256,1088]{1,0:T(8,128)S(1)}) custom-call(bf16[256,1088]{1,0:T(8,128)(2,1)S(1)} %copy-done.21, bf16[1024,1088]{1,0:T(8,128)(2,1)S(1)} %convolution_convert_fusion.k_ref, bf16[1024,1088]{1,0:T(8,128)(2,1)S(1)} %copy-done.15, f32[256,1024]{1,0:T(8,128)S(1)} %copy-done.13), custom_call_target="tpu_custom_call" | custom-call | flops 1140850688 | bytes 6684672 | tf_op jit(solution)/shard_map/pallas_call | solution.py:225
  149.1 4.5 shard_map.278
  153.7 14.6 %multiply_convert_fusion = (bf16[256,4352]{1,0:T(8,128)(2,1)S(1)}, f32[256,4352]{1,0:T(8,128)}, f32[256,4352]{1,0:T(8,128)}) fusion(f32[4352]{0:T(1024)S(1)} %add.318, bf16[256,1088]{1,0:T(8,128)(2,1)S(1)} %copy-done.43, bf16[1088,4352]{1,0:T(8,128)(2,1)S(1)} %shard_map.278), kind=kOutput, calls=%fused_computation.8 | convolution fusion | flops 2497839104 | bytes 21185536 | tf_op jit(solution)/shard_map/dot_general | solution.py:488
  168.3 4.0 shard_map.279
  172.3 3.8 copy-done
  176.0 15.2 %convert_reduce_fusion = (f32[4352]{0:T(1024)}, bf16[256,4352]{1,0:T(8,128)(2,1)}) fusion(f32[256,4352]{1,0:T(8,128)} %get-tuple-element.82, f32[256,4352]{1,0:T(8,128)} %get-tuple-element.178, bf16[4352,1088]{1,0:T(8,128)(2,1)} %copy-done, bf16[1,256,1088]{1,2,0:T(8,128)(2,1)S(1)} %copy-done.52), kind=kOutput, calls=%fused_computation.6 | convolution fusion | flops 2442129152 | bytes 21185536 | tf_op jit(solution)/shard_map/dot_general | solution.py:508
  200.2 4.9 %shard_map.280.refs_0_ = bf16[16,2,2,72,1088]{4,3,2,1,0:T(8,128)(2,1)} custom-call(bf16[2,512,1088]{2,1,0:T(8,128)(2,1)S(1)} %pad_maximum_fusion.4.left_ref, bf16[512,1088]{1,0:T(8,128)(2,1)S(1)} %pad_maximum_fusion.7.right_ref), custom_call_target="tpu_custom_call" | custom-call | flops 2424307712 | bytes 8355840 | tf_op jit(solution)/shard_map/pallas_call | solution.py:294
  205.1 2.6 pad_maximum_fusion.right_ref
  207.7 4.9 %shard_map.281 = bf16[16,2,2,72,1088]{4,3,2,1,0:T(8,128)(2,1)} custom-call(bf16[2,512,272]{2,1,0:T(8,128)(2,1)S(1)} %pad_maximum_fusion.9.left_ref, bf16[512,4352]{1,0:T(8,128)(2,1)S(1)} %pad_maximum_fusion.right_ref, bf16[16,2,2,72,1088]{4,3,2,1,0:T(8,128)(2,1)} %shard_map.280.refs_0_), custom_call_target="tpu_custom_call", output_to_operand_aliasing={{}: (2, {})} | custom-call | flops 2424307712 | bytes 10027008 | tf_op jit(solution)/shard_map/pallas_call | solution.py:294
  212.9 8.6 %fusion.72 = (f32[1088]{0:T(1024)}, f32[256,1088]{0,1:T(8,128)}) fusion(bf16[256,4352]{1,0:T(8,128)(2,1)} %get-tuple-element.184, bf16[1088,4352]{1,0:T(8,128)(2,1)} %copy-done.2), kind=kOutput, calls=%fused_computation.264 | convolution fusion | flops 2424585216 | bytes 12816640 | tf_op jit(solution)/shard_map/dot_general | solution.py:519
  227.2 2.1 convolution_convert_fusion.1
  237.5 21.5 %shard_map.283 = (bf16[256,1088]{1,0:T(8,128)(2,1)S(1)}, bf16[2,2,256,1088]{3,2,1,0:T(8,128)(2,1)S(1)}, bf16[2,2,256,1088]{3,2,1,0:T(8,128)(2,1)S(1)}) custom-call(bf16[256,1088]{1,0:T(8,128)(2,1)S(1)} %copy-done.22, bf16[1024,1088]{1,0:T(8,128)(2,1)S(1)} %copy-done.18, bf16[1024,1088]{1,0:T(8,128)(2,1)S(1)} %copy-done.16, f32[256,1024]{1,0:T(8,128)S(1)} %copy-done.14, ...), custom_call_target="tpu_custom_call" | custom-call | flops 2852126720 | bytes 13369344 | tf_op jit(solution)/shard_map/pallas_call | solution.py:252
  259.7 4.0 collective-permute-done.25
  275.8 19.3 %collective-permute-done.26 = bf16[8,64,1088]{2,1,0:T(8,128)(2,1)} collective-permute-done((bf16[8,64,1088]{2,1,0:T(8,128)(2,1)}, bf16[8,64,1088]{2,1,0:T(8,128)(2,1)}, u32[]{:S(2)}, u32[]{:S(2)}) %collective-permute-start.26) | collective-permute-done | bytes 1114144 | tf_op jit(solution)/shard_map/ppermute | solution.py:42
  298.0 2.7 fusion.66
  300.7 3.9 concatenate.117
  304.6 6.7 %fusion.71 = (f32[1088]{0:T(1024)S(1)}, f32[256,1088]{0,1:T(8,128)}) fusion(bf16[256,3264]{1,0:T(8,128)(2,1)} %concatenate.117, bf16[1088,3264]{1,0:T(8,128)(2,1)} %copy-done.3), kind=kOutput, calls=%fused_computation.263 | convolution fusion | flops 1818508288 | bytes 9892096 | tf_op jit(solution)/shard_map/dot_general | solution.py:542
  311.3 2.7 copy.92
  317.9 3.9 concatenate.122
  325.7 2.2 pad_maximum_fusion.1.right_ref
  327.9 3.9 shard_map.285
  331.8 2.1 dynamic_update_slice.3.x_ref
  335.8 2.3 collective-permute-start.60
  341.2 3.0 fusion.65
  345.6 2.8 collective-permute-start.32
  348.5 6.4 %collective-permute-done.59 = bf16[144,1088]{1,0:T(8,128)(2,1)} collective-permute-done((bf16[144,1088]{1,0:T(8,128)(2,1)S(1)}, bf16[144,1088]{1,0:T(8,128)(2,1)}, u32[]{:S(2)}, u32[]{:S(2)}) %collective-permute-start.59) | collective-permute-done | bytes 313376 | tf_op jit(solution)/shard_map/ppermute | solution.py:42
  356.5 3.0 collective-permute-start.38
  362.2 3.2 collective-permute-done.32
  366.3 12.9 %collective-permute-done.34 = bf16[4,72,1088]{2,1,0:T(8,128)(2,1)} collective-permute-done((bf16[4,72,1088]{2,1,0:T(8,128)(2,1)}, bf16[4,72,1088]{2,1,0:T(8,128)(2,1)}, u32[]{:S(2)}, u32[]{:S(2)}) %collective-permute-start.34) | collective-permute-done | bytes 626720 | tf_op jit(solution)/shard_map/ppermute | solution.py:42
  380.0 2.0 fusion.28
  382.8 3.0 collective-permute-start.35
  385.9 2.0 collective-permute-start.36
  387.9 7.6 %collective-permute-done.40 = bf16[4,72,1088]{2,1,0:T(8,128)(2,1)} collective-permute-done((bf16[4,72,1088]{2,1,0:T(8,128)(2,1)}, bf16[4,72,1088]{2,1,0:T(8,128)(2,1)}, u32[]{:S(2)}, u32[]{:S(2)}) %collective-permute-start.40) | collective-permute-done | bytes 626720 | tf_op jit(solution)/shard_map/ppermute | solution.py:42
  398.3 3.1 collective-permute-start.41
  403.4 7.0 %fusion.9 = f32[1,256,1088]{2,1,0:T(8,128)S(1)} fusion(f32[256,1088]{1,0:T(8,128)S(1)} %copy-done.29, bf16[256,4352]{1,0:T(8,128)(2,1)S(1)} %copy-done.47, bf16[4352,1088]{1,0:T(8,128)(2,1)} %copy-done, f32[1088]{0:T(1024)S(1)} %copy-done.59), kind=kOutput, calls=%fused_computation.31 | convolution fusion | flops 2424864768 | bytes 13930752 | tf_op jit(solution)/shard_map/dot_general | solution.py:490
  411.9 5.5 %collective-permute-done.43 = bf16[72,1088]{1,0:T(8,128)(2,1)S(1)} collective-permute-done((bf16[72,1088]{1,0:T(8,128)(2,1)S(1)}, bf16[72,1088]{1,0:T(8,128)(2,1)S(1)}, u32[]{:S(2)}, u32[]{:S(2)}) %collective-permute-start.43) | collective-permute-done | bytes 156704 | tf_op jit(solution)/shard_map/ppermute | solution.py:42
  423.0 5.5 %collective-permute-done.45 = bf16[72,1088]{1,0:T(8,128)(2,1)S(1)} collective-permute-done((bf16[72,1088]{1,0:T(8,128)(2,1)S(1)}, bf16[72,1088]{1,0:T(8,128)(2,1)S(1)}, u32[]{:S(2)}, u32[]{:S(2)}) %collective-permute-start.45) | collective-permute-done | bytes 156704 | tf_op jit(solution)/shard_map/ppermute | solution.py:42
  429.7 2.8 collective-permute-start.54
  432.5 2.0 collective-permute-start.55
  436.5 2.9 collective-permute-start.48
  445.1 4.8 collective-permute-done.49
  457.0 2.3 collective-permute-done.51
  459.3 2.7 collective-permute-done.50
  468.3 2.2 shard_map.287
  471.2 3.0 slice_bitcast_fusion
  474.2 2.6 shard_map.290
  476.8 2.8 shard_map.289
  (421 shorter events, 147.0 us)
Async XLA Ops:
  7.3 114.2 %all-gather.5.cloned.1.call-start = ((), (), s32[]{:S(2)}) async-start(), calls=%async_computation.1 | async-start | bytes 2367488 | tf_op jit(solution)/shard_map/all_gather | solution.py:360
  10.8 20.5 %collective-permute-start.7 = (bf16[4,64,1088]{2,1,0:T(8,128)(2,1)S(1)}, bf16[4,64,1088]{2,1,0:T(8,128)(2,1)}, u32[]{:S(2)}, u32[]{:S(2)}) collective-permute-start(bf16[4,64,1088]{2,1,0:T(8,128)(2,1)S(1)} %bitcast.294), channel_id=1, source_target_pairs={{0,1},{1,0},{2,3},{3,2},{4,5},{5,4},{6,7},{7,6},{8,9},{9,8},{10,11... | collective-permute-start | bytes 1671176 | tf_op jit(solution)/shard_map/ppermute | solution.py:42
  12.5 87.7 %collective-permute-start.6 = (bf16[288,3264]{1,0:T(8,128)(2,1)}, bf16[288,3264]{1,0:T(8,128)(2,1)}, u32[]{:S(2)}, u32[]{:S(2)}) collective-permute-start(bf16[288,3264]{1,0:T(8,128)(2,1)} %fusion.16.refs_0_), channel_id=1, source_target_pairs={{0,1},{1,0},{2,3},{3,2},{4,5},{5,4},{6,7},{7,6},{8,9},{9,8},{10,11... | collective-permute-start | bytes 5640200 | tf_op jit(solution)/shard_map/ppermute | solution.py:42
  17.1 19.0 %collective-permute-start = (bf16[96,3264]{1,0:T(8,128)(2,1)}, bf16[96,3264]{1,0:T(8,128)(2,1)}, u32[]{:S(2)}, u32[]{:S(2)}) collective-permute-start(bf16[96,3264]{1,0:T(8,128)(2,1)} %pad_maximum_fusion.12), channel_id=1, source_target_pairs={{0,6},{6,0},{2,4},{4,2},{1,7},{7,1},{3,5},{5,3},{8,14},{14,8},{10,... | collective-permute-start | bytes 1880072 | tf_op jit(solution)/shard_map/ppermute | solution.py:42
  21.2 126.3 %collective-permute-start.15 = (bf16[272,4352]{1,0:T(8,128)(2,1)}, bf16[272,4352]{1,0:T(8,128)(2,1)}, u32[]{:S(2)}, u32[]{:S(2)}) collective-permute-start(bf16[272,4352]{1,0:T(8,128)(2,1)} %refs_0_.2), channel_id=1, source_target_pairs={{0,1},{1,0},{2,3},{3,2},{4,5},{5,4},{6,7},{7,6},{8,9},{9,8},{10,11... | collective-permute-start | bytes 7102472 | tf_op jit(solution)/shard_map/ppermute | solution.py:42
  37.4 9.5 %collective-permute-start.10 = (bf16[32,4352]{1,0:T(8,128)(2,1)}, bf16[32,4352]{1,0:T(8,128)(2,1)S(1)}, u32[]{:S(2)}, u32[]{:S(2)}) collective-permute-start(bf16[32,4352]{1,0:T(8,128)(2,1)} %shard_map.274), channel_id=1, source_target_pairs={{0,6},{6,0},{2,4},{4,2},{1,7},{7,1},{3,5},{5,3},{8,14},{14,8},{10,... | collective-permute-start | bytes 835592 | tf_op jit(solution)/shard_map/ppermute | solution.py:42
  47.6 98.9 %all-gather.9.cloned.1.call-start = ((), (), s32[]{:S(2)}) async-start(), calls=%async_computation.4 | async-start | bytes 2506752 | tf_op jit(solution)/shard_map/all_gather | solution.py:360
  48.8 13.9 %collective-permute-start.1 = (bf16[64,3264]{1,0:T(8,128)(2,1)S(1)}, bf16[64,3264]{1,0:T(8,128)(2,1)S(1)}, u32[]{:S(2)}, u32[]{:S(2)}) collective-permute-start(bf16[64,3264]{1,0:T(8,128)(2,1)S(1)} %slice.334), channel_id=1, source_target_pairs={{0,8},{8,0},{16,24},{24,16},{1,9},{9,1},{17,25},{25,17},{2,10},{10... | collective-permute-start | bytes 1253384 | tf_op jit(solution)/shard_map/ppermute | solution.py:42
  50.3 10.0 %collective-permute-start.2 = (bf16[64,3264]{1,0:T(8,128)(2,1)S(1)}, bf16[64,3264]{1,0:T(8,128)(2,1)S(1)}, u32[]{:S(2)}, u32[]{:S(2)}) collective-permute-start(bf16[64,3264]{1,0:T(8,128)(2,1)S(1)} %slice.334), channel_id=1, source_target_pairs={{0,32},{32,0},{64,96},{96,64},{1,33},{33,1},{65,97},{97,65},{2,34}... | collective-permute-start | bytes 1253384 | tf_op jit(solution)/shard_map/ppermute | solution.py:42
  51.9 15.2 %collective-permute-start.8 = (bf16[4,64,1088]{2,1,0:T(8,128)(2,1)}, bf16[4,64,1088]{2,1,0:T(8,128)(2,1)}, u32[]{:S(2)}, u32[]{:S(2)}) collective-permute-start(bf16[4,64,1088]{2,1,0:T(8,128)(2,1)} %bitcast.308), channel_id=1, source_target_pairs={{0,2},{2,0},{1,3},{3,1},{4,6},{6,4},{5,7},{7,5},{8,10},{10,8},{9,1... | collective-permute-start | bytes 1671176 | tf_op jit(solution)/shard_map/ppermute | solution.py:42
  60.4 15.2 %collective-permute-start.11 = (bf16[2,64,1088]{2,1,0:T(8,128)(2,1)}, bf16[2,64,1088]{2,1,0:T(8,128)(2,1)S(1)}, u32[]{:S(2)}, u32[]{:S(2)}) collective-permute-start(bf16[2,64,1088]{2,1,0:T(8,128)(2,1)} %bitcast.312), channel_id=1, source_target_pairs={{0,6},{6,0},{2,4},{4,2},{1,7},{7,1},{3,5},{5,3},{8,14},{14,8},{10,... | collective-permute-start | bytes 835592 | tf_op jit(solution)/shard_map/ppermute | solution.py:42
  62.7 6.7 %collective-permute-start.3 = (bf16[32,3264]{1,0:T(8,128)(2,1)S(1)}, bf16[32,3264]{1,0:T(8,128)(2,1)S(1)}, u32[]{:S(2)}, u32[]{:S(2)}) collective-permute-start(bf16[32,3264]{1,0:T(8,128)(2,1)S(1)} %slice.335), channel_id=1, source_target_pairs={{0,8},{8,0},{16,24},{24,16},{1,9},{9,1},{17,25},{25,17},{2,10},{10... | collective-permute-start | bytes 626696 | tf_op jit(solution)/shard_map/ppermute | solution.py:42
  67.1 5.8 %collective-permute-start.4 = (bf16[32,3264]{1,0:T(8,128)(2,1)S(1)}, bf16[32,3264]{1,0:T(8,128)(2,1)S(1)}, u32[]{:S(2)}, u32[]{:S(2)}) collective-permute-start(bf16[32,3264]{1,0:T(8,128)(2,1)S(1)} %slice.336), channel_id=1, source_target_pairs={{0,32},{32,0},{64,96},{96,64},{1,33},{33,1},{65,97},{97,65},{2,34}... | collective-permute-start | bytes 626696 | tf_op jit(solution)/shard_map/ppermute | solution.py:42
  73.7 27.1 %collective-permute-start.5 = (bf16[288,3264]{1,0:T(8,128)(2,1)}, bf16[288,3264]{1,0:T(8,128)(2,1)}, u32[]{:S(2)}, u32[]{:S(2)}) collective-permute-start(bf16[288,3264]{1,0:T(8,128)(2,1)} %constant_dynamic-update-slice_fusion.refs_2_), channel_id=1, source_target_pairs={{0,1},{1,0},{2,3},{3,2},{4,5},{5,4},{6,7},{7,6},{8,9},{9,8},{10,11... | collective-permute-start | bytes 5640200 | tf_op jit(solution)/shard_map/ppermute | solution.py:42
  73.7 7.0 %collective-permute-start.9 = (bf16[4,64,1088]{2,1,0:T(8,128)(2,1)}, bf16[4,64,1088]{2,1,0:T(8,128)(2,1)}, u32[]{:S(2)}, u32[]{:S(2)}) collective-permute-start(bf16[4,64,1088]{2,1,0:T(8,128)(2,1)} %collective-permute-done.8), channel_id=1, source_target_pairs={{0,1},{1,0},{2,3},{3,2},{4,5},{5,4},{6,7},{7,6},{8,9},{9,8},{10,11... | collective-permute-start | bytes 1671176 | tf_op jit(solution)/shard_map/ppermute | solution.py:42
  76.4 17.6 %collective-permute-start.13 = (bf16[272,1088]{1,0:T(8,128)(2,1)}, bf16[272,1088]{1,0:T(8,128)(2,1)}, u32[]{:S(2)}, u32[]{:S(2)}) collective-permute-start(bf16[272,1088]{1,0:T(8,128)(2,1)} %shard_map.276.refs_0_), channel_id=1, source_target_pairs={{0,6},{6,0},{2,4},{4,2},{1,7},{7,1},{3,5},{5,3},{8,14},{14,8},{10,... | collective-permute-start | bytes 1775624 | tf_op jit(solution)/shard_map/ppermute | solution.py:42
  80.6 253.4 %reduce-scatter.2.cloned.1.call-start = ((), (), s32[]{:S(2)}) async-start(), calls=%async_computation.2 | async-start | bytes 11280384 | tf_op jit(solution)/shard_map/reduce_scatter | solution.py:515
  80.7 14.9 %collective-permute-start.12 = (bf16[272,1088]{1,0:T(8,128)(2,1)}, bf16[272,1088]{1,0:T(8,128)(2,1)}, u32[]{:S(2)}, u32[]{:S(2)}) collective-permute-start(bf16[272,1088]{1,0:T(8,128)(2,1)} %shard_map.276.refs_0_), channel_id=1, source_target_pairs={{0,1},{1,0},{2,3},{3,2},{4,5},{5,4},{6,7},{7,6},{8,9},{9,8},{10,11... | collective-permute-start | bytes 1775624 | tf_op jit(solution)/shard_map/ppermute | solution.py:42
  95.5 72.7 %collective-permute-start.18 = (bf16[1088,1088]{1,0:T(8,128)(2,1)S(1)}, bf16[1088,1088]{1,0:T(8,128)(2,1)}, u32[]{:S(2)}, u32[]{:S(2)}) collective-permute-start(bf16[1088,1088]{1,0:T(8,128)(2,1)S(1)} %copy-done.1), channel_id=1, source_target_pairs={{0,1},{1,0},{2,3},{3,2},{4,5},{5,4},{6,7},{7,6},{8,9},{9,8},{10,11... | collective-permute-start | bytes 7102472 | tf_op jit(solution)/shard_map/ppermute | solution.py:42
  96.4 50.1 %collective-permute-start.17 = (bf16[16,4352]{1,0:T(8,128)(2,1)S(1)}, bf16[16,4352]{1,0:T(8,128)(2,1)}, u32[]{:S(2)}, u32[]{:S(2)}) collective-permute-start(bf16[16,4352]{1,0:T(8,128)(2,1)S(1)} %get-tuple-element.150.refs_3_), channel_id=1, source_target_pairs={{0,1},{1,0},{2,3},{3,2},{4,5},{5,4},{6,7},{7,6},{8,9},{9,8},{10,11... | collective-permute-start | bytes 417800 | tf_op jit(solution)/shard_map/ppermute | solution.py:42
  100.2 68.1 %collective-permute-start.20 = (bf16[64,1088]{1,0:T(8,128)(2,1)S(1)}, bf16[64,1088]{1,0:T(8,128)(2,1)}, u32[]{:S(2)}, u32[]{:S(2)}) collective-permute-start(bf16[64,1088]{1,0:T(8,128)(2,1)S(1)} %get-tuple-element.148.refs_3_), channel_id=1, source_target_pairs={{0,1},{1,0},{2,3},{3,2},{4,5},{5,4},{6,7},{7,6},{8,9},{9,8},{10,11... | collective-permute-start | bytes 417800 | tf_op jit(solution)/shard_map/ppermute | solution.py:42
  121.5 25.9 %collective-permute-start.16 = (bf16[256,4352]{1,0:T(8,128)(2,1)}, bf16[256,4352]{1,0:T(8,128)(2,1)}, u32[]{:S(2)}, u32[]{:S(2)}) collective-permute-start(bf16[256,4352]{1,0:T(8,128)(2,1)} %all-gather.5.cloned.1.call-done.refs_2_), channel_id=1, source_target_pairs={{0,1},{1,0},{2,3},{3,2},{4,5},{5,4},{6,7},{7,6},{8,9},{9,8},{10,11... | collective-permute-start | bytes 6684680 | tf_op jit(solution)/shard_map/ppermute | solution.py:42
  146.5 21.8 %collective-permute-start.19 = (bf16[16,64,1088]{2,1,0:T(8,128)(2,1)}, bf16[16,64,1088]{2,1,0:T(8,128)(2,1)S(1)}, u32[]{:S(2)}, u32[]{:S(2)}) collective-permute-start(bf16[16,64,1088]{2,1,0:T(8,128)(2,1)} %bitcast.287), channel_id=1, source_target_pairs={{0,1},{1,0},{2,3},{3,2},{4,5},{5,4},{6,7},{7,6},{8,9},{9,8},{10,11... | collective-permute-start | bytes 6684680 | tf_op jit(solution)/shard_map/ppermute | solution.py:42
  191.2 13.9 %collective-permute-start.22 = (bf16[256,4352]{1,0:T(8,128)(2,1)}, bf16[256,4352]{1,0:T(8,128)(2,1)}, u32[]{:S(2)}, u32[]{:S(2)}) collective-permute-start(bf16[256,4352]{1,0:T(8,128)(2,1)} %get-tuple-element.184), channel_id=1, source_target_pairs={{0,1},{1,0},{2,3},{3,2},{4,5},{5,4},{6,7},{7,6},{8,9},{9,8},{10,11... | collective-permute-start | bytes 6684680 | tf_op jit(solution)/shard_map/ppermute | solution.py:42
  193.5 5.3 %collective-permute-start.23 = (bf16[8,64,1088]{2,1,0:T(8,128)(2,1)}, bf16[8,64,1088]{2,1,0:T(8,128)(2,1)}, u32[]{:S(2)}, u32[]{:S(2)}) collective-permute-start(bf16[8,64,1088]{2,1,0:T(8,128)(2,1)} %bitcast.40), channel_id=1, source_target_pairs={{0,1},{1,0},{2,3},{3,2},{4,5},{5,4},{6,7},{7,6},{8,9},{9,8},{10,11... | collective-permute-start | bytes 3342344 | tf_op jit(solution)/shard_map/ppermute | solution.py:42
  195.2 2.8 collective-permute-start.24
  195.9 2.8 collective-permute-start.21
  212.7 258.5 %all-gather.7.cloned.1.call-start = ((), (), s32[]{:S(2)}) async-start(), calls=%async_computation.3 | async-start | bytes 5640192 | tf_op jit(solution)/shard_map/all_gather | solution.py:584
  259.0 4.6 collective-permute-start.25
  265.2 29.9 %collective-permute-start.26 = (bf16[8,64,1088]{2,1,0:T(8,128)(2,1)}, bf16[8,64,1088]{2,1,0:T(8,128)(2,1)}, u32[]{:S(2)}, u32[]{:S(2)}) collective-permute-start(bf16[8,64,1088]{2,1,0:T(8,128)(2,1)} %fusion.15), channel_id=1, source_target_pairs={{0,2},{2,0},{1,3},{3,1},{4,6},{6,4},{5,7},{7,5},{8,10},{10,8},{9,1... | collective-permute-start | bytes 3342344 | tf_op jit(solution)/shard_map/ppermute | solution.py:42
  265.4 7.2 %collective-permute-start.30 = (bf16[4,64,1088]{2,1,0:T(8,128)(2,1)}, bf16[4,64,1088]{2,1,0:T(8,128)(2,1)}, u32[]{:S(2)}, u32[]{:S(2)}) collective-permute-start(bf16[4,64,1088]{2,1,0:T(8,128)(2,1)} %bitcast.70), channel_id=1, source_target_pairs={{0,1},{1,0},{2,3},{3,2},{4,5},{5,4},{6,7},{7,6},{8,9},{9,8},{10,11... | collective-permute-start | bytes 1671176 | tf_op jit(solution)/shard_map/ppermute | solution.py:42
  265.9 2.4 collective-permute-start.27
  321.7 4.0 collective-permute-start.28
  321.8 3.2 collective-permute-start.31
  335.8 20.7 %collective-permute-start.60 = (bf16[144,1088]{1,0:T(8,128)(2,1)}, bf16[144,1088]{1,0:T(8,128)(2,1)S(1)}, u32[]{:S(2)}, u32[]{:S(2)}) collective-permute-start(bf16[144,1088]{1,0:T(8,128)(2,1)} %bitcast.123), channel_id=1, source_target_pairs={{0,6},{6,0},{2,4},{4,2},{1,7},{7,1},{3,5},{5,3},{8,14},{14,8},{10,... | collective-permute-start | bytes 940040 | tf_op jit(solution)/shard_map/ppermute | solution.py:42
  338.1 21.4 %collective-permute-start.61 = (bf16[144,1088]{1,0:T(8,128)(2,1)}, bf16[144,1088]{1,0:T(8,128)(2,1)}, u32[]{:S(2)}, u32[]{:S(2)}) collective-permute-start(bf16[144,1088]{1,0:T(8,128)(2,1)} %bitcast.123), channel_id=1, source_target_pairs={{0,2},{2,0},{1,3},{3,1},{4,6},{6,4},{5,7},{7,5},{8,10},{10,8},{9,1... | collective-permute-start | bytes 940040 | tf_op jit(solution)/shard_map/ppermute | solution.py:42
  339.4 15.6 %collective-permute-start.59 = (bf16[144,1088]{1,0:T(8,128)(2,1)S(1)}, bf16[144,1088]{1,0:T(8,128)(2,1)}, u32[]{:S(2)}, u32[]{:S(2)}) collective-permute-start(bf16[144,1088]{1,0:T(8,128)(2,1)S(1)} %bitcast.311), channel_id=1, source_target_pairs={{0,4},{4,0},{1,5},{5,1},{2,6},{6,2},{3,7},{7,3},{8,12},{12,8},{9,1... | collective-permute-start | bytes 940040 | tf_op jit(solution)/shard_map/ppermute | solution.py:42
  345.6 19.7 %collective-permute-start.32 = (bf16[4,72,1088]{2,1,0:T(8,128)(2,1)}, bf16[4,72,1088]{2,1,0:T(8,128)(2,1)}, u32[]{:S(2)}, u32[]{:S(2)}) collective-permute-start(bf16[4,72,1088]{2,1,0:T(8,128)(2,1)} %get-tuple-element.94), channel_id=1, source_target_pairs={{0,16},{8,24},{16,0},{24,8},{1,17},{9,25},{17,1},{25,9},{2,18},{10... | collective-permute-start | bytes 1880072 | tf_op jit(solution)/shard_map/ppermute | solution.py:42
  348.4 30.8 %collective-permute-start.34 = (bf16[4,72,1088]{2,1,0:T(8,128)(2,1)}, bf16[4,72,1088]{2,1,0:T(8,128)(2,1)}, u32[]{:S(2)}, u32[]{:S(2)}) collective-permute-start(bf16[4,72,1088]{2,1,0:T(8,128)(2,1)} %get-tuple-element.95), channel_id=1, source_target_pairs={{0,24},{8,0},{16,8},{24,16},{1,25},{9,1},{17,9},{25,17},{2,26},{10... | collective-permute-start | bytes 1880072 | tf_op jit(solution)/shard_map/ppermute | solution.py:42
  354.9 25.1 %collective-permute-start.33 = (bf16[4,72,1088]{2,1,0:T(8,128)(2,1)}, bf16[4,72,1088]{2,1,0:T(8,128)(2,1)}, u32[]{:S(2)}, u32[]{:S(2)}) collective-permute-start(bf16[4,72,1088]{2,1,0:T(8,128)(2,1)} %get-tuple-element.96), channel_id=1, source_target_pairs={{0,8},{8,16},{16,24},{24,0},{1,9},{9,17},{17,25},{25,1},{2,10},{10... | collective-permute-start | bytes 1880072 | tf_op jit(solution)/shard_map/ppermute | solution.py:42
  356.5 29.4 %collective-permute-start.38 = (bf16[4,72,1088]{2,1,0:T(8,128)(2,1)}, bf16[4,72,1088]{2,1,0:T(8,128)(2,1)}, u32[]{:S(2)}, u32[]{:S(2)}) collective-permute-start(bf16[4,72,1088]{2,1,0:T(8,128)(2,1)} %get-tuple-element.91), channel_id=1, source_target_pairs={{0,64},{32,96},{64,0},{96,32},{1,65},{33,97},{65,1},{97,33},{2,66}... | collective-permute-start | bytes 1880072 | tf_op jit(solution)/shard_map/ppermute | solution.py:42
  359.5 35.9 %collective-permute-start.40 = (bf16[4,72,1088]{2,1,0:T(8,128)(2,1)}, bf16[4,72,1088]{2,1,0:T(8,128)(2,1)}, u32[]{:S(2)}, u32[]{:S(2)}) collective-permute-start(bf16[4,72,1088]{2,1,0:T(8,128)(2,1)} %get-tuple-element.92), channel_id=1, source_target_pairs={{0,96},{32,0},{64,32},{96,64},{1,97},{33,1},{65,33},{97,65},{2,98}... | collective-permute-start | bytes 1880072 | tf_op jit(solution)/shard_map/ppermute | solution.py:42
  365.4 30.1 %collective-permute-start.39 = (bf16[4,72,1088]{2,1,0:T(8,128)(2,1)}, bf16[4,72,1088]{2,1,0:T(8,128)(2,1)S(1)}, u32[]{:S(2)}, u32[]{:S(2)}) collective-permute-start(bf16[4,72,1088]{2,1,0:T(8,128)(2,1)} %get-tuple-element.93), channel_id=1, source_target_pairs={{0,32},{32,64},{64,96},{96,0},{1,33},{33,65},{65,97},{97,1},{2,34}... | collective-permute-start | bytes 1880072 | tf_op jit(solution)/shard_map/ppermute | solution.py:42
  382.8 20.1 %collective-permute-start.35 = (bf16[72,1088]{1,0:T(8,128)(2,1)S(1)}, bf16[72,1088]{1,0:T(8,128)(2,1)S(1)}, u32[]{:S(2)}, u32[]{:S(2)}) collective-permute-start(bf16[72,1088]{1,0:T(8,128)(2,1)S(1)} %get-tuple-element.124), channel_id=1, source_target_pairs={{0,64},{32,96},{64,0},{96,32},{1,65},{33,97},{65,1},{97,33},{2,66}... | collective-permute-start | bytes 470024 | tf_op jit(solution)/shard_map/ppermute | solution.py:42
  385.8 26.0 %collective-permute-start.37 = (bf16[72,1088]{1,0:T(8,128)(2,1)}, bf16[72,1088]{1,0:T(8,128)(2,1)}, u32[]{:S(2)}, u32[]{:S(2)}) collective-permute-start(bf16[72,1088]{1,0:T(8,128)(2,1)} %get-tuple-element.125), channel_id=1, source_target_pairs={{0,96},{32,0},{64,32},{96,64},{1,97},{33,1},{65,33},{97,65},{2,98}... | collective-permute-start | bytes 470024 | tf_op jit(solution)/shard_map/ppermute | solution.py:42
  385.9 26.0 %collective-permute-start.36 = (bf16[72,1088]{1,0:T(8,128)(2,1)}, bf16[72,1088]{1,0:T(8,128)(2,1)}, u32[]{:S(2)}, u32[]{:S(2)}) collective-permute-start(bf16[72,1088]{1,0:T(8,128)(2,1)} %get-tuple-element.126), channel_id=1, source_target_pairs={{0,32},{32,64},{64,96},{96,0},{1,33},{33,65},{65,97},{97,1},{2,34}... | collective-permute-start | bytes 470024 | tf_op jit(solution)/shard_map/ppermute | solution.py:42
  398.3 13.6 %collective-permute-start.41 = (bf16[72,1088]{1,0:T(8,128)(2,1)S(1)}, bf16[72,1088]{1,0:T(8,128)(2,1)S(1)}, u32[]{:S(2)}, u32[]{:S(2)}) collective-permute-start(bf16[72,1088]{1,0:T(8,128)(2,1)S(1)} %get-tuple-element.121), channel_id=1, source_target_pairs={{0,16},{8,24},{16,0},{24,8},{1,17},{9,25},{17,1},{25,9},{2,18},{10... | collective-permute-start | bytes 470024 | tf_op jit(solution)/shard_map/ppermute | solution.py:42
  401.4 16.0 %collective-permute-start.43 = (bf16[72,1088]{1,0:T(8,128)(2,1)S(1)}, bf16[72,1088]{1,0:T(8,128)(2,1)S(1)}, u32[]{:S(2)}, u32[]{:S(2)}) collective-permute-start(bf16[72,1088]{1,0:T(8,128)(2,1)S(1)} %get-tuple-element.122), channel_id=1, source_target_pairs={{0,24},{8,0},{16,8},{24,16},{1,25},{9,1},{17,9},{25,17},{2,26},{10... | collective-permute-start | bytes 470024 | tf_op jit(solution)/shard_map/ppermute | solution.py:42
  402.9 14.5 %collective-permute-start.42 = (bf16[72,1088]{1,0:T(8,128)(2,1)S(1)}, bf16[72,1088]{1,0:T(8,128)(2,1)}, u32[]{:S(2)}, u32[]{:S(2)}) collective-permute-start(bf16[72,1088]{1,0:T(8,128)(2,1)S(1)} %get-tuple-element.123), channel_id=1, source_target_pairs={{0,8},{8,16},{16,24},{24,0},{1,9},{9,17},{17,25},{25,1},{2,10},{10... | collective-permute-start | bytes 470024 | tf_op jit(solution)/shard_map/ppermute | solution.py:42
  418.8 9.7 %collective-permute-start.45 = (bf16[72,1088]{1,0:T(8,128)(2,1)S(1)}, bf16[72,1088]{1,0:T(8,128)(2,1)S(1)}, u32[]{:S(2)}, u32[]{:S(2)}) collective-permute-start(bf16[72,1088]{1,0:T(8,128)(2,1)S(1)} %broadcast_select_fusion.10), channel_id=1, source_target_pairs={{0,6},{6,0},{2,4},{4,2},{1,7},{7,1},{3,5},{5,3},{8,14},{14,8},{10,... | collective-permute-start | bytes 470024 | tf_op jit(solution)/shard_map/ppermute | solution.py:42
  420.8 8.4 %collective-permute-start.46 = (bf16[72,1088]{1,0:T(8,128)(2,1)S(1)}, bf16[72,1088]{1,0:T(8,128)(2,1)S(1)}, u32[]{:S(2)}, u32[]{:S(2)}) collective-permute-start(bf16[72,1088]{1,0:T(8,128)(2,1)S(1)} %broadcast_select_fusion.10), channel_id=1, source_target_pairs={{0,2},{2,0},{1,3},{3,1},{4,6},{6,4},{5,7},{7,5},{8,10},{10,8},{9,1... | collective-permute-start | bytes 470024 | tf_op jit(solution)/shard_map/ppermute | solution.py:42
  421.4 8.2 %collective-permute-start.44 = (bf16[72,1088]{1,0:T(8,128)(2,1)S(1)}, bf16[72,1088]{1,0:T(8,128)(2,1)S(1)}, u32[]{:S(2)}, u32[]{:S(2)}) collective-permute-start(bf16[72,1088]{1,0:T(8,128)(2,1)S(1)} %get-tuple-element.74), channel_id=1, source_target_pairs={{0,4},{4,0},{1,5},{5,1},{2,6},{6,2},{3,7},{7,3},{8,12},{12,8},{9,1... | collective-permute-start | bytes 470024 | tf_op jit(solution)/shard_map/ppermute | solution.py:42
  429.7 10.5 %collective-permute-start.54 = (bf16[32,1088]{1,0:T(8,128)(2,1)S(1)}, bf16[32,1088]{1,0:T(8,128)(2,1)S(1)}, u32[]{:S(2)}, u32[]{:S(2)}) collective-permute-start(bf16[32,1088]{1,0:T(8,128)(2,1)S(1)} %slice.380), channel_id=1, source_target_pairs={{0,64},{32,96},{64,0},{96,32},{1,65},{33,97},{65,1},{97,33},{2,66}... | collective-permute-start | bytes 208904 | tf_op jit(solution)/shard_map/ppermute | solution.py:42
  432.5 8.9 %collective-permute-start.53 = (bf16[32,1088]{1,0:T(8,128)(2,1)S(1)}, bf16[32,1088]{1,0:T(8,128)(2,1)S(1)}, u32[]{:S(2)}, u32[]{:S(2)}) collective-permute-start(bf16[32,1088]{1,0:T(8,128)(2,1)S(1)} %slice.380), channel_id=1, source_target_pairs={{0,96},{32,0},{64,32},{96,64},{1,97},{33,1},{65,33},{97,65},{2,98}... | collective-permute-start | bytes 208904 | tf_op jit(solution)/shard_map/ppermute | solution.py:42
  432.5 8.9 %collective-permute-start.55 = (bf16[32,1088]{1,0:T(8,128)(2,1)S(1)}, bf16[32,1088]{1,0:T(8,128)(2,1)S(1)}, u32[]{:S(2)}, u32[]{:S(2)}) collective-permute-start(bf16[32,1088]{1,0:T(8,128)(2,1)S(1)} %slice.380), channel_id=1, source_target_pairs={{0,32},{32,64},{64,96},{96,0},{1,33},{33,65},{65,97},{97,1},{2,34}... | collective-permute-start | bytes 208904 | tf_op jit(solution)/shard_map/ppermute | solution.py:42
  436.5 7.8 %collective-permute-start.48 = (bf16[40,1088]{1,0:T(8,128)(2,1)S(1)}, bf16[40,1088]{1,0:T(8,128)(2,1)S(1)}, u32[]{:S(2)}, u32[]{:S(2)}) collective-permute-start(bf16[40,1088]{1,0:T(8,128)(2,1)S(1)} %slice.379), channel_id=1, source_target_pairs={{0,16},{8,24},{16,0},{24,8},{1,17},{9,25},{17,1},{25,9},{2,18},{10... | collective-permute-start | bytes 261128 | tf_op jit(solution)/shard_map/ppermute | solution.py:42
  439.4 5.7 %collective-permute-start.47 = (bf16[40,1088]{1,0:T(8,128)(2,1)S(1)}, bf16[40,1088]{1,0:T(8,128)(2,1)S(1)}, u32[]{:S(2)}, u32[]{:S(2)}) collective-permute-start(bf16[40,1088]{1,0:T(8,128)(2,1)S(1)} %slice.379), channel_id=1, source_target_pairs={{0,24},{8,0},{16,8},{24,16},{1,25},{9,1},{17,9},{25,17},{2,26},{10... | collective-permute-start | bytes 261128 | tf_op jit(solution)/shard_map/ppermute | solution.py:42
  440.2 9.7 %collective-permute-start.49 = (bf16[40,1088]{1,0:T(8,128)(2,1)S(1)}, bf16[40,1088]{1,0:T(8,128)(2,1)S(1)}, u32[]{:S(2)}, u32[]{:S(2)}) collective-permute-start(bf16[40,1088]{1,0:T(8,128)(2,1)S(1)} %slice.379), channel_id=1, source_target_pairs={{0,8},{8,16},{16,24},{24,0},{1,9},{9,17},{17,25},{25,1},{2,10},{10... | collective-permute-start | bytes 261128 | tf_op jit(solution)/shard_map/ppermute | solution.py:42
  441.5 11.8 %collective-permute-start.57 = (bf16[4,32,1088]{2,1,0:T(8,128)(2,1)S(1)}, bf16[4,32,1088]{2,1,0:T(8,128)(2,1)S(1)}, u32[]{:S(2)}, u32[]{:S(2)}) collective-permute-start(bf16[4,32,1088]{2,1,0:T(8,128)(2,1)S(1)} %pad_maximum_fusion.23), channel_id=1, source_target_pairs={{0,16},{8,24},{16,0},{24,8},{1,17},{9,25},{17,1},{25,9},{2,18},{10... | collective-permute-start | bytes 835592 | tf_op jit(solution)/shard_map/ppermute | solution.py:42
  442.3 12.4 %collective-permute-start.56 = (bf16[4,32,1088]{2,1,0:T(8,128)(2,1)S(1)}, bf16[4,32,1088]{2,1,0:T(8,128)(2,1)S(1)}, u32[]{:S(2)}, u32[]{:S(2)}) collective-permute-start(bf16[4,32,1088]{2,1,0:T(8,128)(2,1)S(1)} %pad_maximum_fusion.23), channel_id=1, source_target_pairs={{0,24},{8,0},{16,8},{24,16},{1,25},{9,1},{17,9},{25,17},{2,26},{10... | collective-permute-start | bytes 835592 | tf_op jit(solution)/shard_map/ppermute | solution.py:42
  444.3 12.2 %collective-permute-start.58 = (bf16[4,32,1088]{2,1,0:T(8,128)(2,1)S(1)}, bf16[4,32,1088]{2,1,0:T(8,128)(2,1)S(1)}, u32[]{:S(2)}, u32[]{:S(2)}) collective-permute-start(bf16[4,32,1088]{2,1,0:T(8,128)(2,1)S(1)} %pad_maximum_fusion.23), channel_id=1, source_target_pairs={{0,8},{8,16},{16,24},{24,0},{1,9},{9,17},{17,25},{25,1},{2,10},{10... | collective-permute-start | bytes 835592 | tf_op jit(solution)/shard_map/ppermute | solution.py:42
  450.1 9.2 %collective-permute-start.51 = (bf16[4,40,1088]{2,1,0:T(8,128)(2,1)S(1)}, bf16[4,40,1088]{2,1,0:T(8,128)(2,1)S(1)}, u32[]{:S(2)}, u32[]{:S(2)}) collective-permute-start(bf16[4,40,1088]{2,1,0:T(8,128)(2,1)S(1)} %pad_maximum_fusion.21), channel_id=1, source_target_pairs={{0,64},{32,96},{64,0},{96,32},{1,65},{33,97},{65,1},{97,33},{2,66}... | collective-permute-start | bytes 1044488 | tf_op jit(solution)/shard_map/ppermute | solution.py:42
  451.3 10.7 %collective-permute-start.50 = (bf16[4,40,1088]{2,1,0:T(8,128)(2,1)S(1)}, bf16[4,40,1088]{2,1,0:T(8,128)(2,1)S(1)}, u32[]{:S(2)}, u32[]{:S(2)}) collective-permute-start(bf16[4,40,1088]{2,1,0:T(8,128)(2,1)S(1)} %pad_maximum_fusion.21), channel_id=1, source_target_pairs={{0,96},{32,0},{64,32},{96,64},{1,97},{33,1},{65,33},{97,65},{2,98}... | collective-permute-start | bytes 1044488 | tf_op jit(solution)/shard_map/ppermute | solution.py:42
  453.3 9.8 %collective-permute-start.52 = (bf16[4,40,1088]{2,1,0:T(8,128)(2,1)S(1)}, bf16[4,40,1088]{2,1,0:T(8,128)(2,1)S(1)}, u32[]{:S(2)}, u32[]{:S(2)}) collective-permute-start(bf16[4,40,1088]{2,1,0:T(8,128)(2,1)S(1)} %pad_maximum_fusion.21), channel_id=1, source_target_pairs={{0,32},{32,64},{64,96},{96,0},{1,33},{33,65},{65,97},{97,1},{2,34}... | collective-permute-start | bytes 1044488 | tf_op jit(solution)/shard_map/ppermute | solution.py:42
  (73 other events, 575.8 us)
Sparse Core Ops, SparseCore 0:
  47.7 46.5 all-gather.4
  96.5 45.0 all-gather.8
  212.8 89.8 reduce-scatter.1
  362.3 65.5 all-gather.6

commit v2 on v1

--- a/solution.py
+++ b/solution.py
@@ -15,7 +15,7 @@
 QUART = 272
 SLICE = 68
 PAD = 72
-VECTOR = 204
+VECTOR = 272
 AXES = ("y", "x", "zl", "zh", "c")
 BF = jnp.bfloat16
 F32 = jnp.float32
@@ -27,8 +27,10 @@
     return centre * lax.rsqrt(spread + 1e-05) * gain + shift
 
 
-def exact_gelu(values):
-    return jax.nn.gelu(values, approximate=False)
+def gelu_both(values):
+    below = 0.5 * (1.0 + lax.erf(values * 0.7071067811865476))
+    density = jnp.exp(values * values * -0.5) * 0.3989422804014327
+    return values * below, below + values * density
 
 
 def rows_major(x):
@@ -81,13 +83,10 @@
     )(x, done)
 
 
-def pick(values, index, dim):
-    start = [0] * values.ndim
-    start[dim] = index
-    size = list(values.shape)
-    size[dim] = 1
-    part = lax.dynamic_slice(values, start, size, allow_negative_indices=False)
-    return part.reshape(size[:dim] + size[dim + 1 :])
+def rows_of(values, start, size):
+    return lax.dynamic_slice(
+        values, (start, 0), (size, values.shape[1]), allow_negative_indices=False
+    )
 
 
 def natural(parts, place):
@@ -100,14 +99,10 @@
     return jnp.stack(found)
 
 
-def ring_scatter(values, axis, dim):
+def ring_scatter(part, axis):
     place = lax.axis_index(axis)
-
-    def part(step):
-        return pick(values, (place + step) & 3, dim)
-
-    got = [rotate(part(step), axis, step) for step in (2, 1, 3)]
-    total = part(0).astype(F32)
+    got = [rotate(part((place + step) & 3), axis, step) for step in (2, 1, 3)]
+    total = part(place).astype(F32)
     for value in got:
         total = total + value.astype(F32)
     return total.astype(BF)
@@ -271,42 +266,52 @@
     )(queries, keys, values, mask, totals, d_mixed)
 
 
-def weight_grad_kernel(left_ref, right_ref, *refs):
-    out_ref = refs[-1]
-    left = left_ref[0]
+def weight_grad_kernel(count, first, *refs):
+    lefts, rights = refs[:2], refs[2 : 2 + 2 * count]
+    vector_ref, out_ref = refs[2 + 2 * count], refs[-1]
+    left, left_other = lefts[0][0], lefts[1][0]
     pieces = left.shape[1] // SLICE
-    empty = jnp.zeros((PAD - SLICE, D), BF)
-    for at in range(right_ref.shape[1] // D):
-        product = dot_tn(left, right_ref[:, at * D : (at + 1) * D])
-        for piece in range(pieces):
-            part = product[piece * SLICE : (piece + 1) * SLICE].astype(BF)
-            out_ref[at * pieces + piece, 0, 0] = jnp.concatenate([part, empty])
-
-
-def weight_grad(left, right, slots, first, slot, buffer=None):
-    _, tokens, width = left.shape
-    pieces = right.shape[1] // D * (width // SLICE)
-    in_specs = [
-        pl.BlockSpec((1, tokens, width), lambda at: (at, 0, 0)),
-        pl.BlockSpec(right.shape, lambda at: (0, 0)),
-    ]
+    done = 0
+    for own, other in zip(rights[::2], rights[1::2]):
+        for at in range(own.shape[-1] // D):
+            lanes = slice(at * D, (at + 1) * D)
+            product = dot_tn(left, own[:, lanes]) + dot_tn(left_other, other[:, lanes])
+            for piece in range(pieces):
+                part = product[piece * SLICE : (piece + 1) * SLICE]
+                empty = jnp.zeros((PAD - SLICE, D), F32)
+                if first == 0 and count == 3:
+                    row = vector_ref[0, done : done + 1]
+                    empty = jnp.concatenate([row, empty[1:]])
+                out_ref[done, 0, 0] = jnp.concatenate([part, empty]).astype(BF)
+                done += 1
+
+
+def weight_grad(lefts, rights, vectors, slots, first, slot, buffer=None):
+    _, tokens, width = lefts[0].shape
+    rights = [value for pair in rights for value in pair]
+    blocks = sum(value.shape[1] for value in rights[::2]) // D
+    pieces = blocks * (width // SLICE)
+    in_specs = [pl.BlockSpec((1, tokens, width), lambda at: (at, 0, 0))] * 2
+    in_specs += [pl.BlockSpec(value.shape, lambda at: (0, 0)) for value in rights]
+    in_specs += [pl.BlockSpec((1,) + vectors.shape[1:], lambda at: (at, 0, 0))]
     more = () if buffer is None else (buffer,)
+    operands = (*lefts, *rights, vectors)
     return pl.pallas_call(
-        weight_grad_kernel,
+        functools.partial(weight_grad_kernel, len(rights) // 2, first),
         grid=(2,),
         out_shape=jax.ShapeDtypeStruct((16, slots, 2, PAD, D), BF),
         in_specs=in_specs + [pl.BlockSpec(memory_space=pl.ANY)] * len(more),
         out_specs=pl.BlockSpec(
             (pieces, 1, 1, PAD, D), lambda at: (first // pieces, slot, at, 0, 0)
         ),
-        input_output_aliases={2: 0} if more else {},
+        input_output_aliases={len(operands): 0} if more else {},
         compiler_params=pltpu.CompilerParams(vmem_limit_bytes=48 * 2**20),
         cost_estimate=pl.CostEstimate(
-            flops=4 * tokens * width * right.shape[1],
-            bytes_accessed=2 * left.size + 2 * right.size + 2 * pieces * 2 * PAD * D,
+            flops=8 * tokens * width * blocks * D,
+            bytes_accessed=2 * sum(value.size for value in operands) + 4 * pieces * PAD * D,
             transcendentals=0,
         ),
-    )(left, right, *more)
+    )(*operands, *more)
 
 
 def unpack_kernel(in_ref, out_ref):
@@ -331,27 +336,20 @@
     )(pieces)
 
 
-def gather_direct(shard):
-    far = swap_far(shard)
-    return shard, swap_core(shard), far, swap_core(far)
-
-
-def gather_quarters(shard):
+def gather_quarters(shard, small):
     across, down = lax.axis_index("x") & 1, lax.axis_index("y") & 1
     quarter = down * 2 + across
-    main = shard[:256].reshape(4, 64, shard.shape[1])
-    piece = pick(main, quarter, 0)
-    got = swap_far(jnp.concatenate([piece, shard[256:]]))
+    piece = rows_of(shard, quarter * 64, 64)
+    got = swap_far(jnp.concatenate([piece, shard[256:], small]))
     mine = got[:64]
     by_x, by_y = swap_pair(mine, "x"), swap_pair(mine, "y")
     last_x, last_y = swap_pair(by_y[:32], "x"), swap_pair(by_x[32:], "y")
-    return got, jnp.concatenate([got, by_x, by_y, last_x, last_y])
+    return by_x, jnp.concatenate([got, by_x, by_y, last_x, last_y])
 
 
 def far_piece(shard, spot, done):
     unit = shard.shape[0] // 17
-    main = shard[: 16 * unit].reshape(16, unit, shard.shape[1])
-    piece = pick(main, spot, 0)
+    piece = rows_of(shard, spot * unit, unit)
     return swap_far(after(jnp.concatenate([piece, shard[16 * unit :]]), done))
 
 
@@ -411,21 +409,19 @@
     small = jnp.pad(small[None], ((0, 15), (0, 0)))
     rows = block_input.shape[1]
     own_tokens = block_input[0]
-    with_small = jnp.concatenate([w_qkv, small])
-    beside = swap_core(with_small)
-    got_qkv, far_parts = gather_quarters(with_small)
+    by_x, far_parts = gather_quarters(w_qkv, small)
+    beside = swap_core(jnp.concatenate([w_qkv, small]))
     across_parts = swap_core(far_parts)
-    half_tokens = swap_half(after(own_tokens, got_qkv))
+    half_tokens = swap_half(after(own_tokens, by_x))
     tokens = [own_tokens, swap_core(own_tokens), half_tokens, swap_core(half_tokens)]
-    got_up = far_piece(w_up, spot, got_qkv)
+    got_up = far_piece(w_up, spot, by_x)
     got_down = far_piece(w_down, spot, got_up)
-    out_parts = gather_direct(after(w_out, got_down))
     full_up = gather_spread(w_up, got_up)
     full_down = gather_spread(w_down, got_down)
     turns = ((0, 0, 0, 64), (96, 0, 1, 64), (160, 0, 2, 64), (224, 0, 3, 64), (64, 256, None, 16))
     full_qkv = assemble(
         QUART,
-        (with_small, beside, far_parts, across_parts),
+        (w_qkv, beside, far_parts, across_parts),
         ((0, 0, 0, 0, None, QUART), (1, 0, 1, 0, None, QUART))
         + tuple((2, row, 2, *turn) for row, *turn in turns)
         + tuple((3, row, 3, *turn) for row, *turn in turns),
@@ -433,8 +429,11 @@
     smalls = [
         value.astype(F32) for value in (small[0], beside[QUART], far_parts[80], across_parts[80])
     ]
+    far_out = after(swap_far(after(w_out, got_down)), full_qkv)
     full_out = assemble(
-        QUART, out_parts, tuple((flip, 0, flip, 0, None, QUART) for flip in range(4))
+        QUART,
+        (w_out, swap_core(w_out), far_out, swap_core(far_out)),
+        tuple((flip, 0, flip, 0, None, QUART) for flip in range(4)),
     )
 
     ordered = []
@@ -486,11 +485,12 @@
     middle = hidden_in + jnp.dot(mixed, full_out, preferred_element_type=F32) + out_bias
     normed_two = layer_norm(middle, gain_two, shift_two).astype(BF)
     upper = jnp.dot(normed_two, full_up, preferred_element_type=F32) + up_bias
-    activated = exact_gelu(upper).astype(BF)
+    activated, slope = gelu_both(upper)
+    activated = activated.astype(BF)
     block_output = middle + jnp.dot(activated, full_down, preferred_element_type=F32) + down_bias
 
     def paired(value):
-        return jnp.concatenate([value, swap_core(value)])
+        return value, swap_core(value)
 
     def paired_columns(value):
         width = value.shape[1] // 4
@@ -498,7 +498,7 @@
         even, odd = jnp.stack([blocks[0], blocks[2]]), jnp.stack([blocks[1], blocks[3]])
         mine = jnp.where(core == 0, even, odd)
         other = jnp.where(core == 0, odd, even)
-        return jnp.concatenate([mine, swap_core(other)], axis=1)
+        return mine, swap_core(other)
 
     upstream_wide = upstream.astype(F32)
     upstream_pair = paired(upstream)
@@ -506,12 +506,14 @@
     activated_pair = paired_columns(activated)
 
     d_activated = jnp.dot(upstream, full_down.T, preferred_element_type=F32)
-    gelu_back = jax.vjp(exact_gelu, upper)[1]
-    d_upper = gelu_back(d_activated)[0].astype(BF)
+    d_upper = (d_activated * slope).astype(BF)
     grad_up_bias = jnp.sum(d_upper.astype(F32), axis=0)
     normed_two_pair, d_upper_pair = paired_columns(normed_two), paired(d_upper)
-    grad_mlp = weight_grad(activated_pair, upstream_pair, 2, 0, 0)
-    grad_mlp = weight_grad(normed_two_pair, d_upper_pair, 2, 0, 1, grad_mlp)
+    no_vectors = jnp.zeros((2, 12, D), F32)
+    grad_mlp = weight_grad(activated_pair, [upstream_pair], no_vectors, 2, 0, 0)
+    grad_mlp = weight_grad(
+        normed_two_pair, [d_upper_pair], no_vectors, 2, 0, 1, grad_mlp
+    )
     mlp_part = lax.psum_scatter(
         grad_mlp.reshape(64 * PAD, D), ("y", "x"), scatter_dimension=0, tiled=True
     ).reshape(2, 2, PAD, D)
@@ -533,13 +535,19 @@
     d_half = swap_half((d_both[1].astype(F32) + d_beside[1].astype(F32)).astype(BF))
     d_both = d_both[0].astype(F32) + d_beside[0].astype(F32) + d_half.astype(F32)
     d_both = d_both.astype(BF)
-    d_project = jnp.concatenate([d_queries, d_both[0], d_both[1]], axis=1)
+    d_keys, d_values = d_both[0], d_both[1]
     grad_query_bias = jnp.sum(d_queries.astype(F32), axis=0)
-    grad_value_bias = jnp.sum(d_both[1].astype(F32), axis=0)
-    grad_attn = weight_grad(mixed_pair, d_attended_pair, 1, 12, 0)
-    grad_attn = weight_grad(normed_pair, paired(d_project), 1, 0, 0, grad_attn)
-
-    d_normed = jnp.dot(d_project, full_qkv.T, preferred_element_type=F32)
+    grad_value_bias = jnp.sum(d_values.astype(F32), axis=0)
+    rights = [paired(d_queries), paired(d_keys), paired(d_values)]
+    d_normed = None
+    for at, part in enumerate((d_queries, d_keys, d_values)):
+        term = lax.dot_general(
+            part,
+            full_qkv[:, at * D : (at + 1) * D],
+            (((1,), (1,)), ((), ())),
+            preferred_element_type=F32,
+        )
+        d_normed = term if d_normed is None else d_normed + term
     norm_one_back = jax.vjp(layer_norm, hidden_in, gain_one, shift_one)[1]
     d_input_part, grad_gain_one, grad_shift_one = norm_one_back(d_normed)
     grad_input = d_middle + d_input_part
@@ -565,25 +573,44 @@
     mine = jnp.where(core == 0, even, odd)
     other = jnp.where(core == 0, odd, even)
     mine = (mine + swap_core(other.astype(BF)).astype(F32)).astype(BF)
-    mine = mine.reshape(2, 16, VECTOR).transpose(1, 0, 2)[:, :, None]
-
-    grad_attn = lax.dynamic_update_slice(grad_attn[:, 0], mine, (0, 0, SLICE, 0))
-    grad_attn = after(grad_attn, mlp_part)
-    one = ring_scatter(grad_attn[:, 0].reshape(4, 4, PAD, D), "x", 1)
-    two = ring_scatter(grad_attn[:, 1].reshape(4, 4, PAD, D), "y", 0)
-    one, two = ring_scatter(one, "y", 0), ring_scatter(two, "x", 0)
+    mine = jnp.pad(mine.reshape(2, 12, VECTOR).astype(F32), ((0, 0), (0, 0), (0, D - VECTOR)))
+
+    early = depth_sum(mlp_part.transpose(1, 0, 2, 3).reshape(2, 2 * PAD, D), zh)
+    normed_pair = (normed_pair[0], after(normed_pair[1], early))
+    grad_attn = weight_grad(mixed_pair, [d_attended_pair], no_vectors, 1, 12, 0)
+    grad_attn = weight_grad(normed_pair, rights, mine, 1, 0, 0, grad_attn)
+    grad_attn = grad_attn.reshape(4, 4, 2, PAD, D)
+
+    def cut(start, size):
+        return lax.dynamic_slice(grad_attn, start, size, allow_negative_indices=False)
+
+    def part_of(values):
+        return lambda place: cut_row(values, place)
+
+    def cut_row(values, place):
+        return lax.dynamic_slice(
+            values, (place, 0, 0), (1, PAD, D), allow_negative_indices=False
+        )[0]
+
+    one = ring_scatter(
+        lambda place: cut((0, place, 0, 0, 0), (4, 1, 1, PAD, D)).reshape(4, PAD, D), "x"
+    )
+    two = ring_scatter(
+        lambda place: cut((place, 0, 1, 0, 0), (1, 4, 1, PAD, D)).reshape(4, PAD, D), "y"
+    )
+    one, two = ring_scatter(part_of(one), "y"), ring_scatter(part_of(two), "x")
     attn_part = depth_sum(jnp.stack([one, two]), zh)
+    parts = lax.all_gather(early, ("y", "x"), axis=0, tiled=True).reshape(16, 2, PAD, D)
+    grad_down = unpack(parts[:, 0], D)
+    grad_up = unpack(parts[:, 1], QUART)
+    attn_part = after(attn_part, parts)
     one, two = ring_gather(attn_part[:40], "x"), ring_gather(attn_part[40:], "y")
     one, two = ring_gather(one, "y"), ring_gather(two, "x")
     attn = jnp.concatenate([one, two.transpose(1, 0, 2, 3)], axis=2).reshape(16, PAD, D)
+    attn = after(after(attn, grad_up), grad_down)
     grad_qkv = unpack(attn[:12], QUART)
     grad_out = unpack(attn[12:], QUART)
-    vectors = attn[:, SLICE, :VECTOR].reshape(-1).astype(F32)
-
-    early = depth_sum(mlp_part.transpose(1, 0, 2, 3).reshape(2, 2 * PAD, D), zh)
-    parts = lax.all_gather(early, ("y", "x"), axis=0, tiled=True).reshape(16, 2, PAD, D)
-    grad_down = unpack(parts[:, 0], D)
-    grad_up = unpack(parts[:, 1], QUART)
+    vectors = attn[:12, SLICE, :VECTOR].reshape(-1).astype(F32)
 
     def owned(start, size):
         return vectors[start : start + size]

time: 495 us -> 499 us (level)
  waiting for transfers between devices: 117 us -> 136 us
  other arithmetic: 50.5 us -> 38.3 us
  matrix products: 69.7 us -> 61 us
    ppermute x62 -> x64, waiting for transfers between devices: 117 us -> 133 us  [permute(): return rows_major(lax.ppermute(rows_major(x), axis, pairs)).reshape(shape)]
    dot_general x1, matrix products: 14.6 us -> 3.16 us  [body(): upper = jnp.dot(normed_two, full_up, preferred_element_type=F32) + up_bias]
    slice x10 -> x3, local copies, waits for them, and re-layouts: 12 us -> 2.44 us  [the longest x1 2.43 us: body(): d_keys, d_values = (d_both[0], d_both[1])]
    concatenate x10 -> x2, other arithmetic: 10.3 us -> 2.28 us  [the longest x1 1.39 us: body(): beside = swap_core(jnp.concatenate([w_qkv, small]))]
    concatenate x3 -> x1, local copies, waits for them, and re-layouts: 8.43 us -> 1.63 us  [gather_quarters(): return (by_x, jnp.concatenate([got, by_x, by_y, last_x, last_y]))]
    concatenate x11, local copies, waits for them, and re-layouts: 0.27 us -> 6.64 us  [body(): jnp.concatenate([attn_gain, attn_shift, bias_query, bias_value, bias_out,...]
    dot_general x1, matrix products: 15.2 us -> 8.99 us  [body(): d_activated = jnp.dot(upstream, full_down.T, preferred_element_type=F32)]
    squeeze x5 -> x9, local copies, waits for them, and re-layouts: 5.03 us -> 10.8 us  [after(): done = done.reshape((-1,) + done.shape[-2:])[0, :16, :128]]
  transfers between devices with their start and end apart: 66 -> 68, of which waited for: 31 -> 33; matrix products, arithmetic and copies ran while one was open for 34% -> 31% of each run, Pallas kernels for 13% -> 14%
where the time goes in v2:
time: 499 us; the launch traced here: 490 us
  waiting for transfers between devices  136 us (27%)
  local copies, waits for them, and re-layouts  94.8 us (19%)
  Pallas kernels  80 us (16%)
  starting transfers between devices  64.7 us (13%)
  matrix products  61 us (12%)
  other arithmetic  38.3 us (8%)
  between operations  15.3 us (3%)
    ppermute x64, waiting for transfers between devices, permute(): return rows_major(lax.ppermute(rows_major(x), axis, pairs)).reshape(shape)  133 us
    ppermute x64, starting transfers between devices, permute(): return rows_major(lax.ppermute(rows_major(x), axis, pairs)).reshape(shape)  64.4 us
    unnamed x178, local copies, waits for them, and re-layouts  34.4 us
    pallas_call x1, Pallas kernels, attend_backward(): pl.pallas_call(attend_backward_kernel, grid=((HEADS + 1) // 2,), out_shap...  21.5 us
    pallas_call x4, Pallas kernels, weight_grad(): pl.pallas_call(functools.partial(weight_grad_kernel, len(rights) // 2, fi...  19.3 us
    pallas_call x4, Pallas kernels, assemble(): pl.pallas_call(functools.partial(assemble_kernel, spots), out_shape=jax.S...  15.4 us
    pallas_call x1, Pallas kernels, attend_forward(): pl.pallas_call(attend_forward_kernel, grid=((HEADS + 1) // 2,), out_shape...  14.9 us
    dot_general x3, matrix products, body(): lax.dot_general(part, full_qkv[:, at * D:(at + 1) * D], (((1,), (1,)), ((...  11.4 us
  transfers between devices with their start and end apart: 68, of which 33 were waited for; matrix products, arithmetic and copies ran while one was open for 31% of the time, Pallas kernels for 14%

profile of v2, /device:TPU:0, one launch (start us, length us, event | category | flops | bytes accessed | tf_op | source)
XLA Modules:
  0.0 489.9 jit_solution(3309020632078501226)
XLA Ops:
  9.2 6.5 %concatenate.58 = bf16[3264]{0:T(1024)(128)(2,1)S(1)} concatenate(bf16[272]{0:T(512)(128)(2,1)} %param.18, bf16[272]{0:T(512)(128)(2,1)} %param.19, bf16[272]{0:T(512)(128)(2,1)} %param.21, bf16[272]{0:T(512)(128)(2,1)} %param.22, bf16[272]{0:T(512)(128)(2,1)} %param.24, bf16[272]{0:T(512)(128)(2,1)} %param.25, bf16[272]{0:T(512)(128)(2,1)} %param.26, bf16[1088]{0:T(1024)(128)(2,1)} %param.28, ...), dimensions={0} | concatenate | bytes 13056 | tf_op jit(solution)/shard_map/concatenate | solution.py:396
  17.7 4.1 collective-permute-start
  27.9 8.6 %collective-permute-done = bf16[96,3264]{1,0:T(8,128)(2,1)} collective-permute-done((bf16[96,3264]{1,0:T(8,128)(2,1)}, bf16[96,3264]{1,0:T(8,128)(2,1)}, u32[]{:S(2)}, u32[]{:S(2)}) %collective-permute-start) | collective-permute-done | bytes 626720 | tf_op jit(solution)/shard_map/ppermute | solution.py:44
  44.3 5.5 %collective-permute-done.1 = bf16[64,3264]{1,0:T(8,128)(2,1)} collective-permute-done((bf16[64,3264]{1,0:T(8,128)(2,1)}, bf16[64,3264]{1,0:T(8,128)(2,1)}, u32[]{:S(2)}, u32[]{:S(2)}) %collective-permute-start.1) | collective-permute-done | bytes 417824 | tf_op jit(solution)/shard_map/ppermute | solution.py:44
  51.1 2.6 collective-permute-start.11
  55.2 4.5 collective-permute-done.11
  63.0 2.0 constant_dynamic-update-slice_fusion.4
  67.1 6.1 %collective-permute-done.2 = bf16[64,3264]{1,0:T(8,128)(2,1)S(1)} collective-permute-done((bf16[64,3264]{1,0:T(8,128)(2,1)}, bf16[64,3264]{1,0:T(8,128)(2,1)S(1)}, u32[]{:S(2)}, u32[]{:S(2)}) %collective-permute-start.2) | collective-permute-done | bytes 417824 | tf_op jit(solution)/shard_map/ppermute | solution.py:44
  78.0 2.8 collective-permute-done.3
  85.4 7.3 %collective-permute-done.8 = bf16[4,64,1088]{2,1,0:T(8,128)(2,1)} collective-permute-done((bf16[4,64,1088]{2,1,0:T(8,128)(2,1)}, bf16[4,64,1088]{2,1,0:T(8,128)(2,1)}, u32[]{:S(2)}, u32[]{:S(2)}) %collective-permute-start.8) | collective-permute-done | bytes 557088 | tf_op jit(solution)/shard_map/ppermute | solution.py:44
  97.1 3.8 collective-permute-done.12
  112.1 5.8 %shard_map.271 = bf16[1088,3264]{1,0:T(8,128)(2,1)S(1)} custom-call(bf16[272,3264]{1,0:T(8,128)(2,1)S(1)} %copy-done.2, bf16[288,3264]{1,0:T(8,128)(2,1)} %collective-permute-done.6.refs_1_, bf16[288,3264]{1,0:T(8,128)(2,1)} %constant_dynamic-update-slice_fusion.refs_2_, bf16[288,3264]{1,0:T(8,128)(2,1)} %collective-permute-done.5.refs_3_), custom_call_target="tpu_custom_call" | custom-call | bytes 14204928 | tf_op jit(solution)/shard_map/pallas_call | solution.py:147
  117.8 3.0 copy-done
  121.4 4.6 collective-permute-done.13.x_ref
  126.3 2.4 fusion.45
  129.7 8.1 %add_convert_fusion.v_ref = bf16[1024,1088]{1,0:T(8,128)(2,1)} fusion(f32[1088]{0:T(1024)S(1)} %add.315, bf16[1088,3264]{1,0:T(8,128)(2,1)} %copy-done, bf16[256,1088]{1,0:T(8,128)(2,1)S(1)} %get-tuple-element.174, bf16[256,1088]{1,0:T(8,128)(2,1)S(1)} %get-tuple-element.173, bf16[256,1088]{1,0:T(8,128)(2,1)S(1)} %get-tuple-element.172, ...), kind=kOutput, calls=%fused_computation.4 | convolution fusion | flops 2435448832 | bytes 6967552 | tf_op jit(solution)/shard_map/dot_general | solution.py:469
  138.3 7.4 %convolution_convert_fusion.k_ref = bf16[1024,1088]{1,0:T(8,128)(2,1)} fusion(bf16[1088,3264]{1,0:T(8,128)(2,1)} %copy-done, bf16[256,1088]{1,0:T(8,128)(2,1)} %copy-done.48, bf16[256,1088]{1,0:T(8,128)(2,1)} %copy-done.47, bf16[256,1088]{1,0:T(8,128)(2,1)S(1)} %get-tuple-element.172, bf16[256,1088]{1,0:T(8,128)(2,1)S(1)} %get-tuple-element.175), kind=kOutput, calls=%fused_computation.8 | convolution fusion | flops 2434334720 | bytes 7028736 | tf_op jit(solution)/shard_map/dot_general | solution.py:468
  146.2 2.9 fusion.6.q_ref
  150.9 14.9 %shard_map.273 = (bf16[256,1088]{1,0:T(8,128)(2,1)S(1)}, f32[256,1088]{1,0:T(8,128)S(1)}) custom-call(bf16[256,1088]{1,0:T(8,128)(2,1)S(1)} %fusion.6.q_ref, bf16[1024,1088]{1,0:T(8,128)(2,1)S(1)} %copy-done.22, bf16[1024,1088]{1,0:T(8,128)(2,1)S(1)} %copy-done.20, f32[256,1024]{1,0:T(8,128)S(1)} %copy-done.16), custom_call_target="tpu_custom_call" | custom-call | flops 1140850688 | bytes 6684672 | tf_op jit(solution)/shard_map/pallas_call | solution.py:220
  169.6 2.0 shard_map.278
  172.3 2.6 fusion.71
  177.1 4.5 shard_map.279
  181.6 3.2 multiply_convert_fusion
  187.6 3.2 shard_map.280
  190.9 9.0 %convert_reduce_fusion = (f32[4352]{0:T(1024)}, bf16[256,4352]{1,0:T(8,128)(2,1)}) fusion(f32[256,4352]{1,0:T(8,128)S(1)} %get-tuple-element.183, bf16[4352,1088]{1,0:T(8,128)(2,1)S(1)} %shard_map.280, bf16[1,256,1088]{1,2,0:T(8,128)(2,1)S(1)} %copy-done.49), kind=kOutput, calls=%fused_computation.5 | convolution fusion | flops 2437672704 | bytes 16729088 | tf_op jit(solution)/shard_map/dot_general | solution.py:508
  206.9 4.9 %shard_map.281.refs_5_ = bf16[16,2,2,72,1088]{4,3,2,1,0:T(8,128)(2,1)} custom-call(bf16[2,256,1088]{2,1,0:T(8,128)(2,1)S(1)} %get-tuple-element.110.refs_0_, bf16[2,256,1088]{2,1,0:T(8,128)(2,1)S(1)} %bitcast.292, bf16[256,1088]{1,0:T(8,128)(2,1)S(1)} %bitcast.286, bf16[256,1088]{1,0:T(8,128)(2,1)S(1)} %bitcast.295, f32[2,12,1088]{2,1,0:T(8,128)S(1)} %broadcast_in_dim.56.refs_4_), custom_call_target="tpu_custom_call" | custom-call | flops 2424307712 | bytes 8408064 | tf_op jit(solution)/shard_map/pallas_call | solution.py:299
  211.9 7.2 %shard_map.282 = bf16[16,2,2,72,1088]{4,3,2,1,0:T(8,128)(2,1)} custom-call(bf16[2,256,272]{2,1,0:T(8,128)(2,1)S(1)} %get-tuple-element.130.refs_0_, bf16[2,256,272]{2,1,0:T(8,128)(2,1)S(1)} %bitcast.297, bf16[256,4352]{1,0:T(8,128)(2,1)} %get-tuple-element.188.refs_2_, ...), custom_call_target="tpu_custom_call", output_to_operand_aliasing={{}: (5, {})} | custom-call | flops 2424307712 | bytes 10079232 | tf_op jit(solution)/shard_map/pallas_call | solution.py:299
  219.3 8.6 %fusion.72 = (f32[1088]{0:T(1024)}, f32[256,1088]{0,1:T(8,128)}) fusion(bf16[256,4352]{1,0:T(8,128)(2,1)} %get-tuple-element.188.refs_2_, bf16[1088,4352]{1,0:T(8,128)(2,1)} %copy-done.3), kind=kOutput, calls=%fused_computation.262 | convolution fusion | flops 2424585216 | bytes 12816640 | tf_op jit(solution)/shard_map/dot_general | solution.py:521
  227.9 2.0 copy.91
  242.1 21.5 %shard_map.284 = (bf16[256,1088]{1,0:T(8,128)(2,1)S(1)}, bf16[2,2,256,1088]{3,2,1,0:T(8,128)(2,1)S(1)}, bf16[2,2,256,1088]{3,2,1,0:T(8,128)(2,1)S(1)}) custom-call(bf16[256,1088]{1,0:T(8,128)(2,1)S(1)} %copy-done.27, bf16[1024,1088]{1,0:T(8,128)(2,1)S(1)} %copy-done.23, bf16[1024,1088]{1,0:T(8,128)(2,1)S(1)} %copy-done.21, f32[256,1024]{1,0:T(8,128)S(1)} %copy-done.17, ...), custom_call_target="tpu_custom_call" | custom-call | flops 2852126720 | bytes 13369344 | tf_op jit(solution)/shard_map/pallas_call | solution.py:247
  264.1 4.1 collective-permute-done.25
  276.3 2.0 shard_map.286.refs_9_
  280.8 19.2 %collective-permute-done.26 = bf16[8,64,1088]{2,1,0:T(8,128)(2,1)} collective-permute-done((bf16[8,64,1088]{2,1,0:T(8,128)(2,1)}, bf16[8,64,1088]{2,1,0:T(8,128)(2,1)}, u32[]{:S(2)}, u32[]{:S(2)}) %collective-permute-start.26) | collective-permute-done | bytes 1114144 | tf_op jit(solution)/shard_map/ppermute | solution.py:44
  302.7 4.1 fusion.12
  306.8 3.0 reduce-scatter.2.cloned.1.call-done
  311.0 3.0 collective-permute-start.29
  315.2 3.8 fusion.9
  318.9 10.1 %collective-permute-done.28 = bf16[144,1088]{1,0:T(8,128)(2,1)S(1)} collective-permute-done((bf16[144,1088]{1,0:T(8,128)(2,1)S(1)}, bf16[144,1088]{1,0:T(8,128)(2,1)S(1)}, u32[]{:S(2)}, u32[]{:S(2)}) %collective-permute-start.28) | collective-permute-done | bytes 313376 | tf_op jit(solution)/shard_map/ppermute | solution.py:44
  330.3 3.6 fusion.63
  335.7 2.4 fusion.68
  341.4 5.3 %shard_map.287 = bf16[16,1,2,72,1088]{4,3,2,1,0:T(8,128)(2,1)} custom-call(bf16[2,256,272]{2,1,0:T(8,128)(2,1)S(1)} %copy-done.13, bf16[2,256,272]{2,1,0:T(8,128)(2,1)} %shard_map.285.refs_1_, bf16[256,1088]{1,0:T(8,128)(2,1)S(1)} %get-tuple-element.22.refs_2_, bf16[256,1088]{1,0:T(8,128)(2,1)} %bitcast.65.refs_3_, ...), custom_call_target="tpu_custom_call", output_to_operand_aliasing={{}: (9, {})} | custom-call | flops 1818230784 | bytes 7711744 | tf_op jit(solution)/shard_map/pallas_call | solution.py:299
  348.3 2.0 collective-permute-start.37
  352.4 3.1 dynamic-slice_bitcast_fusion.2
  358.6 9.2 %collective-permute-done.37 = bf16[4,72,1088]{2,1,0:T(8,128)(2,1)} collective-permute-done((bf16[4,72,1088]{2,1,0:T(8,128)(2,1)S(1)}, bf16[4,72,1088]{2,1,0:T(8,128)(2,1)}, u32[]{:S(2)}, u32[]{:S(2)}) %collective-permute-start.37) | collective-permute-done | bytes 626720 | tf_op jit(solution)/shard_map/ppermute | solution.py:44
  368.9 6.9 %fusion.5 = f32[1,256,1088]{2,1,0:T(8,128)S(1)} fusion(f32[256,1088]{1,0:T(8,128)S(1)} %copy-done.33, bf16[256,4352]{1,0:T(8,128)(2,1)S(1)} %copy-done.45, bf16[4352,1088]{1,0:T(8,128)(2,1)} %copy-done.1, f32[1088]{0:T(1024)S(1)} %add.341), kind=kOutput, calls=%fused_computation.16 | convolution fusion | flops 2424864768 | bytes 13930752 | tf_op jit(solution)/shard_map/dot_general | solution.py:490
  377.2 8.9 %collective-permute-done.39 = bf16[4,72,1088]{2,1,0:T(8,128)(2,1)} collective-permute-done((bf16[4,72,1088]{2,1,0:T(8,128)(2,1)S(1)}, bf16[4,72,1088]{2,1,0:T(8,128)(2,1)}, u32[]{:S(2)}, u32[]{:S(2)}) %collective-permute-start.39) | collective-permute-done | bytes 626720 | tf_op jit(solution)/shard_map/ppermute | solution.py:44
  386.0 12.9 %collective-permute-done.45 = bf16[4,72,1088]{2,1,0:T(8,128)(2,1)} collective-permute-done((bf16[4,72,1088]{2,1,0:T(8,128)(2,1)}, bf16[4,72,1088]{2,1,0:T(8,128)(2,1)}, u32[]{:S(2)}, u32[]{:S(2)}) %collective-permute-start.45) | collective-permute-done | bytes 626720 | tf_op jit(solution)/shard_map/ppermute | solution.py:44
  399.3 3.2 fusion.25
  403.1 2.2 collective-permute-start.48
  405.7 2.0 collective-permute-start.40
  407.7 2.6 collective-permute-start.42
  415.6 2.2 collective-permute-done.41
  418.1 3.1 collective-permute-start.50
  425.9 2.2 collective-permute-done.51
  431.9 2.0 collective-permute-start.58
  434.8 4.1 collective-permute-start.53
  439.7 3.0 slice_bitcast_fusion
  442.6 2.6 shard_map.291
  446.6 2.8 shard_map.289
  452.3 2.5 collective-permute-start.61
  455.1 3.9 collective-permute-done.54
  468.3 2.5 collective-permute-done.55
  472.5 2.2 pad_maximum_fusion
  481.0 2.2 shard_map.293
  (445 shorter events, 154.4 us)
Async XLA Ops:
  7.2 130.6 %all-gather.5.cloned.1.call-start = ((), (), s32[]{:S(2)}) async-start(), calls=%async_computation.1 | async-start | bytes 2367488 | tf_op jit(solution)/shard_map/all_gather | solution.py:358
  8.6 34.5 %collective-permute-start.7 = (bf16[4,64,1088]{2,1,0:T(8,128)(2,1)S(1)}, bf16[4,64,1088]{2,1,0:T(8,128)(2,1)}, u32[]{:S(2)}, u32[]{:S(2)}) collective-permute-start(bf16[4,64,1088]{2,1,0:T(8,128)(2,1)S(1)} %bitcast.305), channel_id=1, source_target_pairs={{0,1},{1,0},{2,3},{3,2},{4,5},{5,4},{6,7},{7,6},{8,9},{9,8},{10,11... | collective-permute-start | bytes 1671176 | tf_op jit(solution)/shard_map/ppermute | solution.py:44
  8.7 159.0 %collective-permute-start.10 = (bf16[272,1088]{1,0:T(8,128)(2,1)}, bf16[272,1088]{1,0:T(8,128)(2,1)}, u32[]{:S(2)}, u32[]{:S(2)}) collective-permute-start(bf16[272,1088]{1,0:T(8,128)(2,1)} %refs_0_.5), channel_id=1, source_target_pairs={{0,1},{1,0},{2,3},{3,2},{4,5},{5,4},{6,7},{7,6},{8,9},{9,8},{10,11... | collective-permute-start | bytes 1775624 | tf_op jit(solution)/shard_map/ppermute | solution.py:44
  17.7 18.9 %collective-permute-start = (bf16[96,3264]{1,0:T(8,128)(2,1)}, bf16[96,3264]{1,0:T(8,128)(2,1)}, u32[]{:S(2)}, u32[]{:S(2)}) collective-permute-start(bf16[96,3264]{1,0:T(8,128)(2,1)} %pad_maximum_fusion.5), channel_id=1, source_target_pairs={{0,6},{6,0},{2,4},{4,2},{1,7},{7,1},{3,5},{5,3},{8,14},{14,8},{10,... | collective-permute-start | bytes 1880072 | tf_op jit(solution)/shard_map/ppermute | solution.py:44
  23.2 85.3 %collective-permute-start.6 = (bf16[288,3264]{1,0:T(8,128)(2,1)}, bf16[288,3264]{1,0:T(8,128)(2,1)}, u32[]{:S(2)}, u32[]{:S(2)}) collective-permute-start(bf16[288,3264]{1,0:T(8,128)(2,1)} %pad_maximum_fusion.2), channel_id=1, source_target_pairs={{0,1},{1,0},{2,3},{3,2},{4,5},{5,4},{6,7},{7,6},{8,9},{9,8},{10,11... | collective-permute-start | bytes 5640200 | tf_op jit(solution)/shard_map/ppermute | solution.py:44
  23.2 153.7 %collective-permute-start.15 = (bf16[272,4352]{1,0:T(8,128)(2,1)}, bf16[272,4352]{1,0:T(8,128)(2,1)}, u32[]{:S(2)}, u32[]{:S(2)}) collective-permute-start(bf16[272,4352]{1,0:T(8,128)(2,1)} %refs_0_.6), channel_id=1, source_target_pairs={{0,1},{1,0},{2,3},{3,2},{4,5},{5,4},{6,7},{7,6},{8,9},{9,8},{10,11... | collective-permute-start | bytes 7102472 | tf_op jit(solution)/shard_map/ppermute | solution.py:44
  38.4 11.4 %collective-permute-start.1 = (bf16[64,3264]{1,0:T(8,128)(2,1)}, bf16[64,3264]{1,0:T(8,128)(2,1)}, u32[]{:S(2)}, u32[]{:S(2)}) collective-permute-start(bf16[64,3264]{1,0:T(8,128)(2,1)} %slice.359), channel_id=1, source_target_pairs={{0,8},{8,0},{16,24},{24,16},{1,9},{9,1},{17,25},{25,17},{2,10},{10... | collective-permute-start | bytes 1253384 | tf_op jit(solution)/shard_map/ppermute | solution.py:44
  51.1 8.6 %collective-permute-start.11 = (bf16[32,4352]{1,0:T(8,128)(2,1)}, bf16[32,4352]{1,0:T(8,128)(2,1)}, u32[]{:S(2)}, u32[]{:S(2)}) collective-permute-start(bf16[32,4352]{1,0:T(8,128)(2,1)} %shard_map.274), channel_id=1, source_target_pairs={{0,6},{6,0},{2,4},{4,2},{1,7},{7,1},{3,5},{5,3},{8,14},{14,8},{10,... | collective-permute-start | bytes 835592 | tf_op jit(solution)/shard_map/ppermute | solution.py:44
  61.3 110.4 %all-gather.9.cloned.1.call-start = ((), (), s32[]{:S(2)}) async-start(), calls=%async_computation.4 | async-start | bytes 2506752 | tf_op jit(solution)/shard_map/all_gather | solution.py:358
  61.5 11.8 %collective-permute-start.2 = (bf16[64,3264]{1,0:T(8,128)(2,1)}, bf16[64,3264]{1,0:T(8,128)(2,1)S(1)}, u32[]{:S(2)}, u32[]{:S(2)}) collective-permute-start(bf16[64,3264]{1,0:T(8,128)(2,1)} %slice.359), channel_id=1, source_target_pairs={{0,32},{32,0},{64,96},{96,64},{1,33},{33,1},{65,97},{97,65},{2,34}... | collective-permute-start | bytes 1253384 | tf_op jit(solution)/shard_map/ppermute | solution.py:44
  66.7 15.8 %collective-permute-start.4 = (bf16[32,3264]{1,0:T(8,128)(2,1)}, bf16[32,3264]{1,0:T(8,128)(2,1)}, u32[]{:S(2)}, u32[]{:S(2)}) collective-permute-start(bf16[32,3264]{1,0:T(8,128)(2,1)} %slice.361), channel_id=1, source_target_pairs={{0,32},{32,0},{64,96},{96,64},{1,33},{33,1},{65,97},{97,65},{2,34}... | collective-permute-start | bytes 626696 | tf_op jit(solution)/shard_map/ppermute | solution.py:44
  73.9 6.9 %collective-permute-start.3 = (bf16[32,3264]{1,0:T(8,128)(2,1)}, bf16[32,3264]{1,0:T(8,128)(2,1)}, u32[]{:S(2)}, u32[]{:S(2)}) collective-permute-start(bf16[32,3264]{1,0:T(8,128)(2,1)} %slice.360), channel_id=1, source_target_pairs={{0,8},{8,0},{16,24},{24,16},{1,9},{9,1},{17,25},{25,17},{2,10},{10... | collective-permute-start | bytes 626696 | tf_op jit(solution)/shard_map/ppermute | solution.py:44
  80.8 11.8 %collective-permute-start.8 = (bf16[4,64,1088]{2,1,0:T(8,128)(2,1)}, bf16[4,64,1088]{2,1,0:T(8,128)(2,1)}, u32[]{:S(2)}, u32[]{:S(2)}) collective-permute-start(bf16[4,64,1088]{2,1,0:T(8,128)(2,1)} %bitcast.313), channel_id=1, source_target_pairs={{0,2},{2,0},{1,3},{3,1},{4,6},{6,4},{5,7},{7,5},{8,10},{10,8},{9,1... | collective-permute-start | bytes 1671176 | tf_op jit(solution)/shard_map/ppermute | solution.py:44
  84.1 26.0 %collective-permute-start.5 = (bf16[288,3264]{1,0:T(8,128)(2,1)}, bf16[288,3264]{1,0:T(8,128)(2,1)}, u32[]{:S(2)}, u32[]{:S(2)}) collective-permute-start(bf16[288,3264]{1,0:T(8,128)(2,1)} %constant_dynamic-update-slice_fusion.refs_2_), channel_id=1, source_target_pairs={{0,1},{1,0},{2,3},{3,2},{4,5},{5,4},{6,7},{7,6},{8,9},{9,8},{10,11... | collective-permute-start | bytes 5640200 | tf_op jit(solution)/shard_map/ppermute | solution.py:44
  92.6 8.2 %collective-permute-start.12 = (bf16[2,64,1088]{2,1,0:T(8,128)(2,1)}, bf16[2,64,1088]{2,1,0:T(8,128)(2,1)}, u32[]{:S(2)}, u32[]{:S(2)}) collective-permute-start(bf16[2,64,1088]{2,1,0:T(8,128)(2,1)} %bitcast.316), channel_id=1, source_target_pairs={{0,6},{6,0},{2,4},{4,2},{1,7},{7,1},{3,5},{5,3},{8,14},{14,8},{10,... | collective-permute-start | bytes 835592 | tf_op jit(solution)/shard_map/ppermute | solution.py:44
  103.9 206.0 %reduce-scatter.2.cloned.1.call-start = ((), (), s32[]{:S(2)}) async-start(), calls=%async_computation.2 | async-start | bytes 11280384 | tf_op jit(solution)/shard_map/reduce_scatter | solution.py:517
  103.9 82.5 %collective-permute-start.18 = (bf16[1088,1088]{1,0:T(8,128)(2,1)}, bf16[1088,1088]{1,0:T(8,128)(2,1)}, u32[]{:S(2)}, u32[]{:S(2)}) collective-permute-start(bf16[1088,1088]{1,0:T(8,128)(2,1)} %refs_0_.7), channel_id=1, source_target_pairs={{0,1},{1,0},{2,3},{3,2},{4,5},{5,4},{6,7},{7,6},{8,9},{9,8},{10,11... | collective-permute-start | bytes 7102472 | tf_op jit(solution)/shard_map/ppermute | solution.py:44
  108.4 17.6 %collective-permute-start.13 = (bf16[272,1088]{1,0:T(8,128)(2,1)}, bf16[272,1088]{1,0:T(8,128)(2,1)}, u32[]{:S(2)}, u32[]{:S(2)}) collective-permute-start(bf16[272,1088]{1,0:T(8,128)(2,1)} %shard_map.276), channel_id=1, source_target_pairs={{0,6},{6,0},{2,4},{4,2},{1,7},{7,1},{3,5},{5,3},{8,14},{14,8},{10,... | collective-permute-start | bytes 1775624 | tf_op jit(solution)/shard_map/ppermute | solution.py:44
  126.0 41.7 %collective-permute-start.14 = (bf16[272,1088]{1,0:T(8,128)(2,1)}, bf16[272,1088]{1,0:T(8,128)(2,1)S(1)}, u32[]{:S(2)}, u32[]{:S(2)}) collective-permute-start(bf16[272,1088]{1,0:T(8,128)(2,1)} %shard_map.277.refs_2_), channel_id=1, source_target_pairs={{0,1},{1,0},{2,3},{3,2},{4,5},{5,4},{6,7},{7,6},{8,9},{9,8},{10,11... | collective-permute-start | bytes 1775624 | tf_op jit(solution)/shard_map/ppermute | solution.py:44
  137.8 39.1 %collective-permute-start.16 = (bf16[256,4352]{1,0:T(8,128)(2,1)}, bf16[256,4352]{1,0:T(8,128)(2,1)}, u32[]{:S(2)}, u32[]{:S(2)}) collective-permute-start(bf16[256,4352]{1,0:T(8,128)(2,1)} %all-gather.5.cloned.1.call-done.refs_2_), channel_id=1, source_target_pairs={{0,1},{1,0},{2,3},{3,2},{4,5},{5,4},{6,7},{7,6},{8,9},{9,8},{10,11... | collective-permute-start | bytes 6684680 | tf_op jit(solution)/shard_map/ppermute | solution.py:44
  167.7 8.1 %collective-permute-start.17 = (bf16[16,4352]{1,0:T(8,128)(2,1)S(1)}, bf16[16,4352]{1,0:T(8,128)(2,1)}, u32[]{:S(2)}, u32[]{:S(2)}) collective-permute-start(bf16[16,4352]{1,0:T(8,128)(2,1)S(1)} %get-tuple-element.162.refs_3_), channel_id=1, source_target_pairs={{0,1},{1,0},{2,3},{3,2},{4,5},{5,4},{6,7},{7,6},{8,9},{9,8},{10,11... | collective-permute-start | bytes 417800 | tf_op jit(solution)/shard_map/ppermute | solution.py:44
  171.7 14.7 %collective-permute-start.19 = (bf16[16,64,1088]{2,1,0:T(8,128)(2,1)}, bf16[16,64,1088]{2,1,0:T(8,128)(2,1)S(1)}, u32[]{:S(2)}, u32[]{:S(2)}) collective-permute-start(bf16[16,64,1088]{2,1,0:T(8,128)(2,1)} %bitcast.288), channel_id=1, source_target_pairs={{0,1},{1,0},{2,3},{3,2},{4,5},{5,4},{6,7},{7,6},{8,9},{9,8},{10,11... | collective-permute-start | bytes 6684680 | tf_op jit(solution)/shard_map/ppermute | solution.py:44
  175.9 10.6 %collective-permute-start.20 = (bf16[64,1088]{1,0:T(8,128)(2,1)S(1)}, bf16[64,1088]{1,0:T(8,128)(2,1)S(1)}, u32[]{:S(2)}, u32[]{:S(2)}) collective-permute-start(bf16[64,1088]{1,0:T(8,128)(2,1)S(1)} %get-tuple-element.160.refs_3_), channel_id=1, source_target_pairs={{0,1},{1,0},{2,3},{3,2},{4,5},{5,4},{6,7},{7,6},{8,9},{9,8},{10,11... | collective-permute-start | bytes 417800 | tf_op jit(solution)/shard_map/ppermute | solution.py:44
  199.9 12.0 %collective-permute-start.22 = (bf16[256,4352]{1,0:T(8,128)(2,1)}, bf16[256,4352]{1,0:T(8,128)(2,1)}, u32[]{:S(2)}, u32[]{:S(2)}) collective-permute-start(bf16[256,4352]{1,0:T(8,128)(2,1)} %get-tuple-element.188.refs_2_), channel_id=1, source_target_pairs={{0,1},{1,0},{2,3},{3,2},{4,5},{5,4},{6,7},{7,6},{8,9},{9,8},{10,11... | collective-permute-start | bytes 6684680 | tf_op jit(solution)/shard_map/ppermute | solution.py:44
  202.6 4.3 collective-permute-start.23
  206.2 5.6 %collective-permute-start.21 = (bf16[8,64,272]{2,1,0:T(8,128)(2,1)S(1)}, bf16[8,64,272]{2,1,0:T(8,128)(2,1)S(1)}, u32[]{:S(2)}, u32[]{:S(2)}) collective-permute-start(bf16[8,64,272]{2,1,0:T(8,128)(2,1)S(1)} %bitcast.318), channel_id=1, source_target_pairs={{0,1},{1,0},{2,3},{3,2},{4,5},{5,4},{6,7},{7,6},{8,9},{9,8},{10,11... | collective-permute-start | bytes 835592 | tf_op jit(solution)/shard_map/ppermute | solution.py:44
  219.1 209.7 %all-gather.7.cloned.1.call-start = ((), (), s32[]{:S(2)}) async-start(), calls=%async_computation.3 | async-start | bytes 5640192 | tf_op jit(solution)/shard_map/all_gather | solution.py:603
  263.6 4.6 collective-permute-start.25
  270.0 30.0 %collective-permute-start.26 = (bf16[8,64,1088]{2,1,0:T(8,128)(2,1)}, bf16[8,64,1088]{2,1,0:T(8,128)(2,1)}, u32[]{:S(2)}, u32[]{:S(2)}) collective-permute-start(bf16[8,64,1088]{2,1,0:T(8,128)(2,1)} %fusion.8), channel_id=1, source_target_pairs={{0,2},{2,0},{1,3},{3,1},{4,6},{6,4},{5,7},{7,5},{8,10},{10,8},{9,1... | collective-permute-start | bytes 3342344 | tf_op jit(solution)/shard_map/ppermute | solution.py:44
  270.0 6.3 %collective-permute-start.36 = (bf16[4,64,1088]{2,1,0:T(8,128)(2,1)S(1)}, bf16[4,64,1088]{2,1,0:T(8,128)(2,1)S(1)}, u32[]{:S(2)}, u32[]{:S(2)}) collective-permute-start(bf16[4,64,1088]{2,1,0:T(8,128)(2,1)S(1)} %bitcast.291), channel_id=1, source_target_pairs={{0,1},{1,0},{2,3},{3,2},{4,5},{5,4},{6,7},{7,6},{8,9},{9,8},{10,11... | collective-permute-start | bytes 1671176 | tf_op jit(solution)/shard_map/ppermute | solution.py:44
  271.5 4.7 collective-permute-start.35
  273.2 66.9 %collective-permute-start.27 = (bf16[8,64,272]{2,1,0:T(8,128)(2,1)}, bf16[8,64,272]{2,1,0:T(8,128)(2,1)}, u32[]{:S(2)}, u32[]{:S(2)}) collective-permute-start(bf16[8,64,272]{2,1,0:T(8,128)(2,1)} %bitcast.54), channel_id=1, source_target_pairs={{0,1},{1,0},{2,3},{3,2},{4,5},{5,4},{6,7},{7,6},{8,9},{9,8},{10,11... | collective-permute-start | bytes 835592 | tf_op jit(solution)/shard_map/ppermute | solution.py:44
  279.0 61.0 %collective-permute-start.31 = (bf16[4,64,1088]{2,1,0:T(8,128)(2,1)S(1)}, bf16[4,64,1088]{2,1,0:T(8,128)(2,1)}, u32[]{:S(2)}, u32[]{:S(2)}) collective-permute-start(bf16[4,64,1088]{2,1,0:T(8,128)(2,1)S(1)} %bitcast.287), channel_id=1, source_target_pairs={{0,1},{1,0},{2,3},{3,2},{4,5},{5,4},{6,7},{7,6},{8,9},{9,8},{10,11... | collective-permute-start | bytes 1671176 | tf_op jit(solution)/shard_map/ppermute | solution.py:44
  311.0 18.1 %collective-permute-start.29 = (bf16[144,1088]{1,0:T(8,128)(2,1)S(1)}, bf16[144,1088]{1,0:T(8,128)(2,1)S(1)}, u32[]{:S(2)}, u32[]{:S(2)}) collective-permute-start(bf16[144,1088]{1,0:T(8,128)(2,1)S(1)} %bitcast.319), channel_id=1, source_target_pairs={{0,6},{6,0},{2,4},{4,2},{1,7},{7,1},{3,5},{5,3},{8,14},{14,8},{10,... | collective-permute-start | bytes 940040 | tf_op jit(solution)/shard_map/ppermute | solution.py:44
  314.0 15.1 %collective-permute-start.30 = (bf16[144,1088]{1,0:T(8,128)(2,1)S(1)}, bf16[144,1088]{1,0:T(8,128)(2,1)S(1)}, u32[]{:S(2)}, u32[]{:S(2)}) collective-permute-start(bf16[144,1088]{1,0:T(8,128)(2,1)S(1)} %bitcast.320), channel_id=1, source_target_pairs={{0,2},{2,0},{1,3},{3,1},{4,6},{6,4},{5,7},{7,5},{8,10},{10,8},{9,1... | collective-permute-start | bytes 940040 | tf_op jit(solution)/shard_map/ppermute | solution.py:44
  314.8 14.2 %collective-permute-start.28 = (bf16[144,1088]{1,0:T(8,128)(2,1)S(1)}, bf16[144,1088]{1,0:T(8,128)(2,1)S(1)}, u32[]{:S(2)}, u32[]{:S(2)}) collective-permute-start(bf16[144,1088]{1,0:T(8,128)(2,1)S(1)} %bitcast.315), channel_id=1, source_target_pairs={{0,4},{4,0},{1,5},{5,1},{2,6},{6,2},{3,7},{7,3},{8,12},{12,8},{9,1... | collective-permute-start | bytes 940040 | tf_op jit(solution)/shard_map/ppermute | solution.py:44
  335.6 3.0 collective-permute-start.34
  348.3 19.5 %collective-permute-start.37 = (bf16[4,72,1088]{2,1,0:T(8,128)(2,1)S(1)}, bf16[4,72,1088]{2,1,0:T(8,128)(2,1)}, u32[]{:S(2)}, u32[]{:S(2)}) collective-permute-start(bf16[4,72,1088]{2,1,0:T(8,128)(2,1)S(1)} %get-tuple-element.98), channel_id=1, source_target_pairs={{0,16},{8,24},{16,0},{24,8},{1,17},{9,25},{17,1},{25,9},{2,18},{10... | collective-permute-start | bytes 1880072 | tf_op jit(solution)/shard_map/ppermute | solution.py:44
  350.4 35.6 %collective-permute-start.39 = (bf16[4,72,1088]{2,1,0:T(8,128)(2,1)S(1)}, bf16[4,72,1088]{2,1,0:T(8,128)(2,1)}, u32[]{:S(2)}, u32[]{:S(2)}) collective-permute-start(bf16[4,72,1088]{2,1,0:T(8,128)(2,1)S(1)} %get-tuple-element.99), channel_id=1, source_target_pairs={{0,24},{8,0},{16,8},{24,16},{1,25},{9,1},{17,9},{25,17},{2,26},{10... | collective-permute-start | bytes 1880072 | tf_op jit(solution)/shard_map/ppermute | solution.py:44
  351.9 34.1 %collective-permute-start.38 = (bf16[4,72,1088]{2,1,0:T(8,128)(2,1)S(1)}, bf16[4,72,1088]{2,1,0:T(8,128)(2,1)}, u32[]{:S(2)}, u32[]{:S(2)}) collective-permute-start(bf16[4,72,1088]{2,1,0:T(8,128)(2,1)S(1)} %get-tuple-element.100), channel_id=1, source_target_pairs={{0,8},{8,16},{16,24},{24,0},{1,9},{9,17},{17,25},{25,1},{2,10},{10... | collective-permute-start | bytes 1880072 | tf_op jit(solution)/shard_map/ppermute | solution.py:44
  355.5 30.5 %collective-permute-start.43 = (bf16[4,72,1088]{2,1,0:T(8,128)(2,1)}, bf16[4,72,1088]{2,1,0:T(8,128)(2,1)}, u32[]{:S(2)}, u32[]{:S(2)}) collective-permute-start(bf16[4,72,1088]{2,1,0:T(8,128)(2,1)} %get-tuple-element.95), channel_id=1, source_target_pairs={{0,64},{32,96},{64,0},{96,32},{1,65},{33,97},{65,1},{97,33},{2,66}... | collective-permute-start | bytes 1880072 | tf_op jit(solution)/shard_map/ppermute | solution.py:44
  357.3 41.6 %collective-permute-start.45 = (bf16[4,72,1088]{2,1,0:T(8,128)(2,1)}, bf16[4,72,1088]{2,1,0:T(8,128)(2,1)}, u32[]{:S(2)}, u32[]{:S(2)}) collective-permute-start(bf16[4,72,1088]{2,1,0:T(8,128)(2,1)} %get-tuple-element.96), channel_id=1, source_target_pairs={{0,96},{32,0},{64,32},{96,64},{1,97},{33,1},{65,33},{97,65},{2,98}... | collective-permute-start | bytes 1880072 | tf_op jit(solution)/shard_map/ppermute | solution.py:44
  367.8 31.5 %collective-permute-start.44 = (bf16[4,72,1088]{2,1,0:T(8,128)(2,1)}, bf16[4,72,1088]{2,1,0:T(8,128)(2,1)}, u32[]{:S(2)}, u32[]{:S(2)}) collective-permute-start(bf16[4,72,1088]{2,1,0:T(8,128)(2,1)} %get-tuple-element.97), channel_id=1, source_target_pairs={{0,32},{32,64},{64,96},{96,0},{1,33},{33,65},{65,97},{97,1},{2,34}... | collective-permute-start | bytes 1880072 | tf_op jit(solution)/shard_map/ppermute | solution.py:44
  402.6 8.7 %collective-permute-start.46 = (bf16[72,1088]{1,0:T(8,128)(2,1)S(1)}, bf16[72,1088]{1,0:T(8,128)(2,1)S(1)}, u32[]{:S(2)}, u32[]{:S(2)}) collective-permute-start(bf16[72,1088]{1,0:T(8,128)(2,1)S(1)} %get-tuple-element.131), channel_id=1, source_target_pairs={{0,16},{8,24},{16,0},{24,8},{1,17},{9,25},{17,1},{25,9},{2,18},{10... | collective-permute-start | bytes 470024 | tf_op jit(solution)/shard_map/ppermute | solution.py:44
  403.1 10.1 %collective-permute-start.48 = (bf16[72,1088]{1,0:T(8,128)(2,1)S(1)}, bf16[72,1088]{1,0:T(8,128)(2,1)S(1)}, u32[]{:S(2)}, u32[]{:S(2)}) collective-permute-start(bf16[72,1088]{1,0:T(8,128)(2,1)S(1)} %get-tuple-element.132), channel_id=1, source_target_pairs={{0,24},{8,0},{16,8},{24,16},{1,25},{9,1},{17,9},{25,17},{2,26},{10... | collective-permute-start | bytes 470024 | tf_op jit(solution)/shard_map/ppermute | solution.py:44
  405.4 9.4 %collective-permute-start.47 = (bf16[72,1088]{1,0:T(8,128)(2,1)S(1)}, bf16[72,1088]{1,0:T(8,128)(2,1)S(1)}, u32[]{:S(2)}, u32[]{:S(2)}) collective-permute-start(bf16[72,1088]{1,0:T(8,128)(2,1)S(1)} %get-tuple-element.133), channel_id=1, source_target_pairs={{0,8},{8,16},{16,24},{24,0},{1,9},{9,17},{17,25},{25,1},{2,10},{10... | collective-permute-start | bytes 470024 | tf_op jit(solution)/shard_map/ppermute | solution.py:44
  405.7 9.0 %collective-permute-start.40 = (bf16[72,1088]{1,0:T(8,128)(2,1)S(1)}, bf16[72,1088]{1,0:T(8,128)(2,1)S(1)}, u32[]{:S(2)}, u32[]{:S(2)}) collective-permute-start(bf16[72,1088]{1,0:T(8,128)(2,1)S(1)} %get-tuple-element.134), channel_id=1, source_target_pairs={{0,64},{32,96},{64,0},{96,32},{1,65},{33,97},{65,1},{97,33},{2,66}... | collective-permute-start | bytes 470024 | tf_op jit(solution)/shard_map/ppermute | solution.py:44
  407.7 7.9 %collective-permute-start.42 = (bf16[72,1088]{1,0:T(8,128)(2,1)S(1)}, bf16[72,1088]{1,0:T(8,128)(2,1)S(1)}, u32[]{:S(2)}, u32[]{:S(2)}) collective-permute-start(bf16[72,1088]{1,0:T(8,128)(2,1)S(1)} %get-tuple-element.135), channel_id=1, source_target_pairs={{0,96},{32,0},{64,32},{96,64},{1,97},{33,1},{65,33},{97,65},{2,98}... | collective-permute-start | bytes 470024 | tf_op jit(solution)/shard_map/ppermute | solution.py:44
  411.3 6.6 %collective-permute-start.41 = (bf16[72,1088]{1,0:T(8,128)(2,1)S(1)}, bf16[72,1088]{1,0:T(8,128)(2,1)S(1)}, u32[]{:S(2)}, u32[]{:S(2)}) collective-permute-start(bf16[72,1088]{1,0:T(8,128)(2,1)S(1)} %get-tuple-element.136), channel_id=1, source_target_pairs={{0,32},{32,64},{64,96},{96,0},{1,33},{33,65},{65,97},{97,1},{2,34}... | collective-permute-start | bytes 470024 | tf_op jit(solution)/shard_map/ppermute | solution.py:44
  418.1 7.8 %collective-permute-start.50 = (bf16[72,1088]{1,0:T(8,128)(2,1)S(1)}, bf16[72,1088]{1,0:T(8,128)(2,1)S(1)}, u32[]{:S(2)}, u32[]{:S(2)}) collective-permute-start(bf16[72,1088]{1,0:T(8,128)(2,1)S(1)} %broadcast_select_fusion.10), channel_id=1, source_target_pairs={{0,6},{6,0},{2,4},{4,2},{1,7},{7,1},{3,5},{5,3},{8,14},{14,8},{10,... | collective-permute-start | bytes 470024 | tf_op jit(solution)/shard_map/ppermute | solution.py:44
  421.2 6.8 %collective-permute-start.51 = (bf16[72,1088]{1,0:T(8,128)(2,1)S(1)}, bf16[72,1088]{1,0:T(8,128)(2,1)S(1)}, u32[]{:S(2)}, u32[]{:S(2)}) collective-permute-start(bf16[72,1088]{1,0:T(8,128)(2,1)S(1)} %broadcast_select_fusion.10), channel_id=1, source_target_pairs={{0,2},{2,0},{1,3},{3,1},{4,6},{6,4},{5,7},{7,5},{8,10},{10,8},{9,1... | collective-permute-start | bytes 470024 | tf_op jit(solution)/shard_map/ppermute | solution.py:44
  421.8 6.3 %collective-permute-start.49 = (bf16[72,1088]{1,0:T(8,128)(2,1)S(1)}, bf16[72,1088]{1,0:T(8,128)(2,1)S(1)}, u32[]{:S(2)}, u32[]{:S(2)}) collective-permute-start(bf16[72,1088]{1,0:T(8,128)(2,1)S(1)} %get-tuple-element.84), channel_id=1, source_target_pairs={{0,4},{4,0},{1,5},{5,1},{2,6},{6,2},{3,7},{7,3},{8,12},{12,8},{9,1... | collective-permute-start | bytes 470024 | tf_op jit(solution)/shard_map/ppermute | solution.py:44
  431.0 19.7 %collective-permute-start.59 = (bf16[32,1088]{1,0:T(8,128)(2,1)S(1)}, bf16[32,1088]{1,0:T(8,128)(2,1)S(1)}, u32[]{:S(2)}, u32[]{:S(2)}) collective-permute-start(bf16[32,1088]{1,0:T(8,128)(2,1)S(1)} %slice.407), channel_id=1, source_target_pairs={{0,64},{32,96},{64,0},{96,32},{1,65},{33,97},{65,1},{97,33},{2,66}... | collective-permute-start | bytes 208904 | tf_op jit(solution)/shard_map/ppermute | solution.py:44
  431.9 20.0 %collective-permute-start.58 = (bf16[32,1088]{1,0:T(8,128)(2,1)S(1)}, bf16[32,1088]{1,0:T(8,128)(2,1)S(1)}, u32[]{:S(2)}, u32[]{:S(2)}) collective-permute-start(bf16[32,1088]{1,0:T(8,128)(2,1)S(1)} %slice.407), channel_id=1, source_target_pairs={{0,96},{32,0},{64,32},{96,64},{1,97},{33,1},{65,33},{97,65},{2,98}... | collective-permute-start | bytes 208904 | tf_op jit(solution)/shard_map/ppermute | solution.py:44
  433.8 18.1 %collective-permute-start.60 = (bf16[32,1088]{1,0:T(8,128)(2,1)S(1)}, bf16[32,1088]{1,0:T(8,128)(2,1)S(1)}, u32[]{:S(2)}, u32[]{:S(2)}) collective-permute-start(bf16[32,1088]{1,0:T(8,128)(2,1)S(1)} %slice.407), channel_id=1, source_target_pairs={{0,32},{32,64},{64,96},{96,0},{1,33},{33,65},{65,97},{97,1},{2,34}... | collective-permute-start | bytes 208904 | tf_op jit(solution)/shard_map/ppermute | solution.py:44
  434.8 20.0 %collective-permute-start.53 = (bf16[40,1088]{1,0:T(8,128)(2,1)S(1)}, bf16[40,1088]{1,0:T(8,128)(2,1)S(1)}, u32[]{:S(2)}, u32[]{:S(2)}) collective-permute-start(bf16[40,1088]{1,0:T(8,128)(2,1)S(1)} %slice.406), channel_id=1, source_target_pairs={{0,16},{8,24},{16,0},{24,8},{1,17},{9,25},{17,1},{25,9},{2,18},{10... | collective-permute-start | bytes 261128 | tf_op jit(solution)/shard_map/ppermute | solution.py:44
  438.9 16.2 %collective-permute-start.52 = (bf16[40,1088]{1,0:T(8,128)(2,1)S(1)}, bf16[40,1088]{1,0:T(8,128)(2,1)S(1)}, u32[]{:S(2)}, u32[]{:S(2)}) collective-permute-start(bf16[40,1088]{1,0:T(8,128)(2,1)S(1)} %slice.406), channel_id=1, source_target_pairs={{0,24},{8,0},{16,8},{24,16},{1,25},{9,1},{17,9},{25,17},{2,26},{10... | collective-permute-start | bytes 261128 | tf_op jit(solution)/shard_map/ppermute | solution.py:44
  450.6 8.4 %collective-permute-start.54 = (bf16[40,1088]{1,0:T(8,128)(2,1)S(1)}, bf16[40,1088]{1,0:T(8,128)(2,1)S(1)}, u32[]{:S(2)}, u32[]{:S(2)}) collective-permute-start(bf16[40,1088]{1,0:T(8,128)(2,1)S(1)} %slice.406), channel_id=1, source_target_pairs={{0,8},{8,16},{16,24},{24,0},{1,9},{9,17},{17,25},{25,1},{2,10},{10... | collective-permute-start | bytes 261128 | tf_op jit(solution)/shard_map/ppermute | solution.py:44
  452.0 10.7 %collective-permute-start.62 = (bf16[4,32,1088]{2,1,0:T(8,128)(2,1)S(1)}, bf16[4,32,1088]{2,1,0:T(8,128)(2,1)S(1)}, u32[]{:S(2)}, u32[]{:S(2)}) collective-permute-start(bf16[4,32,1088]{2,1,0:T(8,128)(2,1)S(1)} %pad_maximum_fusion.16), channel_id=1, source_target_pairs={{0,16},{8,24},{16,0},{24,8},{1,17},{9,25},{17,1},{25,9},{2,18},{10... | collective-permute-start | bytes 835592 | tf_op jit(solution)/shard_map/ppermute | solution.py:44
  452.3 12.2 %collective-permute-start.61 = (bf16[4,32,1088]{2,1,0:T(8,128)(2,1)S(1)}, bf16[4,32,1088]{2,1,0:T(8,128)(2,1)S(1)}, u32[]{:S(2)}, u32[]{:S(2)}) collective-permute-start(bf16[4,32,1088]{2,1,0:T(8,128)(2,1)S(1)} %pad_maximum_fusion.16), channel_id=1, source_target_pairs={{0,24},{8,0},{16,8},{24,16},{1,25},{9,1},{17,9},{25,17},{2,26},{10... | collective-permute-start | bytes 835592 | tf_op jit(solution)/shard_map/ppermute | solution.py:44
  454.8 11.4 %collective-permute-start.63 = (bf16[4,32,1088]{2,1,0:T(8,128)(2,1)S(1)}, bf16[4,32,1088]{2,1,0:T(8,128)(2,1)S(1)}, u32[]{:S(2)}, u32[]{:S(2)}) collective-permute-start(bf16[4,32,1088]{2,1,0:T(8,128)(2,1)S(1)} %pad_maximum_fusion.16), channel_id=1, source_target_pairs={{0,8},{8,16},{16,24},{24,0},{1,9},{9,17},{17,25},{25,1},{2,10},{10... | collective-permute-start | bytes 835592 | tf_op jit(solution)/shard_map/ppermute | solution.py:44
  459.1 9.2 %collective-permute-start.56 = (bf16[4,40,1088]{2,1,0:T(8,128)(2,1)S(1)}, bf16[4,40,1088]{2,1,0:T(8,128)(2,1)S(1)}, u32[]{:S(2)}, u32[]{:S(2)}) collective-permute-start(bf16[4,40,1088]{2,1,0:T(8,128)(2,1)S(1)} %pad_maximum_fusion.14), channel_id=1, source_target_pairs={{0,64},{32,96},{64,0},{96,32},{1,65},{33,97},{65,1},{97,33},{2,66}... | collective-permute-start | bytes 1044488 | tf_op jit(solution)/shard_map/ppermute | solution.py:44
  460.9 9.9 %collective-permute-start.55 = (bf16[4,40,1088]{2,1,0:T(8,128)(2,1)S(1)}, bf16[4,40,1088]{2,1,0:T(8,128)(2,1)S(1)}, u32[]{:S(2)}, u32[]{:S(2)}) collective-permute-start(bf16[4,40,1088]{2,1,0:T(8,128)(2,1)S(1)} %pad_maximum_fusion.14), channel_id=1, source_target_pairs={{0,96},{32,0},{64,32},{96,64},{1,97},{33,1},{65,33},{97,65},{2,98}... | collective-permute-start | bytes 1044488 | tf_op jit(solution)/shard_map/ppermute | solution.py:44
  462.7 9.5 %collective-permute-start.57 = (bf16[4,40,1088]{2,1,0:T(8,128)(2,1)S(1)}, bf16[4,40,1088]{2,1,0:T(8,128)(2,1)S(1)}, u32[]{:S(2)}, u32[]{:S(2)}) collective-permute-start(bf16[4,40,1088]{2,1,0:T(8,128)(2,1)S(1)} %pad_maximum_fusion.14), channel_id=1, source_target_pairs={{0,32},{32,64},{64,96},{96,0},{1,33},{33,65},{65,97},{97,1},{2,34}... | collective-permute-start | bytes 1044488 | tf_op jit(solution)/shard_map/ppermute | solution.py:44
  (89 other events, 896.9 us)
Sparse Core Ops, SparseCore 0:
  61.4 46.0 all-gather.4
  109.6 45.0 all-gather.8
  219.2 90.5 reduce-scatter.1
  330.2 82.5 all-gather.6

commit v3 on v2

--- a/solution.py
+++ b/solution.py
@@ -73,7 +73,8 @@
 
 
 def after(x, done):
-    done = done.reshape((-1,) + done.shape[-2:])[0, :16, :128]
+    if done.size > 2**19:
+        done = done.reshape((-1,) + done.shape[-2:])[0, :8, :128]
     return pl.pallas_call(
         after_kernel,
         out_shape=jax.ShapeDtypeStruct(x.shape, x.dtype),
@@ -108,15 +109,33 @@
     return total.astype(BF)
 
 
+def ring_scatter_halves(part, axis):
+    place = lax.axis_index(axis)
+    far, ahead, behind = (part((place + step) & 3) for step in (2, 1, 3))
+    half = far.shape[0] // 2
+    from_behind, from_ahead = rotate(far[:half], axis, 1), rotate(far[half:], axis, -1)
+
+    def added(value, more):
+        return (value.astype(F32) + more.astype(F32)).astype(BF)
+
+    ahead = jnp.concatenate([added(ahead[:half], from_behind), ahead[half:]])
+    behind = jnp.concatenate([behind[:half], added(behind[half:], from_ahead)])
+    one, two = rotate(ahead, axis, 1), rotate(behind, axis, -1)
+    total = part(place).astype(F32) + one.astype(F32) + two.astype(F32)
+    return total.astype(BF)
+
+
 def ring_gather(piece, axis):
     far, behind, ahead = (rotate(piece, axis, step) for step in (2, 1, 3))
     return natural([piece, ahead, far, behind], lax.axis_index(axis))
 
 
-def depth_sum(values, zh):
+def depth_sum(values, zh, done=None):
     mine = jnp.where(zh == 0, values[0], values[1])
     other = jnp.where(zh == 0, values[1], values[0])
     far, half, near = swap_far(other), swap_half(other), swap_near(mine)
+    if done is not None:
+        near = after(near, done)
     total = mine.astype(F32) + near.astype(F32) + far.astype(F32) + half.astype(F32)
     return total.astype(BF)
 
@@ -336,40 +355,84 @@
     )(pieces)
 
 
-def gather_quarters(shard, small):
+def gather_quarters(shard):
     across, down = lax.axis_index("x") & 1, lax.axis_index("y") & 1
-    quarter = down * 2 + across
-    piece = rows_of(shard, quarter * 64, 64)
-    got = swap_far(jnp.concatenate([piece, shard[256:], small]))
+    piece = rows_of(shard, (down * 2 + across) * 64, 64)
+    got = swap_far(jnp.concatenate([piece, shard[256:]]))
     mine = got[:64]
     by_x, by_y = swap_pair(mine, "x"), swap_pair(mine, "y")
-    last_x, last_y = swap_pair(by_y[:32], "x"), swap_pair(by_x[32:], "y")
-    return by_x, jnp.concatenate([got, by_x, by_y, last_x, last_y])
-
-
-def far_piece(shard, spot, done):
-    unit = shard.shape[0] // 17
-    piece = rows_of(shard, spot * unit, unit)
-    return swap_far(after(jnp.concatenate([piece, shard[16 * unit :]]), done))
-
-
-def gather_spread(shard, got):
-    unit = shard.shape[0] // 17
-    far = rows_major(lax.all_gather(got[:unit], ("y", "x"), axis=0, tiled=True))
-    rest = got[unit:]
-    rows, main = shard.shape[0], 16 * unit
-    return assemble(
-        rows,
-        (shard, swap_core(shard), far, rest, swap_core(far), swap_core(rest)),
+    last = swap_pair(by_y, "x")
+    return by_x, jnp.concatenate([got, by_x, by_y, last])
+
+
+def widened(value):
+    size = value.shape[0] // 4
+    return jnp.concatenate([value[at * size : (at + 1) * size] for at in range(4)], axis=1)
+
+
+def narrowed(value):
+    return jnp.stack([value[:, :, at * D : (at + 1) * D] for at in range(4)], axis=1).reshape(-1, D)
+
+
+def start_mlp(w_up, w_down, small, spot, done):
+    sent = [
+        rows_of(w_up, spot * 16, 16),
+        widened(rows_of(w_down, spot * 64, 64)),
+        w_up[256:],
+        widened(w_down[1024:]),
+        small,
+    ]
+    got = swap_far(after(jnp.concatenate(sent), done))
+    rest = got[32:]
+    across_rest = swap_core(jnp.concatenate([rest, small]))
+    far = lax.all_gather(got[:32], ("y", "x"), axis=0, tiled=True)
+    smalls = [small[0], across_rest[48], rest[32], across_rest[32]]
+    return got, far, across_rest, [value[: 12 * QUART].astype(F32) for value in smalls]
+
+
+def finish_mlp(w_up, w_down, got, far, across_rest):
+    rest = got[32:]
+    across = swap_core(far).reshape(16, 32, 4 * D)
+    far = far.reshape(16, 32, 4 * D)
+    up = assemble(
+        QUART,
         (
-            (0, 0, 0, 0, None, rows),
-            (1, 0, 1, 0, None, rows),
-            (2, 0, 2, 0, None, main),
-            (3, 0, 2, main, None, unit),
-            (4, 0, 3, 0, None, main),
-            (5, 0, 3, main, None, unit),
-        ),
-    )
+            w_up,
+            swap_core(w_up),
+            far[:, :16].reshape(256, 4 * D),
+            rest,
+            across[:, :16].reshape(256, 4 * D),
+            across_rest,
+        ),
+        (
+            (0, 0, 0, 0, None, QUART),
+            (1, 0, 1, 0, None, QUART),
+            (2, 0, 2, 0, None, 256),
+            (3, 0, 2, 256, None, 16),
+            (4, 0, 3, 0, None, 256),
+            (5, 0, 3, 256, None, 16),
+        ),
+    )
+    down = assemble(
+        D,
+        (
+            w_down,
+            swap_core(w_down),
+            narrowed(far[:, 16:]),
+            narrowed(rest[None, 16:32]),
+            narrowed(across[:, 16:]),
+            narrowed(across_rest[None, 16:32]),
+        ),
+        (
+            (0, 0, 0, 0, None, D),
+            (1, 0, 1, 0, None, D),
+            (2, 0, 2, 0, None, 1024),
+            (3, 0, 2, 1024, None, 64),
+            (4, 0, 3, 0, None, 1024),
+            (5, 0, 3, 1024, None, 64),
+        ),
+    )
+    return up, down
 
 
 def body(
@@ -406,30 +469,23 @@
             bias_down,
         ]
     )
-    small = jnp.pad(small[None], ((0, 15), (0, 0)))
+    small = jnp.pad(small[None], ((0, 15), (0, D)))
     rows = block_input.shape[1]
     own_tokens = block_input[0]
-    by_x, far_parts = gather_quarters(w_qkv, small)
-    beside = swap_core(jnp.concatenate([w_qkv, small]))
+    by_x, far_parts = gather_quarters(w_qkv)
     across_parts = swap_core(far_parts)
     half_tokens = swap_half(after(own_tokens, by_x))
     tokens = [own_tokens, swap_core(own_tokens), half_tokens, swap_core(half_tokens)]
-    got_up = far_piece(w_up, spot, by_x)
-    got_down = far_piece(w_down, spot, got_up)
-    full_up = gather_spread(w_up, got_up)
-    full_down = gather_spread(w_down, got_down)
-    turns = ((0, 0, 0, 64), (96, 0, 1, 64), (160, 0, 2, 64), (224, 0, 3, 64), (64, 256, None, 16))
+    got_mlp, far_mlp, across_rest, smalls = start_mlp(w_up, w_down, small, spot, across_parts)
+    turns = ((0, 0, 0, 64), (80, 0, 1, 64), (144, 0, 2, 64), (208, 0, 3, 64), (64, 256, None, 16))
     full_qkv = assemble(
         QUART,
-        (w_qkv, beside, far_parts, across_parts),
+        (w_qkv, swap_core(w_qkv), far_parts, across_parts),
         ((0, 0, 0, 0, None, QUART), (1, 0, 1, 0, None, QUART))
         + tuple((2, row, 2, *turn) for row, *turn in turns)
         + tuple((3, row, 3, *turn) for row, *turn in turns),
     )
-    smalls = [
-        value.astype(F32) for value in (small[0], beside[QUART], far_parts[80], across_parts[80])
-    ]
-    far_out = after(swap_far(after(w_out, got_down)), full_qkv)
+    far_out = after(swap_far(after(w_out, got_mlp)), full_qkv)
     full_out = assemble(
         QUART,
         (w_out, swap_core(w_out), far_out, swap_core(far_out)),
@@ -482,6 +538,8 @@
     )
     mask = jnp.where(allowed, 0.0, -1e30).astype(F32)
     mixed, log_total = attend_forward(queries, keys, values, mask)
+    far_mlp = after(far_mlp, mixed)
+    full_up, full_down = finish_mlp(w_up, w_down, got_mlp, far_mlp, across_rest)
     middle = hidden_in + jnp.dot(mixed, full_out, preferred_element_type=F32) + out_bias
     normed_two = layer_norm(middle, gain_two, shift_two).astype(BF)
     upper = jnp.dot(normed_two, full_up, preferred_element_type=F32) + up_bias
@@ -533,12 +591,15 @@
     )
     d_beside = swap_core(d_beside)
     d_half = swap_half((d_both[1].astype(F32) + d_beside[1].astype(F32)).astype(BF))
+    queries_pair = paired(d_queries)
+    grad_attn = weight_grad(mixed_pair, [d_attended_pair], no_vectors, 1, 12, 0)
+    d_half = after(after(after(d_half, grad_attn), queries_pair[1]), normed_pair[1])
     d_both = d_both[0].astype(F32) + d_beside[0].astype(F32) + d_half.astype(F32)
     d_both = d_both.astype(BF)
     d_keys, d_values = d_both[0], d_both[1]
     grad_query_bias = jnp.sum(d_queries.astype(F32), axis=0)
     grad_value_bias = jnp.sum(d_values.astype(F32), axis=0)
-    rights = [paired(d_queries), paired(d_keys), paired(d_values)]
+    rights = [queries_pair, paired(d_keys), paired(d_values)]
     d_normed = None
     for at, part in enumerate((d_queries, d_keys, d_values)):
         term = lax.dot_general(
@@ -575,10 +636,8 @@
     mine = (mine + swap_core(other.astype(BF)).astype(F32)).astype(BF)
     mine = jnp.pad(mine.reshape(2, 12, VECTOR).astype(F32), ((0, 0), (0, 0), (0, D - VECTOR)))
 
-    early = depth_sum(mlp_part.transpose(1, 0, 2, 3).reshape(2, 2 * PAD, D), zh)
-    normed_pair = (normed_pair[0], after(normed_pair[1], early))
-    grad_attn = weight_grad(mixed_pair, [d_attended_pair], no_vectors, 1, 12, 0)
     grad_attn = weight_grad(normed_pair, rights, mine, 1, 0, 0, grad_attn)
+    early = depth_sum(mlp_part.transpose(1, 0, 2, 3).reshape(2, 2 * PAD, D), zh, grad_attn)
     grad_attn = grad_attn.reshape(4, 4, 2, PAD, D)
 
     def cut(start, size):
@@ -592,10 +651,10 @@
             values, (place, 0, 0), (1, PAD, D), allow_negative_indices=False
         )[0]
 
-    one = ring_scatter(
+    one = ring_scatter_halves(
         lambda place: cut((0, place, 0, 0, 0), (4, 1, 1, PAD, D)).reshape(4, PAD, D), "x"
     )
-    two = ring_scatter(
+    two = ring_scatter_halves(
         lambda place: cut((place, 0, 1, 0, 0), (1, 4, 1, PAD, D)).reshape(4, PAD, D), "y"
     )
     one, two = ring_scatter(part_of(one), "y"), ring_scatter(part_of(two), "x")

time: 499 us -> 496 us (level)
  matrix products: 61 us -> 53.5 us
  local copies, waits for them, and re-layouts: 94.8 us -> 101 us
  starting transfers between devices: 64.7 us -> 58.5 us
    ppermute x64 -> x62, waiting for transfers between devices: 133 us -> 140 us  [permute(): return rows_major(lax.ppermute(rows_major(x), axis, pairs)).reshape(shape)]
    concatenate x11, local copies, waits for them, and re-layouts: 6.64 us -> 0.28 us  [body(): jnp.concatenate([attn_gain, attn_shift, bias_query, bias_value, bias_out,...]
    another operation x0 -> x5, local copies, waits for them, and re-layouts: none -> 6.1 us  [the longest x4 5.83 us: narrowed(): jnp.stack([value[:, :, at * D:(at + 1) * D] for at in range(4)], axis=1)]
    ppermute x64 -> x62, starting transfers between devices: 64.4 us -> 58.4 us  [permute(): return rows_major(lax.ppermute(rows_major(x), axis, pairs)).reshape(shape)]
    unnamed x178 -> x227, local copies, waits for them, and re-layouts: 34.4 us -> 39.9 us
    squeeze x9 -> x8, local copies, waits for them, and re-layouts: 10.8 us -> 8.72 us  [after(): done = done.reshape((-1,) + done.shape[-2:])[0, :8, :128]]
  transfers between devices with their start and end apart: 68 -> 65, of which waited for: 33 -> 34; matrix products, arithmetic and copies ran while one was open for 31% -> 29% of each run, Pallas kernels for 14% -> 13%
where the time goes in v3:
time: 496 us; the launch traced here: 487 us
  waiting for transfers between devices  140 us (28%)
  local copies, waits for them, and re-layouts  101 us (20%)
  Pallas kernels  80.8 us (16%)
  starting transfers between devices  58.5 us (12%)
  matrix products  53.5 us (11%)
  other arithmetic  38 us (8%)
  between operations  15.7 us (3%)
    ppermute x62, waiting for transfers between devices, permute(): return rows_major(lax.ppermute(rows_major(x), axis, pairs)).reshape(shape)  140 us
    ppermute x62, starting transfers between devices, permute(): return rows_major(lax.ppermute(rows_major(x), axis, pairs)).reshape(shape)  58.4 us
    unnamed x227, local copies, waits for them, and re-layouts  39.9 us
    pallas_call x1, Pallas kernels, attend_backward(): pl.pallas_call(attend_backward_kernel, grid=((HEADS + 1) // 2,), out_shap...  21.8 us
    pallas_call x4, Pallas kernels, weight_grad(): pl.pallas_call(functools.partial(weight_grad_kernel, len(rights) // 2, fi...  20.4 us
    pallas_call x1, Pallas kernels, attend_forward(): pl.pallas_call(attend_forward_kernel, grid=((HEADS + 1) // 2,), out_shape...  15 us
    pallas_call x4, Pallas kernels, assemble(): pl.pallas_call(functools.partial(assemble_kernel, spots), out_shape=jax.S...  14.9 us
  transfers between devices with their start and end apart: 65, of which 34 were waited for; matrix products, arithmetic and copies ran while one was open for 29% of the time, Pallas kernels for 13%

profile of v3, /device:TPU:0, one launch (start us, length us, event | category | flops | bytes accessed | tf_op | source)
XLA Modules:
  0.0 487.4 jit_solution(1603004053699889451)
XLA Ops:
  9.5 4.2 collective-permute-start
  20.5 5.9 %collective-permute-done = bf16[80,3264]{1,0:T(8,128)(2,1)S(1)} collective-permute-done((bf16[80,3264]{1,0:T(8,128)(2,1)S(1)}, bf16[80,3264]{1,0:T(8,128)(2,1)S(1)}, u32[]{:S(2)}, u32[]{:S(2)}) %collective-permute-start) | collective-permute-done | bytes 522272 | tf_op jit(solution)/shard_map/ppermute | solution.py:44
  29.6 8.5 %collective-permute-done.1.done_ref = bf16[64,3264]{1,0:T(8,128)(2,1)S(1)} collective-permute-done((bf16[64,3264]{1,0:T(8,128)(2,1)S(1)}, bf16[64,3264]{1,0:T(8,128)(2,1)S(1)}, u32[]{:S(2)}, u32[]{:S(2)}) %collective-permute-start.1) | collective-permute-done | bytes 417824 | tf_op jit(solution)/shard_map/ppermute | solution.py:44
  39.9 10.4 %collective-permute-done.3 = bf16[64,3264]{1,0:T(8,128)(2,1)S(1)} collective-permute-done((bf16[64,3264]{1,0:T(8,128)(2,1)S(1)}, bf16[64,3264]{1,0:T(8,128)(2,1)S(1)}, u32[]{:S(2)}, u32[]{:S(2)}) %collective-permute-start.3) | collective-permute-done | bytes 417824 | tf_op jit(solution)/shard_map/ppermute | solution.py:44
  56.0 2.8 collective-permute-start.5
  60.7 14.3 %collective-permute-done.5.done_ref = bf16[80,4352]{1,0:T(8,128)(2,1)S(1)} collective-permute-done((bf16[80,4352]{1,0:T(8,128)(2,1)}, bf16[80,4352]{1,0:T(8,128)(2,1)S(1)}, u32[]{:S(2)}, u32[]{:S(2)}) %collective-permute-start.5) | collective-permute-done | bytes 696352 | tf_op jit(solution)/shard_map/ppermute | solution.py:44
  79.5 12.6 %collective-permute-done.9 = bf16[4,64,1088]{2,1,0:T(8,128)(2,1)S(1)} collective-permute-done((bf16[4,64,1088]{2,1,0:T(8,128)(2,1)}, bf16[4,64,1088]{2,1,0:T(8,128)(2,1)S(1)}, u32[]{:S(2)}, u32[]{:S(2)}) %collective-permute-start.9) | collective-permute-done | bytes 557088 | tf_op jit(solution)/shard_map/ppermute | solution.py:44
  99.0 4.6 shard_map.272
  103.6 2.9 copy-done
  108.4 3.0 collective-permute-start.12
  116.4 2.8 fusion.44
  119.2 3.0 fusion.6.q_ref
  122.2 5.8 %convolution_convert_fusion.k_ref = bf16[1024,1088]{1,0:T(8,128)(2,1)S(1)} fusion(bf16[1088,3264]{1,0:T(8,128)(2,1)S(1)} %bitcast.383, bf16[256,1088]{1,0:T(8,128)(2,1)S(1)} %get-tuple-element.196, bf16[256,1088]{1,0:T(8,128)(2,1)S(1)} %get-tuple-element.195, bf16[256,1088]{1,0:T(8,128)(2,1)S(1)} %get-tuple-element.194, ...), kind=kOutput, calls=%fused_computation.8 | convolution fusion | flops 2434334720 | bytes 7094272 | tf_op jit(solution)/shard_map/dot_general | solution.py:524
  128.0 5.4 %add_convert_fusion.v_ref = bf16[1024,1088]{1,0:T(8,128)(2,1)S(1)} fusion(f32[1088]{0:T(1024)S(1)} %copy-done.92, bf16[1088,3264]{1,0:T(8,128)(2,1)S(1)} %bitcast.383, bf16[256,1088]{1,0:T(8,128)(2,1)S(1)} %get-tuple-element.196, bf16[256,1088]{1,0:T(8,128)(2,1)S(1)} %get-tuple-element.195, bf16[256,1088]{1,0:T(8,128)(2,1)S(1)} %get-tuple-element.194, ...), kind=kOutput, calls=%fused_computation.4 | convolution fusion | flops 2435448832 | bytes 7102464 | tf_op jit(solution)/shard_map/dot_general | solution.py:525
  133.5 15.0 %shard_map.274 = (bf16[256,1088]{1,0:T(8,128)(2,1)S(1)}, f32[256,1088]{1,0:T(8,128)S(1)}) custom-call(bf16[256,1088]{1,0:T(8,128)(2,1)S(1)} %fusion.6.q_ref, bf16[1024,1088]{1,0:T(8,128)(2,1)S(1)} %convolution_convert_fusion.k_ref, bf16[1024,1088]{1,0:T(8,128)(2,1)S(1)} %add_convert_fusion.v_ref, f32[256,1024]{1,0:T(8,128)S(1)} %copy-done.21), custom_call_target="tpu_custom_call" | custom-call | flops 1140850688 | bytes 6684672 | tf_op jit(solution)/shard_map/pallas_call | solution.py:239
  154.7 5.8 %collective-permute-done.13.refs_3_ = bf16[272,1088]{1,0:T(8,128)(2,1)S(1)} collective-permute-done((bf16[272,1088]{1,0:T(8,128)(2,1)}, bf16[272,1088]{1,0:T(8,128)(2,1)S(1)}, u32[]{:S(2)}, u32[]{:S(2)}) %collective-permute-start.13) | collective-permute-done | bytes 591904 | tf_op jit(solution)/shard_map/ppermute | solution.py:44
  160.5 2.3 shard_map.277
  169.3 3.2 shard_map.279
  172.5 4.2 slice_bitcast_fusion.9
  177.1 3.3 multiply_convert_fusion
  180.5 4.7 shard_map.280
  185.3 9.0 %convert_reduce_fusion = (f32[4352]{0:T(1024)}, bf16[256,4352]{1,0:T(8,128)(2,1)}) fusion(f32[256,4352]{1,0:T(8,128)S(1)} %get-tuple-element.207, bf16[4352,1088]{1,0:T(8,128)(2,1)S(1)} %shard_map.280, bf16[1,256,1088]{1,2,0:T(8,128)(2,1)S(1)} %copy-done.61), kind=kOutput, calls=%fused_computation.5 | convolution fusion | flops 2437672704 | bytes 16729088 | tf_op jit(solution)/shard_map/dot_general | solution.py:566
  203.5 4.8 shard_map.281.refs_5_
  208.3 7.2 %shard_map.282 = bf16[16,2,2,72,1088]{4,3,2,1,0:T(8,128)(2,1)} custom-call(bf16[2,256,272]{2,1,0:T(8,128)(2,1)S(1)} %get-tuple-element.148.refs_0_, bf16[2,256,272]{2,1,0:T(8,128)(2,1)S(1)} %bitcast.400, bf16[256,4352]{1,0:T(8,128)(2,1)} %get-tuple-element.212.refs_2_, ...), custom_call_target="tpu_custom_call", output_to_operand_aliasing={{}: (5, {})} | custom-call | flops 2424307712 | bytes 10079232 | tf_op jit(solution)/shard_map/pallas_call | solution.py:318
  215.6 8.6 %fusion.75 = (f32[1088]{0:T(1024)}, f32[256,1088]{0,1:T(8,128)}) fusion(bf16[256,4352]{1,0:T(8,128)(2,1)} %get-tuple-element.212.refs_2_, bf16[1088,4352]{1,0:T(8,128)(2,1)} %copy-done.2), kind=kOutput, calls=%fused_computation.302 | convolution fusion | flops 2424585216 | bytes 12816640 | tf_op jit(solution)/shard_map/dot_general | solution.py:579
  224.2 2.8 copy.120
  241.5 21.8 %shard_map.284 = (bf16[256,1088]{1,0:T(8,128)(2,1)S(1)}, bf16[2,2,256,1088]{3,2,1,0:T(8,128)(2,1)S(1)}, bf16[2,2,256,1088]{3,2,1,0:T(8,128)(2,1)}) custom-call(bf16[256,1088]{1,0:T(8,128)(2,1)S(1)} %copy-done.30, bf16[1024,1088]{1,0:T(8,128)(2,1)S(1)} %copy-done.24, bf16[1024,1088]{1,0:T(8,128)(2,1)S(1)} %copy-done.26, f32[256,1024]{1,0:T(8,128)S(1)} %copy-done.22, ...), custom_call_target="tpu_custom_call" | custom-call | flops 2852126720 | bytes 13369344 | tf_op jit(solution)/shard_map/pallas_call | solution.py:266
  266.6 3.8 collective-permute-done.21
  270.5 2.6 fusion.7
  279.9 3.1 shard_map.285.refs_9_
  285.1 2.4 slice.601
  287.4 15.5 %collective-permute-done.22 = bf16[8,64,1088]{2,1,0:T(8,128)(2,1)} collective-permute-done((bf16[8,64,1088]{2,1,0:T(8,128)(2,1)}, bf16[8,64,1088]{2,1,0:T(8,128)(2,1)}, u32[]{:S(2)}, u32[]{:S(2)}) %collective-permute-start.22) | collective-permute-done | bytes 1114144 | tf_op jit(solution)/shard_map/ppermute | solution.py:44
  305.4 2.1 fusion.9
  308.7 3.3 fusion.13
  312.1 2.8 fusion.10
  314.9 3.0 fusion.66
  319.7 2.5 fusion.72
  325.2 3.7 collective-permute-start.47
  328.9 5.3 %shard_map.289 = bf16[16,1,2,72,1088]{4,3,2,1,0:T(8,128)(2,1)} custom-call(bf16[2,256,272]{2,1,0:T(8,128)(2,1)S(1)} %copy-done.18, bf16[2,256,272]{2,1,0:T(8,128)(2,1)} %bitcast.87.done_ref.refs_1_, bf16[256,1088]{1,0:T(8,128)(2,1)S(1)} %get-tuple-element.22.refs_2_, bf16[256,1088]{1,0:T(8,128)(2,1)S(1)} %bitcast.393, ...), custom_call_target="tpu_custom_call", output_to_operand_aliasing={{}: (9, {})} | custom-call | flops 1818230784 | bytes 7711744 | tf_op jit(solution)/shard_map/pallas_call | solution.py:318
  335.4 8.8 %collective-permute-done.47.x_ref = bf16[144,1088]{1,0:T(8,128)(2,1)} collective-permute-done((bf16[144,1088]{1,0:T(8,128)(2,1)S(1)}, bf16[144,1088]{1,0:T(8,128)(2,1)}, u32[]{:S(2)}, u32[]{:S(2)}) %collective-permute-start.47) | collective-permute-done | bytes 313376 | tf_op jit(solution)/shard_map/ppermute | solution.py:44
  344.2 2.2 add_convert_fusion.2
  354.2 2.0 collective-permute-start.39
  359.2 5.1 %collective-permute-done.37 = bf16[2,72,1088]{2,1,0:T(8,128)(2,1)} collective-permute-done((bf16[2,72,1088]{2,1,0:T(8,128)(2,1)S(1)}, bf16[2,72,1088]{2,1,0:T(8,128)(2,1)}, u32[]{:S(2)}, u32[]{:S(2)}) %collective-permute-start.37) | collective-permute-done | bytes 313376 | tf_op jit(solution)/shard_map/ppermute | solution.py:44
  364.3 2.3 collective-permute-done.39
  366.7 2.0 fusion.47
  368.8 3.3 collective-permute-start.40
  376.1 7.3 %fusion.5 = f32[1,256,1088]{2,1,0:T(8,128)S(1)} fusion(f32[256,1088]{1,0:T(8,128)S(1)} %copy-done.37, bf16[256,4352]{1,0:T(8,128)(2,1)S(1)} %copy-done.55, bf16[4352,1088]{1,0:T(8,128)(2,1)} %copy-done.1, f32[1088]{0:T(1024)S(1)} %add.347), kind=kOutput, calls=%fused_computation.16 | convolution fusion | flops 2424864768 | bytes 13930752 | tf_op jit(solution)/shard_map/dot_general | solution.py:548
  384.8 6.9 %collective-permute-done.40 = bf16[4,72,1088]{2,1,0:T(8,128)(2,1)} collective-permute-done((bf16[4,72,1088]{2,1,0:T(8,128)(2,1)S(1)}, bf16[4,72,1088]{2,1,0:T(8,128)(2,1)}, u32[]{:S(2)}, u32[]{:S(2)}) %collective-permute-start.40) | collective-permute-done | bytes 626720 | tf_op jit(solution)/shard_map/ppermute | solution.py:44
  391.7 4.0 collective-permute-done.33
  395.7 6.3 %collective-permute-done.31 = bf16[4,72,1088]{2,1,0:T(8,128)(2,1)} collective-permute-done((bf16[4,72,1088]{2,1,0:T(8,128)(2,1)}, bf16[4,72,1088]{2,1,0:T(8,128)(2,1)}, u32[]{:S(2)}, u32[]{:S(2)}) %collective-permute-start.31) | collective-permute-done | bytes 626720 | tf_op jit(solution)/shard_map/ppermute | solution.py:44
  402.0 3.7 collective-permute-done.38
  405.7 2.6 fusion.25
  412.0 3.4 collective-permute-done.41
  417.6 4.4 collective-permute-done.35
  422.4 4.0 collective-permute-start.44
  428.3 2.3 collective-permute-done.45
  439.8 3.0 slice_bitcast_fusion
  442.7 2.6 shard_map.294
  446.7 2.8 shard_map.292
  451.6 2.6 collective-permute-start.60
  456.6 3.4 collective-permute-start.54
  465.7 3.8 collective-permute-done.53
  470.0 2.2 pad_maximum_fusion
  478.5 2.2 shard_map.296
  (504 shorter events, 149.5 us)
Async XLA Ops:
  7.3 144.4 %all-gather.3.cloned.1.call-start = ((), (), s32[]{:S(2)}) async-start(), calls=%async_computation.1 | async-start | bytes 4734976 | tf_op jit(solution)/shard_map/all_gather | solution.py:388
  7.3 88.6 %collective-permute-start.7 = (bf16[272,3264]{1,0:T(8,128)(2,1)}, bf16[272,3264]{1,0:T(8,128)(2,1)}, u32[]{:S(2)}, u32[]{:S(2)}) collective-permute-start(bf16[272,3264]{1,0:T(8,128)(2,1)} %refs_0_.4), channel_id=1, source_target_pairs={{0,1},{1,0},{2,3},{3,2},{4,5},{5,4},{6,7},{7,6},{8,9},{9,8},{10,11... | collective-permute-start | bytes 5326856 | tf_op jit(solution)/shard_map/ppermute | solution.py:44
  9.5 16.9 %collective-permute-start = (bf16[80,3264]{1,0:T(8,128)(2,1)S(1)}, bf16[80,3264]{1,0:T(8,128)(2,1)S(1)}, u32[]{:S(2)}, u32[]{:S(2)}) collective-permute-start(bf16[80,3264]{1,0:T(8,128)(2,1)S(1)} %pad_maximum_fusion.11), channel_id=1, source_target_pairs={{0,6},{6,0},{2,4},{4,2},{1,7},{7,1},{3,5},{5,3},{8,14},{14,8},{10,... | collective-permute-start | bytes 1566728 | tf_op jit(solution)/shard_map/ppermute | solution.py:44
  13.7 141.0 %collective-permute-start.11 = (bf16[272,1088]{1,0:T(8,128)(2,1)}, bf16[272,1088]{1,0:T(8,128)(2,1)}, u32[]{:S(2)}, u32[]{:S(2)}) collective-permute-start(bf16[272,1088]{1,0:T(8,128)(2,1)} %refs_0_.5), channel_id=1, source_target_pairs={{0,1},{1,0},{2,3},{3,2},{4,5},{5,4},{6,7},{7,6},{8,9},{9,8},{10,11... | collective-permute-start | bytes 1775624 | tf_op jit(solution)/shard_map/ppermute | solution.py:44
  13.9 155.0 %collective-permute-start.14 = (bf16[272,4352]{1,0:T(8,128)(2,1)}, bf16[272,4352]{1,0:T(8,128)(2,1)}, u32[]{:S(2)}, u32[]{:S(2)}) collective-permute-start(bf16[272,4352]{1,0:T(8,128)(2,1)} %refs_0_.6), channel_id=1, source_target_pairs={{0,1},{1,0},{2,3},{3,2},{4,5},{5,4},{6,7},{7,6},{8,9},{9,8},{10,11... | collective-permute-start | bytes 7102472 | tf_op jit(solution)/shard_map/ppermute | solution.py:44
  26.4 11.6 %collective-permute-start.1 = (bf16[64,3264]{1,0:T(8,128)(2,1)S(1)}, bf16[64,3264]{1,0:T(8,128)(2,1)S(1)}, u32[]{:S(2)}, u32[]{:S(2)}) collective-permute-start(bf16[64,3264]{1,0:T(8,128)(2,1)S(1)} %slice.552), channel_id=1, source_target_pairs={{0,8},{8,0},{16,24},{24,16},{1,9},{9,1},{17,25},{25,17},{2,10},{10... | collective-permute-start | bytes 1253384 | tf_op jit(solution)/shard_map/ppermute | solution.py:44
  28.0 11.3 %collective-permute-start.2 = (bf16[64,3264]{1,0:T(8,128)(2,1)S(1)}, bf16[64,3264]{1,0:T(8,128)(2,1)S(1)}, u32[]{:S(2)}, u32[]{:S(2)}) collective-permute-start(bf16[64,3264]{1,0:T(8,128)(2,1)S(1)} %slice.552), channel_id=1, source_target_pairs={{0,32},{32,0},{64,96},{96,64},{1,33},{33,1},{65,97},{97,65},{2,34}... | collective-permute-start | bytes 1253384 | tf_op jit(solution)/shard_map/ppermute | solution.py:44
  38.1 22.5 %collective-permute-start.8 = (bf16[4,64,1088]{2,1,0:T(8,128)(2,1)S(1)}, bf16[4,64,1088]{2,1,0:T(8,128)(2,1)S(1)}, u32[]{:S(2)}, u32[]{:S(2)}) collective-permute-start(bf16[4,64,1088]{2,1,0:T(8,128)(2,1)S(1)} %bitcast.411), channel_id=1, source_target_pairs={{0,1},{1,0},{2,3},{3,2},{4,5},{5,4},{6,7},{7,6},{8,9},{9,8},{10,11... | collective-permute-start | bytes 1671176 | tf_op jit(solution)/shard_map/ppermute | solution.py:44
  39.3 11.0 %collective-permute-start.3 = (bf16[64,3264]{1,0:T(8,128)(2,1)S(1)}, bf16[64,3264]{1,0:T(8,128)(2,1)S(1)}, u32[]{:S(2)}, u32[]{:S(2)}) collective-permute-start(bf16[64,3264]{1,0:T(8,128)(2,1)S(1)} %collective-permute-done.2), channel_id=1, source_target_pairs={{0,8},{8,0},{16,24},{24,16},{1,9},{9,1},{17,25},{25,17},{2,10},{10... | collective-permute-start | bytes 1253384 | tf_op jit(solution)/shard_map/ppermute | solution.py:44
  50.3 3.8 collective-permute-start.4
  56.0 19.1 %collective-permute-start.5 = (bf16[80,4352]{1,0:T(8,128)(2,1)}, bf16[80,4352]{1,0:T(8,128)(2,1)S(1)}, u32[]{:S(2)}, u32[]{:S(2)}) collective-permute-start(bf16[80,4352]{1,0:T(8,128)(2,1)} %shard_map.271), channel_id=1, source_target_pairs={{0,6},{6,0},{2,4},{4,2},{1,7},{7,1},{3,5},{5,3},{8,14},{14,8},{10,... | collective-permute-start | bytes 2088968 | tf_op jit(solution)/shard_map/ppermute | solution.py:44
  60.5 119.9 %collective-permute-start.16 = (bf16[1088,1088]{1,0:T(8,128)(2,1)}, bf16[1088,1088]{1,0:T(8,128)(2,1)}, u32[]{:S(2)}, u32[]{:S(2)}) collective-permute-start(bf16[1088,1088]{1,0:T(8,128)(2,1)} %refs_0_.7), channel_id=1, source_target_pairs={{0,1},{1,0},{2,3},{3,2},{4,5},{5,4},{6,7},{7,6},{8,9},{9,8},{10,11... | collective-permute-start | bytes 7102472 | tf_op jit(solution)/shard_map/ppermute | solution.py:44
  75.9 16.3 %collective-permute-start.9 = (bf16[4,64,1088]{2,1,0:T(8,128)(2,1)}, bf16[4,64,1088]{2,1,0:T(8,128)(2,1)S(1)}, u32[]{:S(2)}, u32[]{:S(2)}) collective-permute-start(bf16[4,64,1088]{2,1,0:T(8,128)(2,1)} %bitcast.422), channel_id=1, source_target_pairs={{0,2},{2,0},{1,3},{3,1},{4,6},{6,4},{5,7},{7,5},{8,10},{10,8},{9,1... | collective-permute-start | bytes 1671176 | tf_op jit(solution)/shard_map/ppermute | solution.py:44
  77.9 245.0 %reduce-scatter.2.cloned.1.call-start = ((), (), s32[]{:S(2)}) async-start(), calls=%async_computation.2 | async-start | bytes 11280384 | tf_op jit(solution)/shard_map/reduce_scatter | solution.py:575
  108.0 5.0 %collective-permute-start.6 = (bf16[64,4352]{1,0:T(8,128)(2,1)}, bf16[64,4352]{1,0:T(8,128)(2,1)}, u32[]{:S(2)}, u32[]{:S(2)}) collective-permute-start(bf16[64,4352]{1,0:T(8,128)(2,1)} %pad_maximum_fusion.10), channel_id=1, source_target_pairs={{0,1},{1,0},{2,3},{3,2},{4,5},{5,4},{6,7},{7,6},{8,9},{9,8},{10,11... | collective-permute-start | bytes 1671176 | tf_op jit(solution)/shard_map/ppermute | solution.py:44
  108.4 45.5 %collective-permute-start.12 = (bf16[272,1088]{1,0:T(8,128)(2,1)}, bf16[272,1088]{1,0:T(8,128)(2,1)}, u32[]{:S(2)}, u32[]{:S(2)}) collective-permute-start(bf16[272,1088]{1,0:T(8,128)(2,1)} %shard_map.275), channel_id=1, source_target_pairs={{0,6},{6,0},{2,4},{4,2},{1,7},{7,1},{3,5},{5,3},{8,14},{14,8},{10,... | collective-permute-start | bytes 1775624 | tf_op jit(solution)/shard_map/ppermute | solution.py:44
  151.8 15.2 %collective-permute-start.15 = (bf16[512,4352]{1,0:T(8,128)(2,1)}, bf16[512,4352]{1,0:T(8,128)(2,1)}, u32[]{:S(2)}, u32[]{:S(2)}) collective-permute-start(bf16[512,4352]{1,0:T(8,128)(2,1)} %shard_map.278), channel_id=1, source_target_pairs={{0,1},{1,0},{2,3},{3,2},{4,5},{5,4},{6,7},{7,6},{8,9},{9,8},{10,11... | collective-permute-start | bytes 13369352 | tf_op jit(solution)/shard_map/ppermute | solution.py:44
  153.9 6.6 %collective-permute-start.13 = (bf16[272,1088]{1,0:T(8,128)(2,1)}, bf16[272,1088]{1,0:T(8,128)(2,1)S(1)}, u32[]{:S(2)}, u32[]{:S(2)}) collective-permute-start(bf16[272,1088]{1,0:T(8,128)(2,1)} %shard_map.276.refs_2_), channel_id=1, source_target_pairs={{0,1},{1,0},{2,3},{3,2},{4,5},{5,4},{6,7},{7,6},{8,9},{9,8},{10,11... | collective-permute-start | bytes 1775624 | tf_op jit(solution)/shard_map/ppermute | solution.py:44
  194.3 14.0 %collective-permute-start.18 = (bf16[256,4352]{1,0:T(8,128)(2,1)}, bf16[256,4352]{1,0:T(8,128)(2,1)}, u32[]{:S(2)}, u32[]{:S(2)}) collective-permute-start(bf16[256,4352]{1,0:T(8,128)(2,1)} %get-tuple-element.212.refs_2_), channel_id=1, source_target_pairs={{0,1},{1,0},{2,3},{3,2},{4,5},{5,4},{6,7},{7,6},{8,9},{9,8},{10,11... | collective-permute-start | bytes 6684680 | tf_op jit(solution)/shard_map/ppermute | solution.py:44
  196.6 4.6 collective-permute-start.19
  198.3 2.8 collective-permute-start.20
  200.2 8.1 %collective-permute-start.17 = (bf16[8,64,272]{2,1,0:T(8,128)(2,1)S(1)}, bf16[8,64,272]{2,1,0:T(8,128)(2,1)S(1)}, u32[]{:S(2)}, u32[]{:S(2)}) collective-permute-start(bf16[8,64,272]{2,1,0:T(8,128)(2,1)S(1)} %bitcast.425), channel_id=1, source_target_pairs={{0,1},{1,0},{2,3},{3,2},{4,5},{5,4},{6,7},{7,6},{8,9},{9,8},{10,11... | collective-permute-start | bytes 835592 | tf_op jit(solution)/shard_map/ppermute | solution.py:44
  215.5 216.7 %all-gather.5.cloned.1.call-start = ((), (), s32[]{:S(2)}) async-start(), calls=%async_computation.3 | async-start | bytes 5640192 | tf_op jit(solution)/shard_map/all_gather | solution.py:662
  264.7 5.7 %collective-permute-start.21 = (bf16[16,64,1088]{2,1,0:T(8,128)(2,1)}, bf16[16,64,1088]{2,1,0:T(8,128)(2,1)}, u32[]{:S(2)}, u32[]{:S(2)}) collective-permute-start(bf16[16,64,1088]{2,1,0:T(8,128)(2,1)} %bitcast.66), channel_id=1, source_target_pairs={{0,1},{1,0},{2,3},{3,2},{4,5},{5,4},{6,7},{7,6},{8,9},{9,8},{10,11... | collective-permute-start | bytes 6684680 | tf_op jit(solution)/shard_map/ppermute | solution.py:44
  264.9 15.1 %collective-permute-start.24 = (bf16[4,64,1088]{2,1,0:T(8,128)(2,1)S(1)}, bf16[4,64,1088]{2,1,0:T(8,128)(2,1)}, u32[]{:S(2)}, u32[]{:S(2)}) collective-permute-start(bf16[4,64,1088]{2,1,0:T(8,128)(2,1)S(1)} %bitcast.391), channel_id=1, source_target_pairs={{0,1},{1,0},{2,3},{3,2},{4,5},{5,4},{6,7},{7,6},{8,9},{9,8},{10,11... | collective-permute-start | bytes 1671176 | tf_op jit(solution)/shard_map/ppermute | solution.py:44
  273.1 29.8 %collective-permute-start.22 = (bf16[8,64,1088]{2,1,0:T(8,128)(2,1)}, bf16[8,64,1088]{2,1,0:T(8,128)(2,1)}, u32[]{:S(2)}, u32[]{:S(2)}) collective-permute-start(bf16[8,64,1088]{2,1,0:T(8,128)(2,1)} %fusion.7), channel_id=1, source_target_pairs={{0,2},{2,0},{1,3},{3,1},{4,6},{6,4},{5,7},{7,5},{8,10},{10,8},{9,1... | collective-permute-start | bytes 3342344 | tf_op jit(solution)/shard_map/ppermute | solution.py:44
  274.3 5.7 %collective-permute-start.23 = (bf16[8,64,272]{2,1,0:T(8,128)(2,1)}, bf16[8,64,272]{2,1,0:T(8,128)(2,1)S(1)}, u32[]{:S(2)}, u32[]{:S(2)}) collective-permute-start(bf16[8,64,272]{2,1,0:T(8,128)(2,1)} %bitcast.74), channel_id=1, source_target_pairs={{0,1},{1,0},{2,3},{3,2},{4,5},{5,4},{6,7},{7,6},{8,9},{9,8},{10,11... | collective-permute-start | bytes 835592 | tf_op jit(solution)/shard_map/ppermute | solution.py:44
  274.4 28.5 %collective-permute-start.25 = (bf16[4,64,1088]{2,1,0:T(8,128)(2,1)S(1)}, bf16[4,64,1088]{2,1,0:T(8,128)(2,1)S(1)}, u32[]{:S(2)}, u32[]{:S(2)}) collective-permute-start(bf16[4,64,1088]{2,1,0:T(8,128)(2,1)S(1)} %bitcast.390), channel_id=1, source_target_pairs={{0,1},{1,0},{2,3},{3,2},{4,5},{5,4},{6,7},{7,6},{8,9},{9,8},{10,11... | collective-permute-start | bytes 1671176 | tf_op jit(solution)/shard_map/ppermute | solution.py:44
  276.3 27.4 %collective-permute-start.26 = (bf16[8,64,272]{2,1,0:T(8,128)(2,1)}, bf16[8,64,272]{2,1,0:T(8,128)(2,1)}, u32[]{:S(2)}, u32[]{:S(2)}) collective-permute-start(bf16[8,64,272]{2,1,0:T(8,128)(2,1)} %bitcast.86), channel_id=1, source_target_pairs={{0,1},{1,0},{2,3},{3,2},{4,5},{5,4},{6,7},{7,6},{8,9},{9,8},{10,11... | collective-permute-start | bytes 835592 | tf_op jit(solution)/shard_map/ppermute | solution.py:44
  319.6 3.1 collective-permute-start.29
  322.2 6.7 %collective-permute-start.28 = (bf16[4,64,1088]{2,1,0:T(8,128)(2,1)}, bf16[4,64,1088]{2,1,0:T(8,128)(2,1)}, u32[]{:S(2)}, u32[]{:S(2)}) collective-permute-start(bf16[4,64,1088]{2,1,0:T(8,128)(2,1)} %bitcast.93), channel_id=1, source_target_pairs={{0,1},{1,0},{2,3},{3,2},{4,5},{5,4},{6,7},{7,6},{8,9},{9,8},{10,11... | collective-permute-start | bytes 1671176 | tf_op jit(solution)/shard_map/ppermute | solution.py:44
  322.7 6.2 %collective-permute-start.27 = (bf16[4,64,1088]{2,1,0:T(8,128)(2,1)}, bf16[4,64,1088]{2,1,0:T(8,128)(2,1)}, u32[]{:S(2)}, u32[]{:S(2)}) collective-permute-start(bf16[4,64,1088]{2,1,0:T(8,128)(2,1)} %bitcast.91), channel_id=1, source_target_pairs={{0,1},{1,0},{2,3},{3,2},{4,5},{5,4},{6,7},{7,6},{8,9},{9,8},{10,11... | collective-permute-start | bytes 1671176 | tf_op jit(solution)/shard_map/ppermute | solution.py:44
  324.8 19.4 %collective-permute-start.48 = (bf16[144,1088]{1,0:T(8,128)(2,1)}, bf16[144,1088]{1,0:T(8,128)(2,1)}, u32[]{:S(2)}, u32[]{:S(2)}) collective-permute-start(bf16[144,1088]{1,0:T(8,128)(2,1)} %bitcast.125), channel_id=1, source_target_pairs={{0,6},{6,0},{2,4},{4,2},{1,7},{7,1},{3,5},{5,3},{8,14},{14,8},{10,... | collective-permute-start | bytes 940040 | tf_op jit(solution)/shard_map/ppermute | solution.py:44
  325.2 19.1 %collective-permute-start.49 = (bf16[144,1088]{1,0:T(8,128)(2,1)}, bf16[144,1088]{1,0:T(8,128)(2,1)}, u32[]{:S(2)}, u32[]{:S(2)}) collective-permute-start(bf16[144,1088]{1,0:T(8,128)(2,1)} %bitcast.125), channel_id=1, source_target_pairs={{0,2},{2,0},{1,3},{3,1},{4,6},{6,4},{5,7},{7,5},{8,10},{10,8},{9,1... | collective-permute-start | bytes 940040 | tf_op jit(solution)/shard_map/ppermute | solution.py:44
  325.2 19.0 %collective-permute-start.47 = (bf16[144,1088]{1,0:T(8,128)(2,1)S(1)}, bf16[144,1088]{1,0:T(8,128)(2,1)}, u32[]{:S(2)}, u32[]{:S(2)}) collective-permute-start(bf16[144,1088]{1,0:T(8,128)(2,1)S(1)} %bitcast.423), channel_id=1, source_target_pairs={{0,4},{4,0},{1,5},{5,1},{2,6},{6,2},{3,7},{7,3},{8,12},{12,8},{9,1... | collective-permute-start | bytes 940040 | tf_op jit(solution)/shard_map/ppermute | solution.py:44
  347.8 10.4 %collective-permute-start.30 = (bf16[2,72,1088]{2,1,0:T(8,128)(2,1)S(1)}, bf16[2,72,1088]{2,1,0:T(8,128)(2,1)}, u32[]{:S(2)}, u32[]{:S(2)}) collective-permute-start(bf16[2,72,1088]{2,1,0:T(8,128)(2,1)S(1)} %get-tuple-element.103), channel_id=1, source_target_pairs={{0,8},{8,16},{16,24},{24,0},{1,9},{9,17},{17,25},{25,1},{2,10},{10... | collective-permute-start | bytes 940040 | tf_op jit(solution)/shard_map/ppermute | solution.py:44
  349.5 9.7 %collective-permute-start.32 = (bf16[2,72,1088]{2,1,0:T(8,128)(2,1)S(1)}, bf16[2,72,1088]{2,1,0:T(8,128)(2,1)}, u32[]{:S(2)}, u32[]{:S(2)}) collective-permute-start(bf16[2,72,1088]{2,1,0:T(8,128)(2,1)S(1)} %get-tuple-element.105), channel_id=1, source_target_pairs={{0,24},{8,0},{16,8},{24,16},{1,25},{9,1},{17,9},{25,17},{2,26},{10... | collective-permute-start | bytes 940040 | tf_op jit(solution)/shard_map/ppermute | solution.py:44
  352.5 11.8 %collective-permute-start.37 = (bf16[2,72,1088]{2,1,0:T(8,128)(2,1)S(1)}, bf16[2,72,1088]{2,1,0:T(8,128)(2,1)}, u32[]{:S(2)}, u32[]{:S(2)}) collective-permute-start(bf16[2,72,1088]{2,1,0:T(8,128)(2,1)S(1)} %get-tuple-element.99), channel_id=1, source_target_pairs={{0,32},{32,64},{64,96},{96,0},{1,33},{33,65},{65,97},{97,1},{2,34}... | collective-permute-start | bytes 940040 | tf_op jit(solution)/shard_map/ppermute | solution.py:44
  354.2 12.5 %collective-permute-start.39 = (bf16[2,72,1088]{2,1,0:T(8,128)(2,1)S(1)}, bf16[2,72,1088]{2,1,0:T(8,128)(2,1)}, u32[]{:S(2)}, u32[]{:S(2)}) collective-permute-start(bf16[2,72,1088]{2,1,0:T(8,128)(2,1)S(1)} %get-tuple-element.102), channel_id=1, source_target_pairs={{0,96},{32,0},{64,32},{96,64},{1,97},{33,1},{65,33},{97,65},{2,98}... | collective-permute-start | bytes 940040 | tf_op jit(solution)/shard_map/ppermute | solution.py:44
  368.8 22.9 %collective-permute-start.40 = (bf16[4,72,1088]{2,1,0:T(8,128)(2,1)S(1)}, bf16[4,72,1088]{2,1,0:T(8,128)(2,1)}, u32[]{:S(2)}, u32[]{:S(2)}) collective-permute-start(bf16[4,72,1088]{2,1,0:T(8,128)(2,1)S(1)} %pad_maximum_fusion.9), channel_id=1, source_target_pairs={{0,96},{32,0},{64,32},{96,64},{1,97},{33,1},{65,33},{97,65},{2,98}... | collective-permute-start | bytes 1880072 | tf_op jit(solution)/shard_map/ppermute | solution.py:44
  372.1 23.6 %collective-permute-start.33 = (bf16[4,72,1088]{2,1,0:T(8,128)(2,1)S(1)}, bf16[4,72,1088]{2,1,0:T(8,128)(2,1)}, u32[]{:S(2)}, u32[]{:S(2)}) collective-permute-start(bf16[4,72,1088]{2,1,0:T(8,128)(2,1)S(1)} %pad_maximum_fusion.7), channel_id=1, source_target_pairs={{0,24},{8,0},{16,8},{24,16},{1,25},{9,1},{17,9},{25,17},{2,26},{10... | collective-permute-start | bytes 1880072 | tf_op jit(solution)/shard_map/ppermute | solution.py:44
  374.1 27.9 %collective-permute-start.31 = (bf16[4,72,1088]{2,1,0:T(8,128)(2,1)}, bf16[4,72,1088]{2,1,0:T(8,128)(2,1)}, u32[]{:S(2)}, u32[]{:S(2)}) collective-permute-start(bf16[4,72,1088]{2,1,0:T(8,128)(2,1)} %pad_maximum_fusion.6), channel_id=1, source_target_pairs={{0,8},{8,16},{16,24},{24,0},{1,9},{9,17},{17,25},{25,1},{2,10},{10... | collective-permute-start | bytes 1880072 | tf_op jit(solution)/shard_map/ppermute | solution.py:44
  376.1 29.6 %collective-permute-start.38 = (bf16[4,72,1088]{2,1,0:T(8,128)(2,1)}, bf16[4,72,1088]{2,1,0:T(8,128)(2,1)}, u32[]{:S(2)}, u32[]{:S(2)}) collective-permute-start(bf16[4,72,1088]{2,1,0:T(8,128)(2,1)} %pad_maximum_fusion.8), channel_id=1, source_target_pairs={{0,32},{32,64},{64,96},{96,0},{1,33},{33,65},{65,97},{97,1},{2,34}... | collective-permute-start | bytes 1880072 | tf_op jit(solution)/shard_map/ppermute | solution.py:44
  408.4 7.0 %collective-permute-start.41 = (bf16[72,1088]{1,0:T(8,128)(2,1)S(1)}, bf16[72,1088]{1,0:T(8,128)(2,1)S(1)}, u32[]{:S(2)}, u32[]{:S(2)}) collective-permute-start(bf16[72,1088]{1,0:T(8,128)(2,1)S(1)} %get-tuple-element.151), channel_id=1, source_target_pairs={{0,16},{8,24},{16,0},{24,8},{1,17},{9,25},{17,1},{25,9},{2,18},{10... | collective-permute-start | bytes 470024 | tf_op jit(solution)/shard_map/ppermute | solution.py:44
  408.5 7.2 %collective-permute-start.43 = (bf16[72,1088]{1,0:T(8,128)(2,1)S(1)}, bf16[72,1088]{1,0:T(8,128)(2,1)S(1)}, u32[]{:S(2)}, u32[]{:S(2)}) collective-permute-start(bf16[72,1088]{1,0:T(8,128)(2,1)S(1)} %get-tuple-element.152), channel_id=1, source_target_pairs={{0,24},{8,0},{16,8},{24,16},{1,25},{9,1},{17,9},{25,17},{2,26},{10... | collective-permute-start | bytes 470024 | tf_op jit(solution)/shard_map/ppermute | solution.py:44
  409.8 7.3 %collective-permute-start.42 = (bf16[72,1088]{1,0:T(8,128)(2,1)S(1)}, bf16[72,1088]{1,0:T(8,128)(2,1)S(1)}, u32[]{:S(2)}, u32[]{:S(2)}) collective-permute-start(bf16[72,1088]{1,0:T(8,128)(2,1)S(1)} %get-tuple-element.153), channel_id=1, source_target_pairs={{0,8},{8,16},{16,24},{24,0},{1,9},{9,17},{17,25},{25,1},{2,10},{10... | collective-permute-start | bytes 470024 | tf_op jit(solution)/shard_map/ppermute | solution.py:44
  410.6 6.9 %collective-permute-start.34 = (bf16[72,1088]{1,0:T(8,128)(2,1)S(1)}, bf16[72,1088]{1,0:T(8,128)(2,1)S(1)}, u32[]{:S(2)}, u32[]{:S(2)}) collective-permute-start(bf16[72,1088]{1,0:T(8,128)(2,1)S(1)} %get-tuple-element.154), channel_id=1, source_target_pairs={{0,64},{32,96},{64,0},{96,32},{1,65},{33,97},{65,1},{97,33},{2,66}... | collective-permute-start | bytes 470024 | tf_op jit(solution)/shard_map/ppermute | solution.py:44
  410.7 6.8 %collective-permute-start.36 = (bf16[72,1088]{1,0:T(8,128)(2,1)S(1)}, bf16[72,1088]{1,0:T(8,128)(2,1)S(1)}, u32[]{:S(2)}, u32[]{:S(2)}) collective-permute-start(bf16[72,1088]{1,0:T(8,128)(2,1)S(1)} %get-tuple-element.155), channel_id=1, source_target_pairs={{0,96},{32,0},{64,32},{96,64},{1,97},{33,1},{65,33},{97,65},{2,98}... | collective-permute-start | bytes 470024 | tf_op jit(solution)/shard_map/ppermute | solution.py:44
  415.4 6.6 %collective-permute-start.35 = (bf16[72,1088]{1,0:T(8,128)(2,1)S(1)}, bf16[72,1088]{1,0:T(8,128)(2,1)S(1)}, u32[]{:S(2)}, u32[]{:S(2)}) collective-permute-start(bf16[72,1088]{1,0:T(8,128)(2,1)S(1)} %get-tuple-element.156), channel_id=1, source_target_pairs={{0,32},{32,64},{64,96},{96,0},{1,33},{33,65},{65,97},{97,1},{2,34}... | collective-permute-start | bytes 470024 | tf_op jit(solution)/shard_map/ppermute | solution.py:44
  422.2 8.4 %collective-permute-start.45 = (bf16[72,1088]{1,0:T(8,128)(2,1)S(1)}, bf16[72,1088]{1,0:T(8,128)(2,1)S(1)}, u32[]{:S(2)}, u32[]{:S(2)}) collective-permute-start(bf16[72,1088]{1,0:T(8,128)(2,1)S(1)} %broadcast_select_fusion.10), channel_id=1, source_target_pairs={{0,6},{6,0},{2,4},{4,2},{1,7},{7,1},{3,5},{5,3},{8,14},{14,8},{10,... | collective-permute-start | bytes 470024 | tf_op jit(solution)/shard_map/ppermute | solution.py:44
  422.3 8.3 %collective-permute-start.46 = (bf16[72,1088]{1,0:T(8,128)(2,1)S(1)}, bf16[72,1088]{1,0:T(8,128)(2,1)S(1)}, u32[]{:S(2)}, u32[]{:S(2)}) collective-permute-start(bf16[72,1088]{1,0:T(8,128)(2,1)S(1)} %broadcast_select_fusion.10), channel_id=1, source_target_pairs={{0,2},{2,0},{1,3},{3,1},{4,6},{6,4},{5,7},{7,5},{8,10},{10,8},{9,1... | collective-permute-start | bytes 470024 | tf_op jit(solution)/shard_map/ppermute | solution.py:44
  422.4 9.1 %collective-permute-start.44 = (bf16[72,1088]{1,0:T(8,128)(2,1)S(1)}, bf16[72,1088]{1,0:T(8,128)(2,1)S(1)}, u32[]{:S(2)}, u32[]{:S(2)}) collective-permute-start(bf16[72,1088]{1,0:T(8,128)(2,1)S(1)} %get-tuple-element.84), channel_id=1, source_target_pairs={{0,4},{4,0},{1,5},{5,1},{2,6},{6,2},{3,7},{7,3},{8,12},{12,8},{9,1... | collective-permute-start | bytes 470024 | tf_op jit(solution)/shard_map/ppermute | solution.py:44
  434.3 16.4 %collective-permute-start.57 = (bf16[32,1088]{1,0:T(8,128)(2,1)S(1)}, bf16[32,1088]{1,0:T(8,128)(2,1)S(1)}, u32[]{:S(2)}, u32[]{:S(2)}) collective-permute-start(bf16[32,1088]{1,0:T(8,128)(2,1)S(1)} %slice.615), channel_id=1, source_target_pairs={{0,64},{32,96},{64,0},{96,32},{1,65},{33,97},{65,1},{97,33},{2,66}... | collective-permute-start | bytes 208904 | tf_op jit(solution)/shard_map/ppermute | solution.py:44
  434.3 17.1 %collective-permute-start.56 = (bf16[32,1088]{1,0:T(8,128)(2,1)S(1)}, bf16[32,1088]{1,0:T(8,128)(2,1)S(1)}, u32[]{:S(2)}, u32[]{:S(2)}) collective-permute-start(bf16[32,1088]{1,0:T(8,128)(2,1)S(1)} %slice.615), channel_id=1, source_target_pairs={{0,96},{32,0},{64,32},{96,64},{1,97},{33,1},{65,33},{97,65},{2,98}... | collective-permute-start | bytes 208904 | tf_op jit(solution)/shard_map/ppermute | solution.py:44
  435.8 15.7 %collective-permute-start.58 = (bf16[32,1088]{1,0:T(8,128)(2,1)S(1)}, bf16[32,1088]{1,0:T(8,128)(2,1)S(1)}, u32[]{:S(2)}, u32[]{:S(2)}) collective-permute-start(bf16[32,1088]{1,0:T(8,128)(2,1)S(1)} %slice.615), channel_id=1, source_target_pairs={{0,32},{32,64},{64,96},{96,0},{1,33},{33,65},{65,97},{97,1},{2,34}... | collective-permute-start | bytes 208904 | tf_op jit(solution)/shard_map/ppermute | solution.py:44
  437.3 18.1 %collective-permute-start.51 = (bf16[40,1088]{1,0:T(8,128)(2,1)S(1)}, bf16[40,1088]{1,0:T(8,128)(2,1)S(1)}, u32[]{:S(2)}, u32[]{:S(2)}) collective-permute-start(bf16[40,1088]{1,0:T(8,128)(2,1)S(1)} %slice.614), channel_id=1, source_target_pairs={{0,16},{8,24},{16,0},{24,8},{1,17},{9,25},{17,1},{25,9},{2,18},{10... | collective-permute-start | bytes 261128 | tf_op jit(solution)/shard_map/ppermute | solution.py:44
  438.4 17.9 %collective-permute-start.50 = (bf16[40,1088]{1,0:T(8,128)(2,1)S(1)}, bf16[40,1088]{1,0:T(8,128)(2,1)S(1)}, u32[]{:S(2)}, u32[]{:S(2)}) collective-permute-start(bf16[40,1088]{1,0:T(8,128)(2,1)S(1)} %slice.614), channel_id=1, source_target_pairs={{0,24},{8,0},{16,8},{24,16},{1,25},{9,1},{17,9},{25,17},{2,26},{10... | collective-permute-start | bytes 261128 | tf_op jit(solution)/shard_map/ppermute | solution.py:44
  450.7 5.8 %collective-permute-start.52 = (bf16[40,1088]{1,0:T(8,128)(2,1)S(1)}, bf16[40,1088]{1,0:T(8,128)(2,1)S(1)}, u32[]{:S(2)}, u32[]{:S(2)}) collective-permute-start(bf16[40,1088]{1,0:T(8,128)(2,1)S(1)} %slice.614), channel_id=1, source_target_pairs={{0,8},{8,16},{16,24},{24,0},{1,9},{9,17},{17,25},{25,1},{2,10},{10... | collective-permute-start | bytes 261128 | tf_op jit(solution)/shard_map/ppermute | solution.py:44
  451.6 9.2 %collective-permute-start.60 = (bf16[4,32,1088]{2,1,0:T(8,128)(2,1)S(1)}, bf16[4,32,1088]{2,1,0:T(8,128)(2,1)S(1)}, u32[]{:S(2)}, u32[]{:S(2)}) collective-permute-start(bf16[4,32,1088]{2,1,0:T(8,128)(2,1)S(1)} %pad_maximum_fusion.21), channel_id=1, source_target_pairs={{0,16},{8,24},{16,0},{24,8},{1,17},{9,25},{17,1},{25,9},{2,18},{10... | collective-permute-start | bytes 835592 | tf_op jit(solution)/shard_map/ppermute | solution.py:44
  454.2 8.7 %collective-permute-start.59 = (bf16[4,32,1088]{2,1,0:T(8,128)(2,1)S(1)}, bf16[4,32,1088]{2,1,0:T(8,128)(2,1)S(1)}, u32[]{:S(2)}, u32[]{:S(2)}) collective-permute-start(bf16[4,32,1088]{2,1,0:T(8,128)(2,1)S(1)} %pad_maximum_fusion.21), channel_id=1, source_target_pairs={{0,24},{8,0},{16,8},{24,16},{1,25},{9,1},{17,9},{25,17},{2,26},{10... | collective-permute-start | bytes 835592 | tf_op jit(solution)/shard_map/ppermute | solution.py:44
  455.5 7.9 %collective-permute-start.61 = (bf16[4,32,1088]{2,1,0:T(8,128)(2,1)S(1)}, bf16[4,32,1088]{2,1,0:T(8,128)(2,1)S(1)}, u32[]{:S(2)}, u32[]{:S(2)}) collective-permute-start(bf16[4,32,1088]{2,1,0:T(8,128)(2,1)S(1)} %pad_maximum_fusion.21), channel_id=1, source_target_pairs={{0,8},{8,16},{16,24},{24,0},{1,9},{9,17},{17,25},{25,1},{2,10},{10... | collective-permute-start | bytes 835592 | tf_op jit(solution)/shard_map/ppermute | solution.py:44
  456.6 9.1 %collective-permute-start.54 = (bf16[4,40,1088]{2,1,0:T(8,128)(2,1)S(1)}, bf16[4,40,1088]{2,1,0:T(8,128)(2,1)S(1)}, u32[]{:S(2)}, u32[]{:S(2)}) collective-permute-start(bf16[4,40,1088]{2,1,0:T(8,128)(2,1)S(1)} %pad_maximum_fusion.20), channel_id=1, source_target_pairs={{0,64},{32,96},{64,0},{96,32},{1,65},{33,97},{65,1},{97,33},{2,66}... | collective-permute-start | bytes 1044488 | tf_op jit(solution)/shard_map/ppermute | solution.py:44
  459.9 9.5 %collective-permute-start.53 = (bf16[4,40,1088]{2,1,0:T(8,128)(2,1)S(1)}, bf16[4,40,1088]{2,1,0:T(8,128)(2,1)S(1)}, u32[]{:S(2)}, u32[]{:S(2)}) collective-permute-start(bf16[4,40,1088]{2,1,0:T(8,128)(2,1)S(1)} %pad_maximum_fusion.20), channel_id=1, source_target_pairs={{0,96},{32,0},{64,32},{96,64},{1,97},{33,1},{65,33},{97,65},{2,98}... | collective-permute-start | bytes 1044488 | tf_op jit(solution)/shard_map/ppermute | solution.py:44
  460.8 8.9 %collective-permute-start.55 = (bf16[4,40,1088]{2,1,0:T(8,128)(2,1)S(1)}, bf16[4,40,1088]{2,1,0:T(8,128)(2,1)S(1)}, u32[]{:S(2)}, u32[]{:S(2)}) collective-permute-start(bf16[4,40,1088]{2,1,0:T(8,128)(2,1)S(1)} %pad_maximum_fusion.20), channel_id=1, source_target_pairs={{0,32},{32,64},{64,96},{96,0},{1,33},{33,65},{65,97},{97,1},{2,34}... | collective-permute-start | bytes 1044488 | tf_op jit(solution)/shard_map/ppermute | solution.py:44
  (108 other events, 711.4 us)
Sparse Core Ops, SparseCore 0:
  78.0 54.4 all-gather.2
  215.7 88.7 reduce-scatter.1
  346.5 68.8 all-gather.4

commit v4 on v3

--- a/solution.py
+++ b/solution.py
@@ -355,6 +355,34 @@
     )(pieces)
 
 
+def unpack_pair_kernel(one_ref, two_ref, wide_ref, last_ref):
+    for down in range(4):
+        for across in range(4):
+            one, two = one_ref[down, across].astype(F32), two_ref[across, down].astype(F32)
+            part = jnp.concatenate([one, two[: SLICE - one.shape[0]]])
+            lines = slice(across * SLICE, (across + 1) * SLICE)
+            if down < 3:
+                wide_ref[lines, down * D : (down + 1) * D] = part
+            else:
+                last_ref[lines, :] = part
+
+
+def unpack_pair(one, two):
+    return pl.pallas_call(
+        unpack_pair_kernel,
+        out_shape=(
+            jax.ShapeDtypeStruct((QUART, 3 * D), F32),
+            jax.ShapeDtypeStruct((QUART, D), F32),
+        ),
+        in_specs=[pl.BlockSpec(memory_space=pltpu.VMEM)] * 2,
+        out_specs=(pl.BlockSpec(memory_space=pltpu.VMEM),) * 2,
+        compiler_params=pltpu.CompilerParams(vmem_limit_bytes=24 * 2**20),
+        cost_estimate=pl.CostEstimate(
+            flops=0, bytes_accessed=(one.size + two.size) * 6, transcendentals=0
+        ),
+    )(one, two)
+
+
 def gather_quarters(shard):
     across, down = lax.axis_index("x") & 1, lax.axis_index("y") & 1
     piece = rows_of(shard, (down * 2 + across) * 64, 64)
@@ -362,7 +390,7 @@
     mine = got[:64]
     by_x, by_y = swap_pair(mine, "x"), swap_pair(mine, "y")
     last = swap_pair(by_y, "x")
-    return by_x, jnp.concatenate([got, by_x, by_y, last])
+    return jnp.concatenate([got, by_x, by_y, last])
 
 
 def widened(value):
@@ -374,24 +402,15 @@
     return jnp.stack([value[:, :, at * D : (at + 1) * D] for at in range(4)], axis=1).reshape(-1, D)
 
 
-def start_mlp(w_up, w_down, small, spot, done):
-    sent = [
-        rows_of(w_up, spot * 16, 16),
-        widened(rows_of(w_down, spot * 64, 64)),
-        w_up[256:],
-        widened(w_down[1024:]),
-        small,
-    ]
+def start_mlp(w_up, w_down, spot, done, done_rest):
+    sent = [rows_of(w_up, spot * 16, 16), widened(rows_of(w_down, spot * 64, 64))]
     got = swap_far(after(jnp.concatenate(sent), done))
-    rest = got[32:]
-    across_rest = swap_core(jnp.concatenate([rest, small]))
-    far = lax.all_gather(got[:32], ("y", "x"), axis=0, tiled=True)
-    smalls = [small[0], across_rest[48], rest[32], across_rest[32]]
-    return got, far, across_rest, [value[: 12 * QUART].astype(F32) for value in smalls]
-
-
-def finish_mlp(w_up, w_down, got, far, across_rest):
-    rest = got[32:]
+    far = lax.all_gather(got, ("y", "x"), axis=0, tiled=True)
+    rest = swap_far(after(jnp.concatenate([w_up[256:], widened(w_down[1024:])]), done_rest))
+    return far, rest, swap_core(rest)
+
+
+def finish_mlp(w_up, w_down, rest, far, across_rest):
     across = swap_core(far).reshape(16, 32, 4 * D)
     far = far.reshape(16, 32, 4 * D)
     up = assemble(
@@ -469,14 +488,19 @@
             bias_down,
         ]
     )
-    small = jnp.pad(small[None], ((0, 15), (0, D)))
+    small = jnp.pad(small.reshape(3, D), ((0, 13), (0, 0)))
     rows = block_input.shape[1]
     own_tokens = block_input[0]
-    by_x, far_parts = gather_quarters(w_qkv)
+    far_parts = gather_quarters(w_qkv)
+    with_small = jnp.concatenate([own_tokens, small])
+    half = swap_half(with_small)
+    token_parts = [with_small, swap_core(with_small), half, swap_core(half)]
+    tokens = [part[:rows] for part in token_parts]
+    smalls = [part[rows : rows + 3].reshape(-1).astype(F32) for part in token_parts]
     across_parts = swap_core(far_parts)
-    half_tokens = swap_half(after(own_tokens, by_x))
-    tokens = [own_tokens, swap_core(own_tokens), half_tokens, swap_core(half_tokens)]
-    got_mlp, far_mlp, across_rest, smalls = start_mlp(w_up, w_down, small, spot, across_parts)
+    far_mlp, got_rest, across_rest = start_mlp(
+        w_up, w_down, spot, far_parts, across_parts
+    )
     turns = ((0, 0, 0, 64), (80, 0, 1, 64), (144, 0, 2, 64), (208, 0, 3, 64), (64, 256, None, 16))
     full_qkv = assemble(
         QUART,
@@ -485,7 +509,7 @@
         + tuple((2, row, 2, *turn) for row, *turn in turns)
         + tuple((3, row, 3, *turn) for row, *turn in turns),
     )
-    far_out = after(swap_far(after(w_out, got_mlp)), full_qkv)
+    far_out = after(swap_far(after(w_out, got_rest)), full_qkv)
     full_out = assemble(
         QUART,
         (w_out, swap_core(w_out), far_out, swap_core(far_out)),
@@ -539,7 +563,7 @@
     mask = jnp.where(allowed, 0.0, -1e30).astype(F32)
     mixed, log_total = attend_forward(queries, keys, values, mask)
     far_mlp = after(far_mlp, mixed)
-    full_up, full_down = finish_mlp(w_up, w_down, got_mlp, far_mlp, across_rest)
+    full_up, full_down = finish_mlp(w_up, w_down, got_rest, far_mlp, across_rest)
     middle = hidden_in + jnp.dot(mixed, full_out, preferred_element_type=F32) + out_bias
     normed_two = layer_norm(middle, gain_two, shift_two).astype(BF)
     upper = jnp.dot(normed_two, full_up, preferred_element_type=F32) + up_bias
@@ -636,8 +660,8 @@
     mine = (mine + swap_core(other.astype(BF)).astype(F32)).astype(BF)
     mine = jnp.pad(mine.reshape(2, 12, VECTOR).astype(F32), ((0, 0), (0, 0), (0, D - VECTOR)))
 
+    early = depth_sum(mlp_part.transpose(1, 0, 2, 3).reshape(2, 2 * PAD, D), zh, d_normed)
     grad_attn = weight_grad(normed_pair, rights, mine, 1, 0, 0, grad_attn)
-    early = depth_sum(mlp_part.transpose(1, 0, 2, 3).reshape(2, 2 * PAD, D), zh, grad_attn)
     grad_attn = grad_attn.reshape(4, 4, 2, PAD, D)
 
     def cut(start, size):
@@ -665,11 +689,9 @@
     attn_part = after(attn_part, parts)
     one, two = ring_gather(attn_part[:40], "x"), ring_gather(attn_part[40:], "y")
     one, two = ring_gather(one, "y"), ring_gather(two, "x")
-    attn = jnp.concatenate([one, two.transpose(1, 0, 2, 3)], axis=2).reshape(16, PAD, D)
-    attn = after(after(attn, grad_up), grad_down)
-    grad_qkv = unpack(attn[:12], QUART)
-    grad_out = unpack(attn[12:], QUART)
-    vectors = attn[:12, SLICE, :VECTOR].reshape(-1).astype(F32)
+    two = after(after(two, grad_up), grad_down)
+    grad_qkv, grad_out = unpack_pair(one, two)
+    vectors = two[:, :3, SLICE - 40, :VECTOR].transpose(1, 0, 2).reshape(-1).astype(F32)
 
     def owned(start, size):
         return vectors[start : start + size]

time: 496 us -> 495 us (level)
  local copies, waits for them, and re-layouts: 101 us -> 80 us
  other arithmetic: 38 us -> 48 us
  waiting for transfers between devices: 140 us -> 150 us
    unnamed x227 -> x194, local copies, waits for them, and re-layouts: 39.9 us -> 28.5 us
    ppermute x62 -> x63, waiting for transfers between devices: 140 us -> 150 us  [permute(): return rows_major(lax.ppermute(rows_major(x), axis, pairs)).reshape(shape)]
    concatenate x11, local copies, waits for them, and re-layouts: 0.28 us -> 6.48 us  [body(): jnp.concatenate([attn_gain, attn_shift, bias_query, bias_value, bias_out,...]
    ppermute x62 -> x63, starting transfers between devices: 58.4 us -> 62.6 us  [permute(): return rows_major(lax.ppermute(rows_major(x), axis, pairs)).reshape(shape)]
  transfers between devices with their start and end apart: 65 -> 66, of which waited for: 34 -> 31; matrix products, arithmetic and copies ran while one was open for 29% -> 27% of each run, Pallas kernels for 13% -> 14%
where the time goes in v4:
time: 495 us; the launch traced here: 487 us
  waiting for transfers between devices  150 us (30%)
  Pallas kernels  81.2 us (16%)
  local copies, waits for them, and re-layouts  80 us (16%)
  starting transfers between devices  62.7 us (13%)
  matrix products  49.3 us (10%)
  other arithmetic  48 us (10%)
  between operations  15.5 us (3%)
    ppermute x63, waiting for transfers between devices, permute(): return rows_major(lax.ppermute(rows_major(x), axis, pairs)).reshape(shape)  150 us
    ppermute x63, starting transfers between devices, permute(): return rows_major(lax.ppermute(rows_major(x), axis, pairs)).reshape(shape)  62.6 us
    unnamed x194, local copies, waits for them, and re-layouts  28.5 us
    pallas_call x1, Pallas kernels, attend_backward(): pl.pallas_call(attend_backward_kernel, grid=((HEADS + 1) // 2,), out_shap...  21.8 us
    pallas_call x4, Pallas kernels, weight_grad(): pl.pallas_call(functools.partial(weight_grad_kernel, len(rights) // 2, fi...  20.2 us
    pallas_call x4, Pallas kernels, assemble(): pl.pallas_call(functools.partial(assemble_kernel, spots), out_shape=jax.S...  16.1 us
    pallas_call x1, Pallas kernels, attend_forward(): pl.pallas_call(attend_forward_kernel, grid=((HEADS + 1) // 2,), out_shape...  15 us
  transfers between devices with their start and end apart: 66, of which 31 were waited for; matrix products, arithmetic and copies ran while one was open for 27% of the time, Pallas kernels for 14%

profile of v4, /device:TPU:0, one launch (start us, length us, event | category | flops | bytes accessed | tf_op | source)
XLA Modules:
  0.0 486.7 jit_solution(5087643635855723713)
XLA Ops:
  7.2 6.3 %concatenate.82 = bf16[3264]{0:T(1024)(128)(2,1)S(1)} concatenate(bf16[272]{0:T(512)(128)(2,1)} %param.18, bf16[272]{0:T(512)(128)(2,1)} %param.19, bf16[272]{0:T(512)(128)(2,1)} %param.21, bf16[272]{0:T(512)(128)(2,1)} %param.22, bf16[272]{0:T(512)(128)(2,1)} %param.24, bf16[272]{0:T(512)(128)(2,1)} %param.25, bf16[272]{0:T(512)(128)(2,1)} %param.26, bf16[1088]{0:T(1024)(128)(2,1)} %param.28, ...), dimensions={0} | concatenate | bytes 13056 | tf_op jit(solution)/shard_map/concatenate | solution.py:478
  16.0 4.0 collective-permute-start
  30.0 15.6 %collective-permute-done.4 = bf16[80,3264]{1,0:T(8,128)(2,1)S(1)} collective-permute-done((bf16[80,3264]{1,0:T(8,128)(2,1)S(1)}, bf16[80,3264]{1,0:T(8,128)(2,1)S(1)}, u32[]{:S(2)}, u32[]{:S(2)}) %collective-permute-start.4) | collective-permute-done | bytes 522272 | tf_op jit(solution)/shard_map/ppermute | solution.py:44
  50.4 7.7 %collective-permute-done.5 = bf16[64,3264]{1,0:T(8,128)(2,1)S(1)} collective-permute-done((bf16[64,3264]{1,0:T(8,128)(2,1)S(1)}, bf16[64,3264]{1,0:T(8,128)(2,1)S(1)}, u32[]{:S(2)}, u32[]{:S(2)}) %collective-permute-start.5) | collective-permute-done | bytes 417824 | tf_op jit(solution)/shard_map/ppermute | solution.py:44
  58.1 1.9 collective-permute-done.6
  60.6 10.5 %collective-permute-done.7 = bf16[64,3264]{1,0:T(8,128)(2,1)S(1)} collective-permute-done((bf16[64,3264]{1,0:T(8,128)(2,1)S(1)}, bf16[64,3264]{1,0:T(8,128)(2,1)S(1)}, u32[]{:S(2)}, u32[]{:S(2)}) %collective-permute-start.7) | collective-permute-done | bytes 417824 | tf_op jit(solution)/shard_map/ppermute | solution.py:44
  71.7 3.4 collective-permute-start.14
  76.4 4.3 collective-permute-done.14
  90.6 4.0 fusion.47
  95.9 3.2 collective-permute-start.10
  99.1 5.7 %shard_map.271 = bf16[1088,3264]{1,0:T(8,128)(2,1)S(1)} custom-call(bf16[272,3264]{1,0:T(8,128)(2,1)} %refs_0_.4, bf16[272,3264]{1,0:T(8,128)(2,1)} %collective-permute-done.3.refs_1_, bf16[272,3264]{1,0:T(8,128)(2,1)S(1)} %constant_dynamic-update-slice_fusion.refs_2_, bf16[272,3264]{1,0:T(8,128)(2,1)} %collective-permute-done.8.refs_3_), custom_call_target="tpu_custom_call" | custom-call | bytes 14204928 | tf_op jit(solution)/shard_map/pallas_call | solution.py:166
  107.5 5.7 %convolution_convert_fusion.k_ref = bf16[1024,1088]{1,0:T(8,128)(2,1)S(1)} fusion(bf16[1088,3264]{1,0:T(8,128)(2,1)S(1)} %shard_map.271, bf16[256,1088]{1,0:T(8,128)(2,1)S(1)} %copy-done.58, bf16[256,1088]{1,0:T(8,128)(2,1)S(1)} %copy-done.57, bf16[256,1088]{1,0:T(8,128)(2,1)S(1)} %copy-done.56, bf16[256,1088]{1,0:T(8,128)(2,1)S(1)} %copy-done.48), kind=kOutput, calls=%fused_computation.7 | convolution fusion | flops 2434334720 | bytes 7094272 | tf_op jit(solution)/shard_map/dot_general | solution.py:548
  113.3 5.4 %add_convert_fusion.v_ref = bf16[1024,1088]{1,0:T(8,128)(2,1)S(1)} fusion(f32[1088]{0:T(1024)S(1)} %add.318, bf16[1088,3264]{1,0:T(8,128)(2,1)S(1)} %shard_map.271, bf16[256,1088]{1,0:T(8,128)(2,1)S(1)} %copy-done.58, bf16[256,1088]{1,0:T(8,128)(2,1)S(1)} %copy-done.57, bf16[256,1088]{1,0:T(8,128)(2,1)S(1)} %copy-done.56, bf16[256,1088]{1,0:T(8,128)(2,1)S(1)} %copy-done.48), kind=kOutput, calls=%fused_computation.2 | convolution fusion | flops 2435448832 | bytes 7102464 | tf_op jit(solution)/shard_map/dot_general | solution.py:549
  118.8 15.0 %shard_map.272 = (bf16[256,1088]{1,0:T(8,128)(2,1)S(1)}, f32[256,1088]{1,0:T(8,128)S(1)}) custom-call(bf16[256,1088]{1,0:T(8,128)(2,1)S(1)} %fusion.4.q_ref, bf16[1024,1088]{1,0:T(8,128)(2,1)S(1)} %convolution_convert_fusion.k_ref, bf16[1024,1088]{1,0:T(8,128)(2,1)S(1)} %add_convert_fusion.v_ref, f32[256,1024]{1,0:T(8,128)S(1)} %copy-done.24), custom_call_target="tpu_custom_call" | custom-call | flops 1140850688 | bytes 6684672 | tf_op jit(solution)/shard_map/pallas_call | solution.py:239
  139.3 16.2 %collective-permute-done.11.x_ref = bf16[272,1088]{1,0:T(8,128)(2,1)S(1)} collective-permute-done((bf16[272,1088]{1,0:T(8,128)(2,1)S(1)}, bf16[272,1088]{1,0:T(8,128)(2,1)S(1)}, u32[]{:S(2)}, u32[]{:S(2)}) %collective-permute-start.11) | collective-permute-done | bytes 591904 | tf_op jit(solution)/shard_map/ppermute | solution.py:44
  156.9 2.1 collective-permute-done.12.refs_3_
  160.1 1.9 shard_map.276
  167.8 3.8 shard_map.279
  171.6 4.2 slice_bitcast_fusion.9
  176.2 3.2 multiply_convert_fusion.1
  179.4 4.7 shard_map.280
  184.2 9.1 %convert_reduce_fusion = (f32[4352]{0:T(1024)}, bf16[256,4352]{1,0:T(8,128)(2,1)}) fusion(f32[256,4352]{1,0:T(8,128)S(1)} %get-tuple-element.211, bf16[4352,1088]{1,0:T(8,128)(2,1)S(1)} %shard_map.280, bf16[1,256,1088]{1,2,0:T(8,128)(2,1)S(1)} %copy-done.59), kind=kOutput, calls=%fused_computation.3 | convolution fusion | flops 2437672704 | bytes 16729088 | tf_op jit(solution)/shard_map/dot_general | solution.py:590
  202.5 4.9 shard_map.281.refs_5_
  207.3 7.2 %shard_map.282 = bf16[16,2,2,72,1088]{4,3,2,1,0:T(8,128)(2,1)} custom-call(bf16[2,256,272]{2,1,0:T(8,128)(2,1)S(1)} %get-tuple-element.142.refs_0_, bf16[2,256,272]{2,1,0:T(8,128)(2,1)S(1)} %bitcast.369, bf16[256,4352]{1,0:T(8,128)(2,1)} %get-tuple-element.216.refs_2_, ...), custom_call_target="tpu_custom_call", output_to_operand_aliasing={{}: (5, {})} | custom-call | flops 2424307712 | bytes 10079232 | tf_op jit(solution)/shard_map/pallas_call | solution.py:318
  214.6 8.6 %fusion.83 = (f32[1088]{0:T(1024)}, f32[256,1088]{0,1:T(8,128)}) fusion(bf16[256,4352]{1,0:T(8,128)(2,1)} %get-tuple-element.216.refs_2_, bf16[1088,4352]{1,0:T(8,128)(2,1)} %copy-done.3), kind=kOutput, calls=%fused_computation.296 | convolution fusion | flops 2424585216 | bytes 12816640 | tf_op jit(solution)/shard_map/dot_general | solution.py:603
  223.2 2.7 copy.116
  226.0 2.3 multiply_reduce_fusion
  240.9 21.8 %shard_map.284 = (bf16[256,1088]{1,0:T(8,128)(2,1)S(1)}, bf16[2,2,256,1088]{3,2,1,0:T(8,128)(2,1)S(1)}, bf16[2,2,256,1088]{3,2,1,0:T(8,128)(2,1)}) custom-call(bf16[256,1088]{1,0:T(8,128)(2,1)S(1)} %copy-done.33, bf16[1024,1088]{1,0:T(8,128)(2,1)S(1)} %copy-done.27, bf16[1024,1088]{1,0:T(8,128)(2,1)S(1)} %copy-done.29, f32[256,1024]{1,0:T(8,128)S(1)} %copy-done.25, ...), custom_call_target="tpu_custom_call" | custom-call | flops 2852126720 | bytes 13369344 | tf_op jit(solution)/shard_map/pallas_call | solution.py:266
  266.0 3.8 collective-permute-done.22
  269.8 2.6 fusion.5
  276.3 3.1 shard_map.285.refs_9_
  280.8 2.4 slice.552
  283.2 19.1 %collective-permute-done.23 = bf16[8,64,1088]{2,1,0:T(8,128)(2,1)} collective-permute-done((bf16[8,64,1088]{2,1,0:T(8,128)(2,1)}, bf16[8,64,1088]{2,1,0:T(8,128)(2,1)}, u32[]{:S(2)}, u32[]{:S(2)}) %collective-permute-start.23) | collective-permute-done | bytes 1114144 | tf_op jit(solution)/shard_map/ppermute | solution.py:44
  303.1 2.6 fusion.7
  305.7 4.1 fusion.11
  311.1 2.2 fusion.74
  313.3 2.0 broadcast_select_fusion.9
  316.1 3.3 collective-permute-start.48
  321.7 11.8 %collective-permute-done.48.x_ref = bf16[144,1088]{1,0:T(8,128)(2,1)S(1)} collective-permute-done((bf16[144,1088]{1,0:T(8,128)(2,1)S(1)}, bf16[144,1088]{1,0:T(8,128)(2,1)S(1)}, u32[]{:S(2)}, u32[]{:S(2)}) %collective-permute-start.48) | collective-permute-done | bytes 313376 | tf_op jit(solution)/shard_map/ppermute | solution.py:44
  334.2 2.0 add_convert_fusion.2
  336.4 2.5 fusion.79
  342.2 5.1 %shard_map.289 = bf16[16,1,2,72,1088]{4,3,2,1,0:T(8,128)(2,1)} custom-call(bf16[2,256,272]{2,1,0:T(8,128)(2,1)S(1)} %get-tuple-element.137.refs_0_, bf16[2,256,272]{2,1,0:T(8,128)(2,1)} %bitcast.84.done_ref.refs_1_, bf16[256,1088]{1,0:T(8,128)(2,1)S(1)} %copy-done.8, bf16[256,1088]{1,0:T(8,128)(2,1)S(1)} %bitcast.362, ...), custom_call_target="tpu_custom_call", output_to_operand_aliasing={{}: (9, {})} | custom-call | flops 1818230784 | bytes 7711744 | tf_op jit(solution)/shard_map/pallas_call | solution.py:318
  349.5 2.4 collective-permute-start.33
  353.3 2.1 collective-permute-start.38
  357.1 6.0 %collective-permute-done.31 = bf16[2,72,1088]{2,1,0:T(8,128)(2,1)S(1)} collective-permute-done((bf16[2,72,1088]{2,1,0:T(8,128)(2,1)S(1)}, bf16[2,72,1088]{2,1,0:T(8,128)(2,1)S(1)}, u32[]{:S(2)}, u32[]{:S(2)}) %collective-permute-start.31) | collective-permute-done | bytes 313376 | tf_op jit(solution)/shard_map/ppermute | solution.py:44
  363.1 2.5 collective-permute-done.38
  367.5 3.0 collective-permute-start.41
  373.7 7.0 %fusion.3 = f32[1,256,1088]{2,1,0:T(8,128)S(1)} fusion(f32[256,1088]{1,0:T(8,128)S(1)} %copy-done.41, bf16[256,4352]{1,0:T(8,128)(2,1)S(1)} %copy-done.54, bf16[4352,1088]{1,0:T(8,128)(2,1)} %copy-done.2, f32[1088]{0:T(1024)S(1)} %add.344), kind=kOutput, calls=%fused_computation.15 | convolution fusion | flops 2424864768 | bytes 13930752 | tf_op jit(solution)/shard_map/dot_general | solution.py:572
  382.1 17.3 %collective-permute-done.41 = bf16[4,72,1088]{2,1,0:T(8,128)(2,1)} collective-permute-done((bf16[4,72,1088]{2,1,0:T(8,128)(2,1)S(1)}, bf16[4,72,1088]{2,1,0:T(8,128)(2,1)}, u32[]{:S(2)}, u32[]{:S(2)}) %collective-permute-start.41) | collective-permute-done | bytes 626720 | tf_op jit(solution)/shard_map/ppermute | solution.py:44
  399.4 2.7 collective-permute-done.34
  402.0 2.3 collective-permute-done.32
  404.3 2.1 collective-permute-done.39
  406.4 2.6 fusion.29
  414.4 2.1 collective-permute-done.42
  419.8 3.3 collective-permute-done.36
  441.7 3.0 slice_bitcast_fusion
  444.6 2.6 shard_map.294
  448.6 2.8 shard_map.292
  453.1 2.2 collective-permute-start.55
  455.3 2.3 collective-permute-start.54
  457.6 4.9 %collective-permute-done.59 = bf16[40,1088]{1,0:T(8,128)(2,1)S(1)} collective-permute-done((bf16[40,1088]{1,0:T(8,128)(2,1)S(1)}, bf16[40,1088]{1,0:T(8,128)(2,1)S(1)}, u32[]{:S(2)}, u32[]{:S(2)}) %collective-permute-start.59) | collective-permute-done | bytes 87072 | tf_op jit(solution)/shard_map/ppermute | solution.py:44
  462.7 3.3 collective-permute-start.61
  472.0 3.2 collective-permute-done.60
  477.4 2.6 shard_map.296
  (473 shorter events, 137.0 us)
Async XLA Ops:
  7.2 129.7 %all-gather.3.cloned.1.call-start = ((), (), s32[]{:S(2)}) async-start(), calls=%async_computation.1 | async-start | bytes 4734976 | tf_op jit(solution)/shard_map/all_gather | solution.py:408
  16.0 29.8 %collective-permute-start = (bf16[272,1088]{1,0:T(8,128)(2,1)}, bf16[272,1088]{1,0:T(8,128)(2,1)}, u32[]{:S(2)}, u32[]{:S(2)}) collective-permute-start(bf16[272,1088]{1,0:T(8,128)(2,1)} %fusion.55), channel_id=1, source_target_pairs={{0,2},{2,0},{1,3},{3,1},{4,6},{6,4},{5,7},{7,5},{8,10},{10,8},{9,1... | collective-permute-start | bytes 1775624 | tf_op jit(solution)/shard_map/ppermute | solution.py:44
  19.9 28.1 %collective-permute-start.2 = (bf16[272,1088]{1,0:T(8,128)(2,1)}, bf16[272,1088]{1,0:T(8,128)(2,1)}, u32[]{:S(2)}, u32[]{:S(2)}) collective-permute-start(bf16[272,1088]{1,0:T(8,128)(2,1)} %fusion.55), channel_id=1, source_target_pairs={{0,1},{1,0},{2,3},{3,2},{4,5},{5,4},{6,7},{7,6},{8,9},{9,8},{10,11... | collective-permute-start | bytes 1775624 | tf_op jit(solution)/shard_map/ppermute | solution.py:44
  19.9 79.2 %collective-permute-start.3 = (bf16[272,3264]{1,0:T(8,128)(2,1)}, bf16[272,3264]{1,0:T(8,128)(2,1)}, u32[]{:S(2)}, u32[]{:S(2)}) collective-permute-start(bf16[272,3264]{1,0:T(8,128)(2,1)} %refs_0_.4), channel_id=1, source_target_pairs={{0,1},{1,0},{2,3},{3,2},{4,5},{5,4},{6,7},{7,6},{8,9},{9,8},{10,11... | collective-permute-start | bytes 5326856 | tf_op jit(solution)/shard_map/ppermute | solution.py:44
  22.4 23.2 %collective-permute-start.4 = (bf16[80,3264]{1,0:T(8,128)(2,1)S(1)}, bf16[80,3264]{1,0:T(8,128)(2,1)S(1)}, u32[]{:S(2)}, u32[]{:S(2)}) collective-permute-start(bf16[80,3264]{1,0:T(8,128)(2,1)S(1)} %pad_maximum_fusion.11), channel_id=1, source_target_pairs={{0,6},{6,0},{2,4},{4,2},{1,7},{7,1},{3,5},{5,3},{8,14},{14,8},{10,... | collective-permute-start | bytes 1566728 | tf_op jit(solution)/shard_map/ppermute | solution.py:44
  23.2 133.7 %collective-permute-start.9 = (bf16[272,1088]{1,0:T(8,128)(2,1)S(1)}, bf16[272,1088]{1,0:T(8,128)(2,1)}, u32[]{:S(2)}, u32[]{:S(2)}) collective-permute-start(bf16[272,1088]{1,0:T(8,128)(2,1)S(1)} %copy-done.13), channel_id=1, source_target_pairs={{0,1},{1,0},{2,3},{3,2},{4,5},{5,4},{6,7},{7,6},{8,9},{9,8},{10,11... | collective-permute-start | bytes 1775624 | tf_op jit(solution)/shard_map/ppermute | solution.py:44
  45.7 122.1 %collective-permute-start.13 = (bf16[272,4352]{1,0:T(8,128)(2,1)}, bf16[272,4352]{1,0:T(8,128)(2,1)}, u32[]{:S(2)}, u32[]{:S(2)}) collective-permute-start(bf16[272,4352]{1,0:T(8,128)(2,1)} %refs_0_.6), channel_id=1, source_target_pairs={{0,1},{1,0},{2,3},{3,2},{4,5},{5,4},{6,7},{7,6},{8,9},{9,8},{10,11... | collective-permute-start | bytes 7102472 | tf_op jit(solution)/shard_map/ppermute | solution.py:44
  45.8 12.3 %collective-permute-start.5 = (bf16[64,3264]{1,0:T(8,128)(2,1)S(1)}, bf16[64,3264]{1,0:T(8,128)(2,1)S(1)}, u32[]{:S(2)}, u32[]{:S(2)}) collective-permute-start(bf16[64,3264]{1,0:T(8,128)(2,1)S(1)} %slice.506), channel_id=1, source_target_pairs={{0,8},{8,0},{16,24},{24,16},{1,9},{9,1},{17,25},{25,17},{2,10},{10... | collective-permute-start | bytes 1253384 | tf_op jit(solution)/shard_map/ppermute | solution.py:44
  48.1 11.9 %collective-permute-start.6 = (bf16[64,3264]{1,0:T(8,128)(2,1)S(1)}, bf16[64,3264]{1,0:T(8,128)(2,1)S(1)}, u32[]{:S(2)}, u32[]{:S(2)}) collective-permute-start(bf16[64,3264]{1,0:T(8,128)(2,1)S(1)} %slice.506), channel_id=1, source_target_pairs={{0,32},{32,0},{64,96},{96,64},{1,33},{33,1},{65,97},{97,65},{2,34}... | collective-permute-start | bytes 1253384 | tf_op jit(solution)/shard_map/ppermute | solution.py:44
  58.1 121.3 %collective-permute-start.17 = (bf16[1088,1088]{1,0:T(8,128)(2,1)}, bf16[1088,1088]{1,0:T(8,128)(2,1)}, u32[]{:S(2)}, u32[]{:S(2)}) collective-permute-start(bf16[1088,1088]{1,0:T(8,128)(2,1)} %refs_0_.7), channel_id=1, source_target_pairs={{0,1},{1,0},{2,3},{3,2},{4,5},{5,4},{6,7},{7,6},{8,9},{9,8},{10,11... | collective-permute-start | bytes 7102472 | tf_op jit(solution)/shard_map/ppermute | solution.py:44
  60.0 11.1 %collective-permute-start.7 = (bf16[64,3264]{1,0:T(8,128)(2,1)S(1)}, bf16[64,3264]{1,0:T(8,128)(2,1)S(1)}, u32[]{:S(2)}, u32[]{:S(2)}) collective-permute-start(bf16[64,3264]{1,0:T(8,128)(2,1)S(1)} %collective-permute-done.6), channel_id=1, source_target_pairs={{0,8},{8,0},{16,24},{24,16},{1,9},{9,1},{17,25},{25,17},{2,10},{10... | collective-permute-start | bytes 1253384 | tf_op jit(solution)/shard_map/ppermute | solution.py:44
  71.7 8.9 %collective-permute-start.14 = (bf16[32,4352]{1,0:T(8,128)(2,1)}, bf16[32,4352]{1,0:T(8,128)(2,1)S(1)}, u32[]{:S(2)}, u32[]{:S(2)}) collective-permute-start(bf16[32,4352]{1,0:T(8,128)(2,1)} %shard_map.277), channel_id=1, source_target_pairs={{0,6},{6,0},{2,4},{4,2},{1,7},{7,1},{3,5},{5,3},{8,14},{14,8},{10,... | collective-permute-start | bytes 835592 | tf_op jit(solution)/shard_map/ppermute | solution.py:44
  80.6 5.0 %collective-permute-start.1 = (bf16[272,1088]{1,0:T(8,128)(2,1)}, bf16[272,1088]{1,0:T(8,128)(2,1)}, u32[]{:S(2)}, u32[]{:S(2)}) collective-permute-start(bf16[272,1088]{1,0:T(8,128)(2,1)} %collective-permute-done), channel_id=1, source_target_pairs={{0,1},{1,0},{2,3},{3,2},{4,5},{5,4},{6,7},{7,6},{8,9},{9,8},{10,11... | collective-permute-start | bytes 1775624 | tf_op jit(solution)/shard_map/ppermute | solution.py:44
  81.3 232.0 %reduce-scatter.2.cloned.1.call-start = ((), (), s32[]{:S(2)}) async-start(), calls=%async_computation.2 | async-start | bytes 11280384 | tf_op jit(solution)/shard_map/reduce_scatter | solution.py:599
  86.5 8.1 %collective-permute-start.8 = (bf16[272,3264]{1,0:T(8,128)(2,1)S(1)}, bf16[272,3264]{1,0:T(8,128)(2,1)}, u32[]{:S(2)}, u32[]{:S(2)}) collective-permute-start(bf16[272,3264]{1,0:T(8,128)(2,1)S(1)} %constant_dynamic-update-slice_fusion.refs_2_), channel_id=1, source_target_pairs={{0,1},{1,0},{2,3},{3,2},{4,5},{5,4},{6,7},{7,6},{8,9},{9,8},{10,11... | collective-permute-start | bytes 5326856 | tf_op jit(solution)/shard_map/ppermute | solution.py:44
  95.9 40.3 %collective-permute-start.10 = (bf16[32,4352]{1,0:T(8,128)(2,1)}, bf16[32,4352]{1,0:T(8,128)(2,1)S(1)}, u32[]{:S(2)}, u32[]{:S(2)}) collective-permute-start(bf16[32,4352]{1,0:T(8,128)(2,1)} %shard_map.273), channel_id=1, source_target_pairs={{0,6},{6,0},{2,4},{4,2},{1,7},{7,1},{3,5},{5,3},{8,14},{14,8},{10,... | collective-permute-start | bytes 835592 | tf_op jit(solution)/shard_map/ppermute | solution.py:44
  136.9 29.0 %collective-permute-start.15 = (bf16[512,4352]{1,0:T(8,128)(2,1)}, bf16[512,4352]{1,0:T(8,128)(2,1)}, u32[]{:S(2)}, u32[]{:S(2)}) collective-permute-start(bf16[512,4352]{1,0:T(8,128)(2,1)} %shard_map.278), channel_id=1, source_target_pairs={{0,1},{1,0},{2,3},{3,2},{4,5},{5,4},{6,7},{7,6},{8,9},{9,8},{10,11... | collective-permute-start | bytes 13369352 | tf_op jit(solution)/shard_map/ppermute | solution.py:44
  138.0 17.5 %collective-permute-start.11 = (bf16[272,1088]{1,0:T(8,128)(2,1)S(1)}, bf16[272,1088]{1,0:T(8,128)(2,1)S(1)}, u32[]{:S(2)}, u32[]{:S(2)}) collective-permute-start(bf16[272,1088]{1,0:T(8,128)(2,1)S(1)} %copy-done.52), channel_id=1, source_target_pairs={{0,6},{6,0},{2,4},{4,2},{1,7},{7,1},{3,5},{5,3},{8,14},{14,8},{10,... | collective-permute-start | bytes 1775624 | tf_op jit(solution)/shard_map/ppermute | solution.py:44
  156.3 2.8 collective-permute-start.12
  193.3 14.0 %collective-permute-start.19 = (bf16[256,4352]{1,0:T(8,128)(2,1)}, bf16[256,4352]{1,0:T(8,128)(2,1)}, u32[]{:S(2)}, u32[]{:S(2)}) collective-permute-start(bf16[256,4352]{1,0:T(8,128)(2,1)} %get-tuple-element.216.refs_2_), channel_id=1, source_target_pairs={{0,1},{1,0},{2,3},{3,2},{4,5},{5,4},{6,7},{7,6},{8,9},{9,8},{10,11... | collective-permute-start | bytes 6684680 | tf_op jit(solution)/shard_map/ppermute | solution.py:44
  195.6 4.6 collective-permute-start.20
  197.3 2.8 collective-permute-start.21
  199.2 8.1 %collective-permute-start.18 = (bf16[8,64,272]{2,1,0:T(8,128)(2,1)S(1)}, bf16[8,64,272]{2,1,0:T(8,128)(2,1)S(1)}, u32[]{:S(2)}, u32[]{:S(2)}) collective-permute-start(bf16[8,64,272]{2,1,0:T(8,128)(2,1)S(1)} %bitcast.390), channel_id=1, source_target_pairs={{0,1},{1,0},{2,3},{3,2},{4,5},{5,4},{6,7},{7,6},{8,9},{9,8},{10,11... | collective-permute-start | bytes 835592 | tf_op jit(solution)/shard_map/ppermute | solution.py:44
  214.6 218.7 %all-gather.5.cloned.1.call-start = ((), (), s32[]{:S(2)}) async-start(), calls=%async_computation.3 | async-start | bytes 5640192 | tf_op jit(solution)/shard_map/all_gather | solution.py:686
  264.1 5.7 %collective-permute-start.22 = (bf16[16,64,1088]{2,1,0:T(8,128)(2,1)}, bf16[16,64,1088]{2,1,0:T(8,128)(2,1)}, u32[]{:S(2)}, u32[]{:S(2)}) collective-permute-start(bf16[16,64,1088]{2,1,0:T(8,128)(2,1)} %bitcast.63), channel_id=1, source_target_pairs={{0,1},{1,0},{2,3},{3,2},{4,5},{5,4},{6,7},{7,6},{8,9},{9,8},{10,11... | collective-permute-start | bytes 6684680 | tf_op jit(solution)/shard_map/ppermute | solution.py:44
  264.2 12.0 %collective-permute-start.25 = (bf16[4,64,1088]{2,1,0:T(8,128)(2,1)S(1)}, bf16[4,64,1088]{2,1,0:T(8,128)(2,1)}, u32[]{:S(2)}, u32[]{:S(2)}) collective-permute-start(bf16[4,64,1088]{2,1,0:T(8,128)(2,1)S(1)} %bitcast.360), channel_id=1, source_target_pairs={{0,1},{1,0},{2,3},{3,2},{4,5},{5,4},{6,7},{7,6},{8,9},{9,8},{10,11... | collective-permute-start | bytes 1671176 | tf_op jit(solution)/shard_map/ppermute | solution.py:44
  272.4 29.8 %collective-permute-start.23 = (bf16[8,64,1088]{2,1,0:T(8,128)(2,1)}, bf16[8,64,1088]{2,1,0:T(8,128)(2,1)}, u32[]{:S(2)}, u32[]{:S(2)}) collective-permute-start(bf16[8,64,1088]{2,1,0:T(8,128)(2,1)} %fusion.5), channel_id=1, source_target_pairs={{0,2},{2,0},{1,3},{3,1},{4,6},{6,4},{5,7},{7,5},{8,10},{10,8},{9,1... | collective-permute-start | bytes 3342344 | tf_op jit(solution)/shard_map/ppermute | solution.py:44
  273.6 2.6 collective-permute-start.24
  273.8 28.5 %collective-permute-start.26 = (bf16[4,64,1088]{2,1,0:T(8,128)(2,1)S(1)}, bf16[4,64,1088]{2,1,0:T(8,128)(2,1)S(1)}, u32[]{:S(2)}, u32[]{:S(2)}) collective-permute-start(bf16[4,64,1088]{2,1,0:T(8,128)(2,1)S(1)} %bitcast.358), channel_id=1, source_target_pairs={{0,1},{1,0},{2,3},{3,2},{4,5},{5,4},{6,7},{7,6},{8,9},{9,8},{10,11... | collective-permute-start | bytes 1671176 | tf_op jit(solution)/shard_map/ppermute | solution.py:44
  275.7 27.4 %collective-permute-start.27 = (bf16[8,64,272]{2,1,0:T(8,128)(2,1)}, bf16[8,64,272]{2,1,0:T(8,128)(2,1)}, u32[]{:S(2)}, u32[]{:S(2)}) collective-permute-start(bf16[8,64,272]{2,1,0:T(8,128)(2,1)} %bitcast.83), channel_id=1, source_target_pairs={{0,1},{1,0},{2,3},{3,2},{4,5},{5,4},{6,7},{7,6},{8,9},{9,8},{10,11... | collective-permute-start | bytes 835592 | tf_op jit(solution)/shard_map/ppermute | solution.py:44
  315.3 18.9 %collective-permute-start.49 = (bf16[144,1088]{1,0:T(8,128)(2,1)}, bf16[144,1088]{1,0:T(8,128)(2,1)S(1)}, u32[]{:S(2)}, u32[]{:S(2)}) collective-permute-start(bf16[144,1088]{1,0:T(8,128)(2,1)} %bitcast.120), channel_id=1, source_target_pairs={{0,6},{6,0},{2,4},{4,2},{1,7},{7,1},{3,5},{5,3},{8,14},{14,8},{10,... | collective-permute-start | bytes 940040 | tf_op jit(solution)/shard_map/ppermute | solution.py:44
  316.1 18.1 %collective-permute-start.50 = (bf16[144,1088]{1,0:T(8,128)(2,1)}, bf16[144,1088]{1,0:T(8,128)(2,1)}, u32[]{:S(2)}, u32[]{:S(2)}) collective-permute-start(bf16[144,1088]{1,0:T(8,128)(2,1)} %bitcast.120), channel_id=1, source_target_pairs={{0,2},{2,0},{1,3},{3,1},{4,6},{6,4},{5,7},{7,5},{8,10},{10,8},{9,1... | collective-permute-start | bytes 940040 | tf_op jit(solution)/shard_map/ppermute | solution.py:44
  316.1 17.4 %collective-permute-start.48 = (bf16[144,1088]{1,0:T(8,128)(2,1)S(1)}, bf16[144,1088]{1,0:T(8,128)(2,1)S(1)}, u32[]{:S(2)}, u32[]{:S(2)}) collective-permute-start(bf16[144,1088]{1,0:T(8,128)(2,1)S(1)} %bitcast.388), channel_id=1, source_target_pairs={{0,4},{4,0},{1,5},{5,1},{2,6},{6,2},{3,7},{7,3},{8,12},{12,8},{9,1... | collective-permute-start | bytes 940040 | tf_op jit(solution)/shard_map/ppermute | solution.py:44
  336.3 3.1 collective-permute-start.30
  339.3 2.8 collective-permute-start.28
  348.6 14.5 %collective-permute-start.31 = (bf16[2,72,1088]{2,1,0:T(8,128)(2,1)S(1)}, bf16[2,72,1088]{2,1,0:T(8,128)(2,1)S(1)}, u32[]{:S(2)}, u32[]{:S(2)}) collective-permute-start(bf16[2,72,1088]{2,1,0:T(8,128)(2,1)S(1)} %get-tuple-element.99), channel_id=1, source_target_pairs={{0,8},{8,16},{16,24},{24,0},{1,9},{9,17},{17,25},{25,1},{2,10},{10... | collective-permute-start | bytes 940040 | tf_op jit(solution)/shard_map/ppermute | solution.py:44
  349.5 13.5 %collective-permute-start.33 = (bf16[2,72,1088]{2,1,0:T(8,128)(2,1)S(1)}, bf16[2,72,1088]{2,1,0:T(8,128)(2,1)S(1)}, u32[]{:S(2)}, u32[]{:S(2)}) collective-permute-start(bf16[2,72,1088]{2,1,0:T(8,128)(2,1)S(1)} %get-tuple-element.101), channel_id=1, source_target_pairs={{0,24},{8,0},{16,8},{24,16},{1,25},{9,1},{17,9},{25,17},{2,26},{10... | collective-permute-start | bytes 940040 | tf_op jit(solution)/shard_map/ppermute | solution.py:44
  353.3 12.2 %collective-permute-start.38 = (bf16[2,72,1088]{2,1,0:T(8,128)(2,1)S(1)}, bf16[2,72,1088]{2,1,0:T(8,128)(2,1)}, u32[]{:S(2)}, u32[]{:S(2)}) collective-permute-start(bf16[2,72,1088]{2,1,0:T(8,128)(2,1)S(1)} %get-tuple-element.95), channel_id=1, source_target_pairs={{0,32},{32,64},{64,96},{96,0},{1,33},{33,65},{65,97},{97,1},{2,34}... | collective-permute-start | bytes 940040 | tf_op jit(solution)/shard_map/ppermute | solution.py:44
  355.4 10.2 %collective-permute-start.40 = (bf16[2,72,1088]{2,1,0:T(8,128)(2,1)S(1)}, bf16[2,72,1088]{2,1,0:T(8,128)(2,1)}, u32[]{:S(2)}, u32[]{:S(2)}) collective-permute-start(bf16[2,72,1088]{2,1,0:T(8,128)(2,1)S(1)} %get-tuple-element.98), channel_id=1, source_target_pairs={{0,96},{32,0},{64,32},{96,64},{1,97},{33,1},{65,33},{97,65},{2,98}... | collective-permute-start | bytes 940040 | tf_op jit(solution)/shard_map/ppermute | solution.py:44
  367.5 31.9 %collective-permute-start.41 = (bf16[4,72,1088]{2,1,0:T(8,128)(2,1)S(1)}, bf16[4,72,1088]{2,1,0:T(8,128)(2,1)}, u32[]{:S(2)}, u32[]{:S(2)}) collective-permute-start(bf16[4,72,1088]{2,1,0:T(8,128)(2,1)S(1)} %pad_maximum_fusion.10), channel_id=1, source_target_pairs={{0,96},{32,0},{64,32},{96,64},{1,97},{33,1},{65,33},{97,65},{2,98}... | collective-permute-start | bytes 1880072 | tf_op jit(solution)/shard_map/ppermute | solution.py:44
  370.5 31.5 %collective-permute-start.34 = (bf16[4,72,1088]{2,1,0:T(8,128)(2,1)S(1)}, bf16[4,72,1088]{2,1,0:T(8,128)(2,1)}, u32[]{:S(2)}, u32[]{:S(2)}) collective-permute-start(bf16[4,72,1088]{2,1,0:T(8,128)(2,1)S(1)} %pad_maximum_fusion.8), channel_id=1, source_target_pairs={{0,24},{8,0},{16,8},{24,16},{1,25},{9,1},{17,9},{25,17},{2,26},{10... | collective-permute-start | bytes 1880072 | tf_op jit(solution)/shard_map/ppermute | solution.py:44
  371.6 32.7 %collective-permute-start.32 = (bf16[4,72,1088]{2,1,0:T(8,128)(2,1)S(1)}, bf16[4,72,1088]{2,1,0:T(8,128)(2,1)}, u32[]{:S(2)}, u32[]{:S(2)}) collective-permute-start(bf16[4,72,1088]{2,1,0:T(8,128)(2,1)S(1)} %pad_maximum_fusion.7), channel_id=1, source_target_pairs={{0,8},{8,16},{16,24},{24,0},{1,9},{9,17},{17,25},{25,1},{2,10},{10... | collective-permute-start | bytes 1880072 | tf_op jit(solution)/shard_map/ppermute | solution.py:44
  373.7 32.7 %collective-permute-start.39 = (bf16[4,72,1088]{2,1,0:T(8,128)(2,1)}, bf16[4,72,1088]{2,1,0:T(8,128)(2,1)}, u32[]{:S(2)}, u32[]{:S(2)}) collective-permute-start(bf16[4,72,1088]{2,1,0:T(8,128)(2,1)} %pad_maximum_fusion.9), channel_id=1, source_target_pairs={{0,32},{32,64},{64,96},{96,0},{1,33},{33,65},{65,97},{97,1},{2,34}... | collective-permute-start | bytes 1880072 | tf_op jit(solution)/shard_map/ppermute | solution.py:44
  409.1 7.4 %collective-permute-start.42 = (bf16[72,1088]{1,0:T(8,128)(2,1)S(1)}, bf16[72,1088]{1,0:T(8,128)(2,1)S(1)}, u32[]{:S(2)}, u32[]{:S(2)}) collective-permute-start(bf16[72,1088]{1,0:T(8,128)(2,1)S(1)} %get-tuple-element.145), channel_id=1, source_target_pairs={{0,16},{8,24},{16,0},{24,8},{1,17},{9,25},{17,1},{25,9},{2,18},{10... | collective-permute-start | bytes 470024 | tf_op jit(solution)/shard_map/ppermute | solution.py:44
  410.6 7.2 %collective-permute-start.44 = (bf16[72,1088]{1,0:T(8,128)(2,1)S(1)}, bf16[72,1088]{1,0:T(8,128)(2,1)S(1)}, u32[]{:S(2)}, u32[]{:S(2)}) collective-permute-start(bf16[72,1088]{1,0:T(8,128)(2,1)S(1)} %get-tuple-element.146), channel_id=1, source_target_pairs={{0,24},{8,0},{16,8},{24,16},{1,25},{9,1},{17,9},{25,17},{2,26},{10... | collective-permute-start | bytes 470024 | tf_op jit(solution)/shard_map/ppermute | solution.py:44
  411.9 6.7 %collective-permute-start.43 = (bf16[72,1088]{1,0:T(8,128)(2,1)S(1)}, bf16[72,1088]{1,0:T(8,128)(2,1)S(1)}, u32[]{:S(2)}, u32[]{:S(2)}) collective-permute-start(bf16[72,1088]{1,0:T(8,128)(2,1)S(1)} %get-tuple-element.147), channel_id=1, source_target_pairs={{0,8},{8,16},{16,24},{24,0},{1,9},{9,17},{17,25},{25,1},{2,10},{10... | collective-permute-start | bytes 470024 | tf_op jit(solution)/shard_map/ppermute | solution.py:44
  412.7 7.0 %collective-permute-start.35 = (bf16[72,1088]{1,0:T(8,128)(2,1)S(1)}, bf16[72,1088]{1,0:T(8,128)(2,1)S(1)}, u32[]{:S(2)}, u32[]{:S(2)}) collective-permute-start(bf16[72,1088]{1,0:T(8,128)(2,1)S(1)} %get-tuple-element.148), channel_id=1, source_target_pairs={{0,64},{32,96},{64,0},{96,32},{1,65},{33,97},{65,1},{97,33},{2,66}... | collective-permute-start | bytes 470024 | tf_op jit(solution)/shard_map/ppermute | solution.py:44
  412.8 6.9 %collective-permute-start.37 = (bf16[72,1088]{1,0:T(8,128)(2,1)S(1)}, bf16[72,1088]{1,0:T(8,128)(2,1)S(1)}, u32[]{:S(2)}, u32[]{:S(2)}) collective-permute-start(bf16[72,1088]{1,0:T(8,128)(2,1)S(1)} %get-tuple-element.149), channel_id=1, source_target_pairs={{0,96},{32,0},{64,32},{96,64},{1,97},{33,1},{65,33},{97,65},{2,98}... | collective-permute-start | bytes 470024 | tf_op jit(solution)/shard_map/ppermute | solution.py:44
  416.5 6.6 %collective-permute-start.36 = (bf16[72,1088]{1,0:T(8,128)(2,1)S(1)}, bf16[72,1088]{1,0:T(8,128)(2,1)S(1)}, u32[]{:S(2)}, u32[]{:S(2)}) collective-permute-start(bf16[72,1088]{1,0:T(8,128)(2,1)S(1)} %get-tuple-element.150), channel_id=1, source_target_pairs={{0,32},{32,64},{64,96},{96,0},{1,33},{33,65},{65,97},{97,1},{2,34}... | collective-permute-start | bytes 470024 | tf_op jit(solution)/shard_map/ppermute | solution.py:44
  423.3 6.6 %collective-permute-start.46 = (bf16[72,1088]{1,0:T(8,128)(2,1)S(1)}, bf16[72,1088]{1,0:T(8,128)(2,1)S(1)}, u32[]{:S(2)}, u32[]{:S(2)}) collective-permute-start(bf16[72,1088]{1,0:T(8,128)(2,1)S(1)} %broadcast_select_fusion.10), channel_id=1, source_target_pairs={{0,6},{6,0},{2,4},{4,2},{1,7},{7,1},{3,5},{5,3},{8,14},{14,8},{10,... | collective-permute-start | bytes 470024 | tf_op jit(solution)/shard_map/ppermute | solution.py:44
  424.9 6.8 %collective-permute-start.47 = (bf16[72,1088]{1,0:T(8,128)(2,1)S(1)}, bf16[72,1088]{1,0:T(8,128)(2,1)S(1)}, u32[]{:S(2)}, u32[]{:S(2)}) collective-permute-start(bf16[72,1088]{1,0:T(8,128)(2,1)S(1)} %broadcast_select_fusion.10), channel_id=1, source_target_pairs={{0,2},{2,0},{1,3},{3,1},{4,6},{6,4},{5,7},{7,5},{8,10},{10,8},{9,1... | collective-permute-start | bytes 470024 | tf_op jit(solution)/shard_map/ppermute | solution.py:44
  425.8 6.7 %collective-permute-start.45 = (bf16[72,1088]{1,0:T(8,128)(2,1)S(1)}, bf16[72,1088]{1,0:T(8,128)(2,1)S(1)}, u32[]{:S(2)}, u32[]{:S(2)}) collective-permute-start(bf16[72,1088]{1,0:T(8,128)(2,1)S(1)} %get-tuple-element.80), channel_id=1, source_target_pairs={{0,4},{4,0},{1,5},{5,1},{2,6},{6,2},{3,7},{7,3},{8,12},{12,8},{9,1... | collective-permute-start | bytes 470024 | tf_op jit(solution)/shard_map/ppermute | solution.py:44
  435.5 17.1 %collective-permute-start.52 = (bf16[32,1088]{1,0:T(8,128)(2,1)S(1)}, bf16[32,1088]{1,0:T(8,128)(2,1)S(1)}, u32[]{:S(2)}, u32[]{:S(2)}) collective-permute-start(bf16[32,1088]{1,0:T(8,128)(2,1)S(1)} %slice.564), channel_id=1, source_target_pairs={{0,64},{32,96},{64,0},{96,32},{1,65},{33,97},{65,1},{97,33},{2,66}... | collective-permute-start | bytes 208904 | tf_op jit(solution)/shard_map/ppermute | solution.py:44
  435.5 17.5 %collective-permute-start.51 = (bf16[32,1088]{1,0:T(8,128)(2,1)S(1)}, bf16[32,1088]{1,0:T(8,128)(2,1)S(1)}, u32[]{:S(2)}, u32[]{:S(2)}) collective-permute-start(bf16[32,1088]{1,0:T(8,128)(2,1)S(1)} %slice.564), channel_id=1, source_target_pairs={{0,96},{32,0},{64,32},{96,64},{1,97},{33,1},{65,33},{97,65},{2,98}... | collective-permute-start | bytes 208904 | tf_op jit(solution)/shard_map/ppermute | solution.py:44
  436.9 16.1 %collective-permute-start.53 = (bf16[32,1088]{1,0:T(8,128)(2,1)S(1)}, bf16[32,1088]{1,0:T(8,128)(2,1)S(1)}, u32[]{:S(2)}, u32[]{:S(2)}) collective-permute-start(bf16[32,1088]{1,0:T(8,128)(2,1)S(1)} %slice.564), channel_id=1, source_target_pairs={{0,32},{32,64},{64,96},{96,0},{1,33},{33,65},{65,97},{97,1},{2,34}... | collective-permute-start | bytes 208904 | tf_op jit(solution)/shard_map/ppermute | solution.py:44
  438.5 19.2 %collective-permute-start.58 = (bf16[40,1088]{1,0:T(8,128)(2,1)S(1)}, bf16[40,1088]{1,0:T(8,128)(2,1)S(1)}, u32[]{:S(2)}, u32[]{:S(2)}) collective-permute-start(bf16[40,1088]{1,0:T(8,128)(2,1)S(1)} %slice.572), channel_id=1, source_target_pairs={{0,16},{8,24},{16,0},{24,8},{1,17},{9,25},{17,1},{25,9},{2,18},{10... | collective-permute-start | bytes 261128 | tf_op jit(solution)/shard_map/ppermute | solution.py:44
  439.9 17.8 %collective-permute-start.57 = (bf16[40,1088]{1,0:T(8,128)(2,1)S(1)}, bf16[40,1088]{1,0:T(8,128)(2,1)S(1)}, u32[]{:S(2)}, u32[]{:S(2)}) collective-permute-start(bf16[40,1088]{1,0:T(8,128)(2,1)S(1)} %slice.572), channel_id=1, source_target_pairs={{0,24},{8,0},{16,8},{24,16},{1,25},{9,1},{17,9},{25,17},{2,26},{10... | collective-permute-start | bytes 261128 | tf_op jit(solution)/shard_map/ppermute | solution.py:44
  452.6 10.0 %collective-permute-start.59 = (bf16[40,1088]{1,0:T(8,128)(2,1)S(1)}, bf16[40,1088]{1,0:T(8,128)(2,1)S(1)}, u32[]{:S(2)}, u32[]{:S(2)}) collective-permute-start(bf16[40,1088]{1,0:T(8,128)(2,1)S(1)} %slice.572), channel_id=1, source_target_pairs={{0,8},{8,16},{16,24},{24,0},{1,9},{9,17},{17,25},{25,1},{2,10},{10... | collective-permute-start | bytes 261128 | tf_op jit(solution)/shard_map/ppermute | solution.py:44
  453.1 13.7 %collective-permute-start.55 = (bf16[4,32,1088]{2,1,0:T(8,128)(2,1)S(1)}, bf16[4,32,1088]{2,1,0:T(8,128)(2,1)S(1)}, u32[]{:S(2)}, u32[]{:S(2)}) collective-permute-start(bf16[4,32,1088]{2,1,0:T(8,128)(2,1)S(1)} %pad_maximum_fusion.21), channel_id=1, source_target_pairs={{0,16},{8,24},{16,0},{24,8},{1,17},{9,25},{17,1},{25,9},{2,18},{10... | collective-permute-start | bytes 835592 | tf_op jit(solution)/shard_map/ppermute | solution.py:44
  455.3 12.8 %collective-permute-start.54 = (bf16[4,32,1088]{2,1,0:T(8,128)(2,1)S(1)}, bf16[4,32,1088]{2,1,0:T(8,128)(2,1)S(1)}, u32[]{:S(2)}, u32[]{:S(2)}) collective-permute-start(bf16[4,32,1088]{2,1,0:T(8,128)(2,1)S(1)} %pad_maximum_fusion.21), channel_id=1, source_target_pairs={{0,24},{8,0},{16,8},{24,16},{1,25},{9,1},{17,9},{25,17},{2,26},{10... | collective-permute-start | bytes 835592 | tf_op jit(solution)/shard_map/ppermute | solution.py:44
  457.6 10.5 %collective-permute-start.56 = (bf16[4,32,1088]{2,1,0:T(8,128)(2,1)S(1)}, bf16[4,32,1088]{2,1,0:T(8,128)(2,1)S(1)}, u32[]{:S(2)}, u32[]{:S(2)}) collective-permute-start(bf16[4,32,1088]{2,1,0:T(8,128)(2,1)S(1)} %pad_maximum_fusion.21), channel_id=1, source_target_pairs={{0,8},{8,16},{16,24},{24,0},{1,9},{9,17},{17,25},{25,1},{2,10},{10... | collective-permute-start | bytes 835592 | tf_op jit(solution)/shard_map/ppermute | solution.py:44
  462.7 9.3 %collective-permute-start.61 = (bf16[4,40,1088]{2,1,0:T(8,128)(2,1)S(1)}, bf16[4,40,1088]{2,1,0:T(8,128)(2,1)S(1)}, u32[]{:S(2)}, u32[]{:S(2)}) collective-permute-start(bf16[4,40,1088]{2,1,0:T(8,128)(2,1)S(1)} %pad_maximum_fusion.20), channel_id=1, source_target_pairs={{0,64},{32,96},{64,0},{96,32},{1,65},{33,97},{65,1},{97,33},{2,66}... | collective-permute-start | bytes 1044488 | tf_op jit(solution)/shard_map/ppermute | solution.py:44
  466.0 9.2 %collective-permute-start.60 = (bf16[4,40,1088]{2,1,0:T(8,128)(2,1)S(1)}, bf16[4,40,1088]{2,1,0:T(8,128)(2,1)S(1)}, u32[]{:S(2)}, u32[]{:S(2)}) collective-permute-start(bf16[4,40,1088]{2,1,0:T(8,128)(2,1)S(1)} %pad_maximum_fusion.20), channel_id=1, source_target_pairs={{0,96},{32,0},{64,32},{96,64},{1,97},{33,1},{65,33},{97,65},{2,98}... | collective-permute-start | bytes 1044488 | tf_op jit(solution)/shard_map/ppermute | solution.py:44
  466.8 8.9 %collective-permute-start.62 = (bf16[4,40,1088]{2,1,0:T(8,128)(2,1)S(1)}, bf16[4,40,1088]{2,1,0:T(8,128)(2,1)S(1)}, u32[]{:S(2)}, u32[]{:S(2)}) collective-permute-start(bf16[4,40,1088]{2,1,0:T(8,128)(2,1)S(1)} %pad_maximum_fusion.20), channel_id=1, source_target_pairs={{0,32},{32,64},{64,96},{96,0},{1,33},{33,65},{65,97},{97,1},{2,34}... | collective-permute-start | bytes 1044488 | tf_op jit(solution)/shard_map/ppermute | solution.py:44
  (95 other events, 596.4 us)
Sparse Core Ops, SparseCore 0:
  81.5 53.7 all-gather.2
  214.7 88.5 reduce-scatter.1
  336.4 71.7 all-gather.4

commit v5 on v4

--- a/solution.py
+++ b/solution.py
@@ -390,7 +390,7 @@
     mine = got[:64]
     by_x, by_y = swap_pair(mine, "x"), swap_pair(mine, "y")
     last = swap_pair(by_y, "x")
-    return jnp.concatenate([got, by_x, by_y, last])
+    return got, jnp.concatenate([got, by_x, by_y, last])
 
 
 def widened(value):
@@ -491,9 +491,9 @@
     small = jnp.pad(small.reshape(3, D), ((0, 13), (0, 0)))
     rows = block_input.shape[1]
     own_tokens = block_input[0]
-    far_parts = gather_quarters(w_qkv)
+    got_qkv, far_parts = gather_quarters(w_qkv)
     with_small = jnp.concatenate([own_tokens, small])
-    half = swap_half(with_small)
+    half = swap_half(after(with_small, got_qkv))
     token_parts = [with_small, swap_core(with_small), half, swap_core(half)]
     tokens = [part[:rows] for part in token_parts]
     smalls = [part[rows : rows + 3].reshape(-1).astype(F32) for part in token_parts]
@@ -509,7 +509,7 @@
         + tuple((2, row, 2, *turn) for row, *turn in turns)
         + tuple((3, row, 3, *turn) for row, *turn in turns),
     )
-    far_out = after(swap_far(after(w_out, got_rest)), full_qkv)
+    far_out = after(swap_far(after(w_out, half)), full_qkv)
     full_out = assemble(
         QUART,
         (w_out, swap_core(w_out), far_out, swap_core(far_out)),
@@ -660,7 +660,6 @@
     mine = (mine + swap_core(other.astype(BF)).astype(F32)).astype(BF)
     mine = jnp.pad(mine.reshape(2, 12, VECTOR).astype(F32), ((0, 0), (0, 0), (0, D - VECTOR)))
 
-    early = depth_sum(mlp_part.transpose(1, 0, 2, 3).reshape(2, 2 * PAD, D), zh, d_normed)
     grad_attn = weight_grad(normed_pair, rights, mine, 1, 0, 0, grad_attn)
     grad_attn = grad_attn.reshape(4, 4, 2, PAD, D)
 
@@ -681,15 +680,15 @@
     two = ring_scatter_halves(
         lambda place: cut((place, 0, 1, 0, 0), (1, 4, 1, PAD, D)).reshape(4, PAD, D), "y"
     )
+    mlp_part = after(mlp_part, one)
+    early = depth_sum(mlp_part.transpose(1, 0, 2, 3).reshape(2, 2 * PAD, D), zh)
     one, two = ring_scatter(part_of(one), "y"), ring_scatter(part_of(two), "x")
     attn_part = depth_sum(jnp.stack([one, two]), zh)
     parts = lax.all_gather(early, ("y", "x"), axis=0, tiled=True).reshape(16, 2, PAD, D)
     grad_down = unpack(parts[:, 0], D)
     grad_up = unpack(parts[:, 1], QUART)
-    attn_part = after(attn_part, parts)
     one, two = ring_gather(attn_part[:40], "x"), ring_gather(attn_part[40:], "y")
     one, two = ring_gather(one, "y"), ring_gather(two, "x")
-    two = after(after(two, grad_up), grad_down)
     grad_qkv, grad_out = unpack_pair(one, two)
     vectors = two[:, :3, SLICE - 40, :VECTOR].transpose(1, 0, 2).reshape(-1).astype(F32)
 

time: 495 us -> 456 us (0.921)
  waiting for transfers between devices: 150 us -> 118 us
  local copies, waits for them, and re-layouts: 80 us -> 71.2 us
  other arithmetic: 48 us -> 39.9 us
  starting transfers between devices: 62.7 us -> 68.7 us
    ppermute x63, waiting for transfers between devices: 150 us -> 118 us  [permute(): return rows_major(lax.ppermute(rows_major(x), axis, pairs)).reshape(shape)]
    concatenate x11, local copies, waits for them, and re-layouts: 6.48 us -> 0.27 us  [body(): jnp.concatenate([attn_gain, attn_shift, bias_query, bias_value, bias_out,...]
    ppermute x63, starting transfers between devices: 62.6 us -> 68.5 us  [permute(): return rows_major(lax.ppermute(rows_major(x), axis, pairs)).reshape(shape)]
    unnamed x194 -> x180, local copies, waits for them, and re-layouts: 28.5 us -> 34.4 us
  transfers between devices with their start and end apart: 66 -> 66, of which waited for: 31 -> 32; matrix products, arithmetic and copies ran while one was open for 27% -> 28% of each run, Pallas kernels for 14% -> 14%
where the time goes in v5:
time: 456 us; the launch traced here: 447 us
  waiting for transfers between devices  118 us (26%)
  Pallas kernels  81.3 us (18%)
  local copies, waits for them, and re-layouts  71.2 us (16%)
  starting transfers between devices  68.7 us (15%)
  matrix products  53.2 us (12%)
  other arithmetic  39.9 us (9%)
  between operations  15.6 us (3%)
    ppermute x63, waiting for transfers between devices, permute(): return rows_major(lax.ppermute(rows_major(x), axis, pairs)).reshape(shape)  118 us
    ppermute x63, starting transfers between devices, permute(): return rows_major(lax.ppermute(rows_major(x), axis, pairs)).reshape(shape)  68.5 us
    unnamed x180, local copies, waits for them, and re-layouts  34.4 us
    pallas_call x1, Pallas kernels, attend_backward(): pl.pallas_call(attend_backward_kernel, grid=((HEADS + 1) // 2,), out_shap...  21.9 us
    pallas_call x4, Pallas kernels, weight_grad(): pl.pallas_call(functools.partial(weight_grad_kernel, len(rights) // 2, fi...  20.5 us
    pallas_call x4, Pallas kernels, assemble(): pl.pallas_call(functools.partial(assemble_kernel, spots), out_shape=jax.S...  16 us
    pallas_call x1, Pallas kernels, attend_forward(): pl.pallas_call(attend_forward_kernel, grid=((HEADS + 1) // 2,), out_shape...  14.9 us
  transfers between devices with their start and end apart: 66, of which 32 were waited for; matrix products, arithmetic and copies ran while one was open for 28% of the time, Pallas kernels for 14%

profile of v5, /device:TPU:0, one launch (start us, length us, event | category | flops | bytes accessed | tf_op | source)
XLA Modules:
  0.0 447.5 jit_solution(9924981055354734756)
XLA Ops:
  9.5 4.2 collective-permute-start
  23.6 2.8 collective-permute-done.done_ref
  31.8 7.3 %collective-permute-done.5 = bf16[64,3264]{1,0:T(8,128)(2,1)S(1)} collective-permute-done((bf16[64,3264]{1,0:T(8,128)(2,1)}, bf16[64,3264]{1,0:T(8,128)(2,1)S(1)}, u32[]{:S(2)}, u32[]{:S(2)}) %collective-permute-start.5) | collective-permute-done | bytes 417824 | tf_op jit(solution)/shard_map/ppermute | solution.py:44
  43.2 9.0 %collective-permute-done.7 = bf16[64,3264]{1,0:T(8,128)(2,1)S(1)} collective-permute-done((bf16[64,3264]{1,0:T(8,128)(2,1)}, bf16[64,3264]{1,0:T(8,128)(2,1)S(1)}, u32[]{:S(2)}, u32[]{:S(2)}) %collective-permute-start.7) | collective-permute-done | bytes 417824 | tf_op jit(solution)/shard_map/ppermute | solution.py:44
  52.8 2.6 collective-permute-start.13
  56.8 5.1 %collective-permute-done.13 = bf16[32,4352]{1,0:T(8,128)(2,1)S(1)} collective-permute-done((bf16[32,4352]{1,0:T(8,128)(2,1)}, bf16[32,4352]{1,0:T(8,128)(2,1)S(1)}, u32[]{:S(2)}, u32[]{:S(2)}) %collective-permute-start.13) | collective-permute-done | bytes 278560 | tf_op jit(solution)/shard_map/ppermute | solution.py:44
  63.5 2.5 collective-permute-start.10
  73.3 3.4 fusion.47
  81.5 5.1 %shard_map.272 = bf16[1088,3264]{1,0:T(8,128)(2,1)S(1)} custom-call(bf16[272,3264]{1,0:T(8,128)(2,1)S(1)} %copy-done.5, bf16[272,3264]{1,0:T(8,128)(2,1)} %collective-permute-done.4.refs_1_, bf16[272,3264]{1,0:T(8,128)(2,1)S(1)} %constant_dynamic-update-slice_fusion.refs_2_, bf16[272,3264]{1,0:T(8,128)(2,1)} %collective-permute-done.8.refs_3_), custom_call_target="tpu_custom_call" | custom-call | bytes 14204928 | tf_op jit(solution)/shard_map/pallas_call | solution.py:166
  86.6 2.9 copy-done
  90.2 6.3 %convolution_convert_fusion.k_ref = bf16[1024,1088]{1,0:T(8,128)(2,1)S(1)} fusion(bf16[1088,3264]{1,0:T(8,128)(2,1)} %copy-done, bf16[256,1088]{1,0:T(8,128)(2,1)} %get-tuple-element.202, bf16[256,1088]{1,0:T(8,128)(2,1)} %get-tuple-element.201, bf16[256,1088]{1,0:T(8,128)(2,1)} %get-tuple-element.200, bf16[256,1088]{1,0:T(8,128)(2,1)} %get-tuple-element.203), kind=kOutput, calls=%fused_computation.7 | convolution fusion | flops 2434334720 | bytes 7094272 | tf_op jit(solution)/shard_map/dot_general | solution.py:548
  96.5 5.4 %add_convert_fusion.v_ref = bf16[1024,1088]{1,0:T(8,128)(2,1)S(1)} fusion(f32[1088]{0:T(1024)S(1)} %add.318, bf16[1088,3264]{1,0:T(8,128)(2,1)S(1)} %bitcast.341, bf16[256,1088]{1,0:T(8,128)(2,1)S(1)} %copy-done.50, bf16[256,1088]{1,0:T(8,128)(2,1)S(1)} %copy-done.49, bf16[256,1088]{1,0:T(8,128)(2,1)S(1)} %copy-done.48, bf16[256,1088]{1,0:T(8,128)(2,1)S(1)} %copy-done.44), kind=kOutput, calls=%fused_computation.2 | convolution fusion | flops 2435448832 | bytes 7102464 | tf_op jit(solution)/shard_map/dot_general | solution.py:549
  104.0 14.9 %shard_map.273 = (bf16[256,1088]{1,0:T(8,128)(2,1)S(1)}, f32[256,1088]{1,0:T(8,128)S(1)}) custom-call(bf16[256,1088]{1,0:T(8,128)(2,1)S(1)} %fusion.4.q_ref, bf16[1024,1088]{1,0:T(8,128)(2,1)S(1)} %convolution_convert_fusion.k_ref, bf16[1024,1088]{1,0:T(8,128)(2,1)S(1)} %add_convert_fusion.v_ref, f32[256,1024]{1,0:T(8,128)S(1)} %copy-done.14), custom_call_target="tpu_custom_call" | custom-call | flops 1140850688 | bytes 6684672 | tf_op jit(solution)/shard_map/pallas_call | solution.py:239
  123.2 6.7 %collective-permute-done.11.refs_3_ = bf16[272,1088]{1,0:T(8,128)(2,1)S(1)} collective-permute-done((bf16[272,1088]{1,0:T(8,128)(2,1)}, bf16[272,1088]{1,0:T(8,128)(2,1)S(1)}, u32[]{:S(2)}, u32[]{:S(2)}) %collective-permute-start.11) | collective-permute-done | bytes 591904 | tf_op jit(solution)/shard_map/ppermute | solution.py:44
  129.8 2.3 shard_map.276
  136.2 3.8 shard_map.280
  141.1 2.5 copy-done.2
  143.6 3.2 multiply_convert_fusion.1
  146.8 4.7 %shard_map.281 = bf16[4352,1088]{1,0:T(8,128)(2,1)S(1)} custom-call(bf16[1088,1088]{1,0:T(8,128)(2,1)} %refs_0_.7, bf16[1088,1088]{1,0:T(8,128)(2,1)} %collective-permute-done.17.refs_1_, bf16[1024,1088]{1,0:T(8,128)(2,1)S(1)} %bitcast.342, bf16[64,1088]{1,0:T(8,128)(2,1)S(1)} %bitcast.354, bf16[1024,1088]{1,0:T(8,128)(2,1)S(1)} %bitcast.343, ...), custom_call_target="tpu_custom_call" | custom-call | bytes 18939904 | tf_op jit(solution)/shard_map/pallas_call | solution.py:166
  151.6 9.0 %convert_reduce_fusion = (f32[4352]{0:T(1024)}, bf16[256,4352]{1,0:T(8,128)(2,1)}) fusion(f32[256,4352]{1,0:T(8,128)S(1)} %get-tuple-element.211, bf16[4352,1088]{1,0:T(8,128)(2,1)S(1)} %shard_map.281, bf16[1,256,1088]{1,2,0:T(8,128)(2,1)S(1)} %copy-done.52), kind=kOutput, calls=%fused_computation.3 | convolution fusion | flops 2437672704 | bytes 16729088 | tf_op jit(solution)/shard_map/dot_general | solution.py:590
  169.8 4.9 %shard_map.282.refs_5_ = bf16[16,2,2,72,1088]{4,3,2,1,0:T(8,128)(2,1)} custom-call(bf16[2,256,1088]{2,1,0:T(8,128)(2,1)S(1)} %get-tuple-element.122.refs_0_, bf16[2,256,1088]{2,1,0:T(8,128)(2,1)S(1)} %bitcast.353, bf16[256,1088]{1,0:T(8,128)(2,1)S(1)} %bitcast.345, bf16[256,1088]{1,0:T(8,128)(2,1)S(1)} %bitcast.356, f32[2,12,1088]{2,1,0:T(8,128)S(1)} %broadcast_in_dim.60.refs_4_), custom_call_target="tpu_custom_call" | custom-call | flops 2424307712 | bytes 8408064 | tf_op jit(solution)/shard_map/pallas_call | solution.py:318
  174.7 7.2 %shard_map.283 = bf16[16,2,2,72,1088]{4,3,2,1,0:T(8,128)(2,1)} custom-call(bf16[2,256,272]{2,1,0:T(8,128)(2,1)S(1)} %get-tuple-element.142.refs_0_, bf16[2,256,272]{2,1,0:T(8,128)(2,1)S(1)} %bitcast.357, bf16[256,4352]{1,0:T(8,128)(2,1)} %get-tuple-element.216.refs_2_, ...), custom_call_target="tpu_custom_call", output_to_operand_aliasing={{}: (5, {})} | custom-call | flops 2424307712 | bytes 10079232 | tf_op jit(solution)/shard_map/pallas_call | solution.py:318
  181.9 8.6 %fusion.85 = (f32[1088]{0:T(1024)}, f32[256,1088]{0,1:T(8,128)}) fusion(bf16[256,4352]{1,0:T(8,128)(2,1)} %get-tuple-element.216.refs_2_, bf16[1088,4352]{1,0:T(8,128)(2,1)} %copy-done.2), kind=kOutput, calls=%fused_computation.295 | convolution fusion | flops 2424585216 | bytes 12816640 | tf_op jit(solution)/shard_map/dot_general | solution.py:603
  190.5 2.8 copy.114
  193.3 2.3 multiply_reduce_fusion
  207.9 21.9 %shard_map.285 = (bf16[256,1088]{1,0:T(8,128)(2,1)S(1)}, bf16[2,2,256,1088]{3,2,1,0:T(8,128)(2,1)S(1)}, bf16[2,2,256,1088]{3,2,1,0:T(8,128)(2,1)}) custom-call(bf16[256,1088]{1,0:T(8,128)(2,1)S(1)} %copy-done.23, bf16[1024,1088]{1,0:T(8,128)(2,1)S(1)} %copy-done.17, bf16[1024,1088]{1,0:T(8,128)(2,1)S(1)} %copy-done.19, f32[256,1024]{1,0:T(8,128)S(1)} %copy-done.15, ...), custom_call_target="tpu_custom_call" | custom-call | flops 2852126720 | bytes 13369344 | tf_op jit(solution)/shard_map/pallas_call | solution.py:266
  233.0 3.9 collective-permute-done.22
  236.9 2.6 fusion.5
  243.6 3.2 shard_map.286.refs_9_
  248.2 2.4 slice.540
  250.6 19.0 %collective-permute-done.23 = bf16[8,64,1088]{2,1,0:T(8,128)(2,1)} collective-permute-done((bf16[8,64,1088]{2,1,0:T(8,128)(2,1)}, bf16[8,64,1088]{2,1,0:T(8,128)(2,1)}, u32[]{:S(2)}, u32[]{:S(2)}) %collective-permute-start.23) | collective-permute-done | bytes 1114144 | tf_op jit(solution)/shard_map/ppermute | solution.py:44
  270.4 2.5 fusion.7
  273.1 3.3 fusion.11
  276.4 2.8 fusion.8
  279.3 3.0 fusion.74
  283.4 2.5 fusion.81
  289.2 5.2 %shard_map.290 = bf16[16,1,2,72,1088]{4,3,2,1,0:T(8,128)(2,1)} custom-call(bf16[2,256,272]{2,1,0:T(8,128)(2,1)S(1)} %get-tuple-element.137.refs_0_, bf16[2,256,272]{2,1,0:T(8,128)(2,1)} %bitcast.84.done_ref.refs_1_, bf16[256,1088]{1,0:T(8,128)(2,1)S(1)} %get-tuple-element.24.refs_2_, ...), custom_call_target="tpu_custom_call", output_to_operand_aliasing={{}: (9, {})} | custom-call | flops 1818230784 | bytes 7711744 | tf_op jit(solution)/shard_map/pallas_call | solution.py:318
  303.8 3.3 collective-permute-done.31
  307.4 4.2 collective-permute-done.38
  313.3 3.1 collective-permute-start.41
  319.3 10.4 %collective-permute-done.41 = bf16[4,72,1088]{2,1,0:T(8,128)(2,1)} collective-permute-done((bf16[4,72,1088]{2,1,0:T(8,128)(2,1)S(1)}, bf16[4,72,1088]{2,1,0:T(8,128)(2,1)}, u32[]{:S(2)}, u32[]{:S(2)}) %collective-permute-start.41) | collective-permute-done | bytes 626720 | tf_op jit(solution)/shard_map/ppermute | solution.py:44
  329.7 2.5 collective-permute-done.34
  332.2 3.1 collective-permute-done.32
  335.6 3.4 fusion.29
  340.3 2.5 collective-permute-start.61
  344.3 6.4 %collective-permute-done.60 = bf16[144,1088]{1,0:T(8,128)(2,1)S(1)} collective-permute-done((bf16[144,1088]{1,0:T(8,128)(2,1)S(1)}, bf16[144,1088]{1,0:T(8,128)(2,1)S(1)}, u32[]{:S(2)}, u32[]{:S(2)}) %collective-permute-start.60) | collective-permute-done | bytes 313376 | tf_op jit(solution)/shard_map/ppermute | solution.py:44
  350.7 3.6 collective-permute-done.61
  364.8 8.6 %fusion.3 = f32[1,256,1088]{2,1,0:T(8,128)} fusion(f32[256,1088]{1,0:T(8,128)S(1)} %copy-done.30, bf16[256,4352]{1,0:T(8,128)(2,1)} %copy-done.47, bf16[4352,1088]{1,0:T(8,128)(2,1)} %copy-done.1, f32[1088]{0:T(1024)S(1)} %add.344), kind=kOutput, calls=%fused_computation.15 | convolution fusion | flops 2424864768 | bytes 13930752 | tf_op jit(solution)/shard_map/dot_general | solution.py:572
  373.5 2.6 copy.132
  377.8 2.1 collective-permute-start.46
  382.0 2.5 collective-permute-done.46
  384.4 2.3 collective-permute-done.47
  387.2 3.3 collective-permute-start.49
  394.4 2.1 collective-permute-start.55
  396.5 2.4 collective-permute-start.54
  400.7 2.4 collective-permute-start.51
  405.3 2.1 collective-permute-done.54
  409.6 3.1 collective-permute-start.57
  412.7 7.4 %collective-permute-done.52 = bf16[4,32,1088]{2,1,0:T(8,128)(2,1)S(1)} collective-permute-done((bf16[4,32,1088]{2,1,0:T(8,128)(2,1)S(1)}, bf16[4,32,1088]{2,1,0:T(8,128)(2,1)S(1)}, u32[]{:S(2)}, u32[]{:S(2)}) %collective-permute-start.52) | collective-permute-done | bytes 278560 | tf_op jit(solution)/shard_map/ppermute | solution.py:44
  421.0 5.4 %collective-permute-done.51 = bf16[4,32,1088]{2,1,0:T(8,128)(2,1)S(1)} collective-permute-done((bf16[4,32,1088]{2,1,0:T(8,128)(2,1)S(1)}, bf16[4,32,1088]{2,1,0:T(8,128)(2,1)S(1)}, u32[]{:S(2)}, u32[]{:S(2)}) %collective-permute-start.51) | collective-permute-done | bytes 278560 | tf_op jit(solution)/shard_map/ppermute | solution.py:44
  429.8 2.6 shard_map.291
  432.4 3.0 slice_bitcast_fusion
  435.4 2.6 shard_map.294
  438.0 2.8 shard_map.293
  (454 shorter events, 130.3 us)
Async XLA Ops:
  7.3 113.7 %all-gather.3.cloned.1.call-start = ((), (), s32[]{:S(2)}) async-start(), calls=%async_computation.1 | async-start | bytes 4734976 | tf_op jit(solution)/shard_map/all_gather | solution.py:408
  7.3 71.7 %collective-permute-start.4 = (bf16[272,3264]{1,0:T(8,128)(2,1)}, bf16[272,3264]{1,0:T(8,128)(2,1)}, u32[]{:S(2)}, u32[]{:S(2)}) collective-permute-start(bf16[272,3264]{1,0:T(8,128)(2,1)} %refs_0_.4), channel_id=1, source_target_pairs={{0,1},{1,0},{2,3},{3,2},{4,5},{5,4},{6,7},{7,6},{8,9},{9,8},{10,11... | collective-permute-start | bytes 5326856 | tf_op jit(solution)/shard_map/ppermute | solution.py:44
  9.5 16.9 %collective-permute-start = (bf16[80,3264]{1,0:T(8,128)(2,1)S(1)}, bf16[80,3264]{1,0:T(8,128)(2,1)S(1)}, u32[]{:S(2)}, u32[]{:S(2)}) collective-permute-start(bf16[80,3264]{1,0:T(8,128)(2,1)S(1)} %pad_maximum_fusion.11), channel_id=1, source_target_pairs={{0,6},{6,0},{2,4},{4,2},{1,7},{7,1},{3,5},{5,3},{8,14},{14,8},{10,... | collective-permute-start | bytes 1566728 | tf_op jit(solution)/shard_map/ppermute | solution.py:44
  15.2 14.7 %collective-permute-start.3 = (bf16[272,1088]{1,0:T(8,128)(2,1)}, bf16[272,1088]{1,0:T(8,128)(2,1)S(1)}, u32[]{:S(2)}, u32[]{:S(2)}) collective-permute-start(bf16[272,1088]{1,0:T(8,128)(2,1)} %fusion.55.x_ref), channel_id=1, source_target_pairs={{0,1},{1,0},{2,3},{3,2},{4,5},{5,4},{6,7},{7,6},{8,9},{9,8},{10,11... | collective-permute-start | bytes 1775624 | tf_op jit(solution)/shard_map/ppermute | solution.py:44
  15.4 107.8 %collective-permute-start.9 = (bf16[272,1088]{1,0:T(8,128)(2,1)}, bf16[272,1088]{1,0:T(8,128)(2,1)}, u32[]{:S(2)}, u32[]{:S(2)}) collective-permute-start(bf16[272,1088]{1,0:T(8,128)(2,1)} %refs_0_.5), channel_id=1, source_target_pairs={{0,1},{1,0},{2,3},{3,2},{4,5},{5,4},{6,7},{7,6},{8,9},{9,8},{10,11... | collective-permute-start | bytes 1775624 | tf_op jit(solution)/shard_map/ppermute | solution.py:44
  15.7 120.4 %collective-permute-start.12 = (bf16[272,4352]{1,0:T(8,128)(2,1)}, bf16[272,4352]{1,0:T(8,128)(2,1)}, u32[]{:S(2)}, u32[]{:S(2)}) collective-permute-start(bf16[272,4352]{1,0:T(8,128)(2,1)} %refs_0_.6), channel_id=1, source_target_pairs={{0,1},{1,0},{2,3},{3,2},{4,5},{5,4},{6,7},{7,6},{8,9},{9,8},{10,11... | collective-permute-start | bytes 7102472 | tf_op jit(solution)/shard_map/ppermute | solution.py:44
  27.3 11.8 %collective-permute-start.5 = (bf16[64,3264]{1,0:T(8,128)(2,1)}, bf16[64,3264]{1,0:T(8,128)(2,1)S(1)}, u32[]{:S(2)}, u32[]{:S(2)}) collective-permute-start(bf16[64,3264]{1,0:T(8,128)(2,1)} %slice.494), channel_id=1, source_target_pairs={{0,8},{8,0},{16,24},{24,16},{1,9},{9,1},{17,25},{25,17},{2,10},{10... | collective-permute-start | bytes 1253384 | tf_op jit(solution)/shard_map/ppermute | solution.py:44
  29.9 11.7 %collective-permute-start.6 = (bf16[64,3264]{1,0:T(8,128)(2,1)}, bf16[64,3264]{1,0:T(8,128)(2,1)}, u32[]{:S(2)}, u32[]{:S(2)}) collective-permute-start(bf16[64,3264]{1,0:T(8,128)(2,1)} %slice.494), channel_id=1, source_target_pairs={{0,32},{32,0},{64,96},{96,64},{1,33},{33,1},{65,97},{97,65},{2,34}... | collective-permute-start | bytes 1253384 | tf_op jit(solution)/shard_map/ppermute | solution.py:44
  39.1 23.6 %collective-permute-start.1 = (bf16[272,1088]{1,0:T(8,128)(2,1)}, bf16[272,1088]{1,0:T(8,128)(2,1)S(1)}, u32[]{:S(2)}, u32[]{:S(2)}) collective-permute-start(bf16[272,1088]{1,0:T(8,128)(2,1)} %shard_map.271), channel_id=1, source_target_pairs={{0,2},{2,0},{1,3},{3,1},{4,6},{6,4},{5,7},{7,5},{8,10},{10,8},{9,1... | collective-permute-start | bytes 1775624 | tf_op jit(solution)/shard_map/ppermute | solution.py:44
  41.6 10.6 %collective-permute-start.7 = (bf16[64,3264]{1,0:T(8,128)(2,1)}, bf16[64,3264]{1,0:T(8,128)(2,1)S(1)}, u32[]{:S(2)}, u32[]{:S(2)}) collective-permute-start(bf16[64,3264]{1,0:T(8,128)(2,1)} %collective-permute-done.6), channel_id=1, source_target_pairs={{0,8},{8,0},{16,24},{24,16},{1,9},{9,1},{17,25},{25,17},{2,10},{10... | collective-permute-start | bytes 1253384 | tf_op jit(solution)/shard_map/ppermute | solution.py:44
  52.8 9.1 %collective-permute-start.13 = (bf16[32,4352]{1,0:T(8,128)(2,1)}, bf16[32,4352]{1,0:T(8,128)(2,1)S(1)}, u32[]{:S(2)}, u32[]{:S(2)}) collective-permute-start(bf16[32,4352]{1,0:T(8,128)(2,1)} %shard_map.277), channel_id=1, source_target_pairs={{0,6},{6,0},{2,4},{4,2},{1,7},{7,1},{3,5},{5,3},{8,14},{14,8},{10,... | collective-permute-start | bytes 835592 | tf_op jit(solution)/shard_map/ppermute | solution.py:44
  62.6 276.4 %reduce-scatter.2.cloned.1.call-start = ((), (), s32[]{:S(2)}) async-start(), calls=%async_computation.2 | async-start | bytes 11280384 | tf_op jit(solution)/shard_map/reduce_scatter | solution.py:599
  63.5 26.6 %collective-permute-start.10 = (bf16[272,1088]{1,0:T(8,128)(2,1)}, bf16[272,1088]{1,0:T(8,128)(2,1)}, u32[]{:S(2)}, u32[]{:S(2)}) collective-permute-start(bf16[272,1088]{1,0:T(8,128)(2,1)} %shard_map.274), channel_id=1, source_target_pairs={{0,6},{6,0},{2,4},{4,2},{1,7},{7,1},{3,5},{5,3},{8,14},{14,8},{10,... | collective-permute-start | bytes 1775624 | tf_op jit(solution)/shard_map/ppermute | solution.py:44
  66.0 2.6 collective-permute-start.2
  68.7 8.5 %collective-permute-start.8 = (bf16[272,3264]{1,0:T(8,128)(2,1)S(1)}, bf16[272,3264]{1,0:T(8,128)(2,1)}, u32[]{:S(2)}, u32[]{:S(2)}) collective-permute-start(bf16[272,3264]{1,0:T(8,128)(2,1)S(1)} %constant_dynamic-update-slice_fusion.refs_2_), channel_id=1, source_target_pairs={{0,1},{1,0},{2,3},{3,2},{4,5},{5,4},{6,7},{7,6},{8,9},{9,8},{10,11... | collective-permute-start | bytes 5326856 | tf_op jit(solution)/shard_map/ppermute | solution.py:44
  77.2 69.6 %collective-permute-start.17 = (bf16[1088,1088]{1,0:T(8,128)(2,1)}, bf16[1088,1088]{1,0:T(8,128)(2,1)}, u32[]{:S(2)}, u32[]{:S(2)}) collective-permute-start(bf16[1088,1088]{1,0:T(8,128)(2,1)} %refs_0_.7), channel_id=1, source_target_pairs={{0,1},{1,0},{2,3},{3,2},{4,5},{5,4},{6,7},{7,6},{8,9},{9,8},{10,11... | collective-permute-start | bytes 7102472 | tf_op jit(solution)/shard_map/ppermute | solution.py:44
  79.0 41.8 %collective-permute-start.14 = (bf16[32,4352]{1,0:T(8,128)(2,1)}, bf16[32,4352]{1,0:T(8,128)(2,1)S(1)}, u32[]{:S(2)}, u32[]{:S(2)}) collective-permute-start(bf16[32,4352]{1,0:T(8,128)(2,1)} %shard_map.279), channel_id=1, source_target_pairs={{0,6},{6,0},{2,4},{4,2},{1,7},{7,1},{3,5},{5,3},{8,14},{14,8},{10,... | collective-permute-start | bytes 835592 | tf_op jit(solution)/shard_map/ppermute | solution.py:44
  121.0 15.0 %collective-permute-start.15 = (bf16[512,4352]{1,0:T(8,128)(2,1)}, bf16[512,4352]{1,0:T(8,128)(2,1)S(1)}, u32[]{:S(2)}, u32[]{:S(2)}) collective-permute-start(bf16[512,4352]{1,0:T(8,128)(2,1)} %shard_map.278), channel_id=1, source_target_pairs={{0,1},{1,0},{2,3},{3,2},{4,5},{5,4},{6,7},{7,6},{8,9},{9,8},{10,11... | collective-permute-start | bytes 13369352 | tf_op jit(solution)/shard_map/ppermute | solution.py:44
  122.4 7.5 %collective-permute-start.11 = (bf16[272,1088]{1,0:T(8,128)(2,1)}, bf16[272,1088]{1,0:T(8,128)(2,1)S(1)}, u32[]{:S(2)}, u32[]{:S(2)}) collective-permute-start(bf16[272,1088]{1,0:T(8,128)(2,1)} %shard_map.275.refs_2_), channel_id=1, source_target_pairs={{0,1},{1,0},{2,3},{3,2},{4,5},{5,4},{6,7},{7,6},{8,9},{9,8},{10,11... | collective-permute-start | bytes 1775624 | tf_op jit(solution)/shard_map/ppermute | solution.py:44
  160.6 14.1 %collective-permute-start.19 = (bf16[256,4352]{1,0:T(8,128)(2,1)}, bf16[256,4352]{1,0:T(8,128)(2,1)}, u32[]{:S(2)}, u32[]{:S(2)}) collective-permute-start(bf16[256,4352]{1,0:T(8,128)(2,1)} %get-tuple-element.216.refs_2_), channel_id=1, source_target_pairs={{0,1},{1,0},{2,3},{3,2},{4,5},{5,4},{6,7},{7,6},{8,9},{9,8},{10,11... | collective-permute-start | bytes 6684680 | tf_op jit(solution)/shard_map/ppermute | solution.py:44
  163.1 4.4 collective-permute-start.20
  164.6 2.9 collective-permute-start.21
  166.7 7.9 %collective-permute-start.18 = (bf16[8,64,272]{2,1,0:T(8,128)(2,1)S(1)}, bf16[8,64,272]{2,1,0:T(8,128)(2,1)S(1)}, u32[]{:S(2)}, u32[]{:S(2)}) collective-permute-start(bf16[8,64,272]{2,1,0:T(8,128)(2,1)S(1)} %bitcast.378), channel_id=1, source_target_pairs={{0,1},{1,0},{2,3},{3,2},{4,5},{5,4},{6,7},{7,6},{8,9},{9,8},{10,11... | collective-permute-start | bytes 835592 | tf_op jit(solution)/shard_map/ppermute | solution.py:44
  181.9 250.5 %all-gather.5.cloned.1.call-start = ((), (), s32[]{:S(2)}) async-start(), calls=%async_computation.3 | async-start | bytes 5640192 | tf_op jit(solution)/shard_map/all_gather | solution.py:687
  231.1 5.8 %collective-permute-start.22 = (bf16[16,64,1088]{2,1,0:T(8,128)(2,1)}, bf16[16,64,1088]{2,1,0:T(8,128)(2,1)}, u32[]{:S(2)}, u32[]{:S(2)}) collective-permute-start(bf16[16,64,1088]{2,1,0:T(8,128)(2,1)} %bitcast.63), channel_id=1, source_target_pairs={{0,1},{1,0},{2,3},{3,2},{4,5},{5,4},{6,7},{7,6},{8,9},{9,8},{10,11... | collective-permute-start | bytes 6684680 | tf_op jit(solution)/shard_map/ppermute | solution.py:44
  231.6 12.0 %collective-permute-start.25 = (bf16[4,64,1088]{2,1,0:T(8,128)(2,1)S(1)}, bf16[4,64,1088]{2,1,0:T(8,128)(2,1)}, u32[]{:S(2)}, u32[]{:S(2)}) collective-permute-start(bf16[4,64,1088]{2,1,0:T(8,128)(2,1)S(1)} %bitcast.350), channel_id=1, source_target_pairs={{0,1},{1,0},{2,3},{3,2},{4,5},{5,4},{6,7},{7,6},{8,9},{9,8},{10,11... | collective-permute-start | bytes 1671176 | tf_op jit(solution)/shard_map/ppermute | solution.py:44
  239.5 30.1 %collective-permute-start.23 = (bf16[8,64,1088]{2,1,0:T(8,128)(2,1)}, bf16[8,64,1088]{2,1,0:T(8,128)(2,1)}, u32[]{:S(2)}, u32[]{:S(2)}) collective-permute-start(bf16[8,64,1088]{2,1,0:T(8,128)(2,1)} %fusion.5), channel_id=1, source_target_pairs={{0,2},{2,0},{1,3},{3,1},{4,6},{6,4},{5,7},{7,5},{8,10},{10,8},{9,1... | collective-permute-start | bytes 3342344 | tf_op jit(solution)/shard_map/ppermute | solution.py:44
  240.7 2.8 collective-permute-start.24
  241.1 28.5 %collective-permute-start.26 = (bf16[4,64,1088]{2,1,0:T(8,128)(2,1)S(1)}, bf16[4,64,1088]{2,1,0:T(8,128)(2,1)S(1)}, u32[]{:S(2)}, u32[]{:S(2)}) collective-permute-start(bf16[4,64,1088]{2,1,0:T(8,128)(2,1)S(1)} %bitcast.348), channel_id=1, source_target_pairs={{0,1},{1,0},{2,3},{3,2},{4,5},{5,4},{6,7},{7,6},{8,9},{9,8},{10,11... | collective-permute-start | bytes 1671176 | tf_op jit(solution)/shard_map/ppermute | solution.py:44
  242.8 27.7 %collective-permute-start.27 = (bf16[8,64,272]{2,1,0:T(8,128)(2,1)}, bf16[8,64,272]{2,1,0:T(8,128)(2,1)}, u32[]{:S(2)}, u32[]{:S(2)}) collective-permute-start(bf16[8,64,272]{2,1,0:T(8,128)(2,1)} %bitcast.83), channel_id=1, source_target_pairs={{0,1},{1,0},{2,3},{3,2},{4,5},{5,4},{6,7},{7,6},{8,9},{9,8},{10,11... | collective-permute-start | bytes 835592 | tf_op jit(solution)/shard_map/ppermute | solution.py:44
  283.4 3.1 collective-permute-start.30
  286.4 2.8 collective-permute-start.28
  295.8 11.4 %collective-permute-start.31 = (bf16[2,72,1088]{2,1,0:T(8,128)(2,1)S(1)}, bf16[2,72,1088]{2,1,0:T(8,128)(2,1)S(1)}, u32[]{:S(2)}, u32[]{:S(2)}) collective-permute-start(bf16[2,72,1088]{2,1,0:T(8,128)(2,1)S(1)} %get-tuple-element.99), channel_id=1, source_target_pairs={{0,8},{8,16},{16,24},{24,0},{1,9},{9,17},{17,25},{25,1},{2,10},{10... | collective-permute-start | bytes 940040 | tf_op jit(solution)/shard_map/ppermute | solution.py:44
  297.6 9.8 %collective-permute-start.33 = (bf16[2,72,1088]{2,1,0:T(8,128)(2,1)S(1)}, bf16[2,72,1088]{2,1,0:T(8,128)(2,1)S(1)}, u32[]{:S(2)}, u32[]{:S(2)}) collective-permute-start(bf16[2,72,1088]{2,1,0:T(8,128)(2,1)S(1)} %get-tuple-element.101), channel_id=1, source_target_pairs={{0,24},{8,0},{16,8},{24,16},{1,25},{9,1},{17,9},{25,17},{2,26},{10... | collective-permute-start | bytes 940040 | tf_op jit(solution)/shard_map/ppermute | solution.py:44
  300.5 11.1 %collective-permute-start.38 = (bf16[2,72,1088]{2,1,0:T(8,128)(2,1)S(1)}, bf16[2,72,1088]{2,1,0:T(8,128)(2,1)S(1)}, u32[]{:S(2)}, u32[]{:S(2)}) collective-permute-start(bf16[2,72,1088]{2,1,0:T(8,128)(2,1)S(1)} %get-tuple-element.95), channel_id=1, source_target_pairs={{0,32},{32,64},{64,96},{96,0},{1,33},{33,65},{65,97},{97,1},{2,34}... | collective-permute-start | bytes 940040 | tf_op jit(solution)/shard_map/ppermute | solution.py:44
  302.3 9.3 %collective-permute-start.40 = (bf16[2,72,1088]{2,1,0:T(8,128)(2,1)S(1)}, bf16[2,72,1088]{2,1,0:T(8,128)(2,1)S(1)}, u32[]{:S(2)}, u32[]{:S(2)}) collective-permute-start(bf16[2,72,1088]{2,1,0:T(8,128)(2,1)S(1)} %get-tuple-element.98), channel_id=1, source_target_pairs={{0,96},{32,0},{64,32},{96,64},{1,97},{33,1},{65,33},{97,65},{2,98}... | collective-permute-start | bytes 940040 | tf_op jit(solution)/shard_map/ppermute | solution.py:44
  313.3 16.4 %collective-permute-start.41 = (bf16[4,72,1088]{2,1,0:T(8,128)(2,1)S(1)}, bf16[4,72,1088]{2,1,0:T(8,128)(2,1)}, u32[]{:S(2)}, u32[]{:S(2)}) collective-permute-start(bf16[4,72,1088]{2,1,0:T(8,128)(2,1)S(1)} %pad_maximum_fusion.10), channel_id=1, source_target_pairs={{0,96},{32,0},{64,32},{96,64},{1,97},{33,1},{65,33},{97,65},{2,98}... | collective-permute-start | bytes 1880072 | tf_op jit(solution)/shard_map/ppermute | solution.py:44
  316.5 15.7 %collective-permute-start.34 = (bf16[4,72,1088]{2,1,0:T(8,128)(2,1)S(1)}, bf16[4,72,1088]{2,1,0:T(8,128)(2,1)}, u32[]{:S(2)}, u32[]{:S(2)}) collective-permute-start(bf16[4,72,1088]{2,1,0:T(8,128)(2,1)S(1)} %pad_maximum_fusion.8), channel_id=1, source_target_pairs={{0,24},{8,0},{16,8},{24,16},{1,25},{9,1},{17,9},{25,17},{2,26},{10... | collective-permute-start | bytes 1880072 | tf_op jit(solution)/shard_map/ppermute | solution.py:44
  318.3 17.0 %collective-permute-start.32 = (bf16[4,72,1088]{2,1,0:T(8,128)(2,1)S(1)}, bf16[4,72,1088]{2,1,0:T(8,128)(2,1)}, u32[]{:S(2)}, u32[]{:S(2)}) collective-permute-start(bf16[4,72,1088]{2,1,0:T(8,128)(2,1)S(1)} %pad_maximum_fusion.7), channel_id=1, source_target_pairs={{0,8},{8,16},{16,24},{24,0},{1,9},{9,17},{17,25},{25,1},{2,10},{10... | collective-permute-start | bytes 1880072 | tf_op jit(solution)/shard_map/ppermute | solution.py:44
  319.2 16.4 %collective-permute-start.39 = (bf16[4,72,1088]{2,1,0:T(8,128)(2,1)S(1)}, bf16[4,72,1088]{2,1,0:T(8,128)(2,1)}, u32[]{:S(2)}, u32[]{:S(2)}) collective-permute-start(bf16[4,72,1088]{2,1,0:T(8,128)(2,1)S(1)} %pad_maximum_fusion.9), channel_id=1, source_target_pairs={{0,32},{32,64},{64,96},{96,0},{1,33},{33,65},{65,97},{97,1},{2,34}... | collective-permute-start | bytes 1880072 | tf_op jit(solution)/shard_map/ppermute | solution.py:44
  340.1 10.6 %collective-permute-start.60 = (bf16[144,1088]{1,0:T(8,128)(2,1)S(1)}, bf16[144,1088]{1,0:T(8,128)(2,1)S(1)}, u32[]{:S(2)}, u32[]{:S(2)}) collective-permute-start(bf16[144,1088]{1,0:T(8,128)(2,1)S(1)} %bitcast.377), channel_id=1, source_target_pairs={{0,4},{4,0},{1,5},{5,1},{2,6},{6,2},{3,7},{7,3},{8,12},{12,8},{9,1... | collective-permute-start | bytes 940040 | tf_op jit(solution)/shard_map/ppermute | solution.py:44
  340.3 14.0 %collective-permute-start.61 = (bf16[144,1088]{1,0:T(8,128)(2,1)S(1)}, bf16[144,1088]{1,0:T(8,128)(2,1)S(1)}, u32[]{:S(2)}, u32[]{:S(2)}) collective-permute-start(bf16[144,1088]{1,0:T(8,128)(2,1)S(1)} %bitcast.379), channel_id=1, source_target_pairs={{0,6},{6,0},{2,4},{4,2},{1,7},{7,1},{3,5},{5,3},{8,14},{14,8},{10,... | collective-permute-start | bytes 940040 | tf_op jit(solution)/shard_map/ppermute | solution.py:44
  342.8 13.3 %collective-permute-start.62 = (bf16[144,1088]{1,0:T(8,128)(2,1)S(1)}, bf16[144,1088]{1,0:T(8,128)(2,1)S(1)}, u32[]{:S(2)}, u32[]{:S(2)}) collective-permute-start(bf16[144,1088]{1,0:T(8,128)(2,1)S(1)} %bitcast.380), channel_id=1, source_target_pairs={{0,2},{2,0},{1,3},{3,1},{4,6},{6,4},{5,7},{7,5},{8,10},{10,8},{9,1... | collective-permute-start | bytes 940040 | tf_op jit(solution)/shard_map/ppermute | solution.py:44
  358.0 6.8 %collective-permute-start.42 = (bf16[72,1088]{1,0:T(8,128)(2,1)S(1)}, bf16[72,1088]{1,0:T(8,128)(2,1)S(1)}, u32[]{:S(2)}, u32[]{:S(2)}) collective-permute-start(bf16[72,1088]{1,0:T(8,128)(2,1)S(1)} %get-tuple-element.145), channel_id=1, source_target_pairs={{0,16},{8,24},{16,0},{24,8},{1,17},{9,25},{17,1},{25,9},{2,18},{10... | collective-permute-start | bytes 470024 | tf_op jit(solution)/shard_map/ppermute | solution.py:44
  359.7 16.5 %collective-permute-start.44 = (bf16[72,1088]{1,0:T(8,128)(2,1)}, bf16[72,1088]{1,0:T(8,128)(2,1)}, u32[]{:S(2)}, u32[]{:S(2)}) collective-permute-start(bf16[72,1088]{1,0:T(8,128)(2,1)} %get-tuple-element.146), channel_id=1, source_target_pairs={{0,24},{8,0},{16,8},{24,16},{1,25},{9,1},{17,9},{25,17},{2,26},{10... | collective-permute-start | bytes 470024 | tf_op jit(solution)/shard_map/ppermute | solution.py:44
  361.1 15.1 %collective-permute-start.43 = (bf16[72,1088]{1,0:T(8,128)(2,1)}, bf16[72,1088]{1,0:T(8,128)(2,1)}, u32[]{:S(2)}, u32[]{:S(2)}) collective-permute-start(bf16[72,1088]{1,0:T(8,128)(2,1)} %get-tuple-element.147), channel_id=1, source_target_pairs={{0,8},{8,16},{16,24},{24,0},{1,9},{9,17},{17,25},{25,1},{2,10},{10... | collective-permute-start | bytes 470024 | tf_op jit(solution)/shard_map/ppermute | solution.py:44
  362.5 13.7 %collective-permute-start.35 = (bf16[72,1088]{1,0:T(8,128)(2,1)}, bf16[72,1088]{1,0:T(8,128)(2,1)}, u32[]{:S(2)}, u32[]{:S(2)}) collective-permute-start(bf16[72,1088]{1,0:T(8,128)(2,1)} %get-tuple-element.148), channel_id=1, source_target_pairs={{0,64},{32,96},{64,0},{96,32},{1,65},{33,97},{65,1},{97,33},{2,66}... | collective-permute-start | bytes 470024 | tf_op jit(solution)/shard_map/ppermute | solution.py:44
  362.5 13.7 %collective-permute-start.37 = (bf16[72,1088]{1,0:T(8,128)(2,1)}, bf16[72,1088]{1,0:T(8,128)(2,1)}, u32[]{:S(2)}, u32[]{:S(2)}) collective-permute-start(bf16[72,1088]{1,0:T(8,128)(2,1)} %get-tuple-element.149), channel_id=1, source_target_pairs={{0,96},{32,0},{64,32},{96,64},{1,97},{33,1},{65,33},{97,65},{2,98}... | collective-permute-start | bytes 470024 | tf_op jit(solution)/shard_map/ppermute | solution.py:44
  364.8 11.3 %collective-permute-start.36 = (bf16[72,1088]{1,0:T(8,128)(2,1)}, bf16[72,1088]{1,0:T(8,128)(2,1)}, u32[]{:S(2)}, u32[]{:S(2)}) collective-permute-start(bf16[72,1088]{1,0:T(8,128)(2,1)} %get-tuple-element.150), channel_id=1, source_target_pairs={{0,32},{32,64},{64,96},{96,0},{1,33},{33,65},{65,97},{97,1},{2,34}... | collective-permute-start | bytes 470024 | tf_op jit(solution)/shard_map/ppermute | solution.py:44
  377.8 6.6 %collective-permute-start.46 = (bf16[72,1088]{1,0:T(8,128)(2,1)S(1)}, bf16[72,1088]{1,0:T(8,128)(2,1)S(1)}, u32[]{:S(2)}, u32[]{:S(2)}) collective-permute-start(bf16[72,1088]{1,0:T(8,128)(2,1)S(1)} %broadcast_select_fusion.10), channel_id=1, source_target_pairs={{0,6},{6,0},{2,4},{4,2},{1,7},{7,1},{3,5},{5,3},{8,14},{14,8},{10,... | collective-permute-start | bytes 470024 | tf_op jit(solution)/shard_map/ppermute | solution.py:44
  379.9 6.8 %collective-permute-start.47 = (bf16[72,1088]{1,0:T(8,128)(2,1)S(1)}, bf16[72,1088]{1,0:T(8,128)(2,1)S(1)}, u32[]{:S(2)}, u32[]{:S(2)}) collective-permute-start(bf16[72,1088]{1,0:T(8,128)(2,1)S(1)} %broadcast_select_fusion.10), channel_id=1, source_target_pairs={{0,2},{2,0},{1,3},{3,1},{4,6},{6,4},{5,7},{7,5},{8,10},{10,8},{9,1... | collective-permute-start | bytes 470024 | tf_op jit(solution)/shard_map/ppermute | solution.py:44
  380.2 6.9 %collective-permute-start.45 = (bf16[72,1088]{1,0:T(8,128)(2,1)S(1)}, bf16[72,1088]{1,0:T(8,128)(2,1)S(1)}, u32[]{:S(2)}, u32[]{:S(2)}) collective-permute-start(bf16[72,1088]{1,0:T(8,128)(2,1)S(1)} %get-tuple-element.80), channel_id=1, source_target_pairs={{0,4},{4,0},{1,5},{5,1},{2,6},{6,2},{3,7},{7,3},{8,12},{12,8},{9,1... | collective-permute-start | bytes 470024 | tf_op jit(solution)/shard_map/ppermute | solution.py:44
  387.2 11.8 %collective-permute-start.49 = (bf16[32,1088]{1,0:T(8,128)(2,1)S(1)}, bf16[32,1088]{1,0:T(8,128)(2,1)S(1)}, u32[]{:S(2)}, u32[]{:S(2)}) collective-permute-start(bf16[32,1088]{1,0:T(8,128)(2,1)S(1)} %slice.549), channel_id=1, source_target_pairs={{0,64},{32,96},{64,0},{96,32},{1,65},{33,97},{65,1},{97,33},{2,66}... | collective-permute-start | bytes 208904 | tf_op jit(solution)/shard_map/ppermute | solution.py:44
  390.5 8.5 %collective-permute-start.48 = (bf16[32,1088]{1,0:T(8,128)(2,1)S(1)}, bf16[32,1088]{1,0:T(8,128)(2,1)S(1)}, u32[]{:S(2)}, u32[]{:S(2)}) collective-permute-start(bf16[32,1088]{1,0:T(8,128)(2,1)S(1)} %slice.549), channel_id=1, source_target_pairs={{0,96},{32,0},{64,32},{96,64},{1,97},{33,1},{65,33},{97,65},{2,98}... | collective-permute-start | bytes 208904 | tf_op jit(solution)/shard_map/ppermute | solution.py:44
  391.2 7.9 %collective-permute-start.50 = (bf16[32,1088]{1,0:T(8,128)(2,1)S(1)}, bf16[32,1088]{1,0:T(8,128)(2,1)S(1)}, u32[]{:S(2)}, u32[]{:S(2)}) collective-permute-start(bf16[32,1088]{1,0:T(8,128)(2,1)S(1)} %slice.549), channel_id=1, source_target_pairs={{0,32},{32,64},{64,96},{96,0},{1,33},{33,65},{65,97},{97,1},{2,34}... | collective-permute-start | bytes 208904 | tf_op jit(solution)/shard_map/ppermute | solution.py:44
  394.4 9.1 %collective-permute-start.55 = (bf16[40,1088]{1,0:T(8,128)(2,1)S(1)}, bf16[40,1088]{1,0:T(8,128)(2,1)S(1)}, u32[]{:S(2)}, u32[]{:S(2)}) collective-permute-start(bf16[40,1088]{1,0:T(8,128)(2,1)S(1)} %slice.553), channel_id=1, source_target_pairs={{0,16},{8,24},{16,0},{24,8},{1,17},{9,25},{17,1},{25,9},{2,18},{10... | collective-permute-start | bytes 261128 | tf_op jit(solution)/shard_map/ppermute | solution.py:44
  396.5 10.9 %collective-permute-start.54 = (bf16[40,1088]{1,0:T(8,128)(2,1)S(1)}, bf16[40,1088]{1,0:T(8,128)(2,1)S(1)}, u32[]{:S(2)}, u32[]{:S(2)}) collective-permute-start(bf16[40,1088]{1,0:T(8,128)(2,1)S(1)} %slice.553), channel_id=1, source_target_pairs={{0,24},{8,0},{16,8},{24,16},{1,25},{9,1},{17,9},{25,17},{2,26},{10... | collective-permute-start | bytes 261128 | tf_op jit(solution)/shard_map/ppermute | solution.py:44
  399.0 10.0 %collective-permute-start.56 = (bf16[40,1088]{1,0:T(8,128)(2,1)S(1)}, bf16[40,1088]{1,0:T(8,128)(2,1)S(1)}, u32[]{:S(2)}, u32[]{:S(2)}) collective-permute-start(bf16[40,1088]{1,0:T(8,128)(2,1)S(1)} %slice.553), channel_id=1, source_target_pairs={{0,8},{8,16},{16,24},{24,0},{1,9},{9,17},{17,25},{25,1},{2,10},{10... | collective-permute-start | bytes 261128 | tf_op jit(solution)/shard_map/ppermute | solution.py:44
  399.1 20.9 %collective-permute-start.52 = (bf16[4,32,1088]{2,1,0:T(8,128)(2,1)S(1)}, bf16[4,32,1088]{2,1,0:T(8,128)(2,1)S(1)}, u32[]{:S(2)}, u32[]{:S(2)}) collective-permute-start(bf16[4,32,1088]{2,1,0:T(8,128)(2,1)S(1)} %pad_maximum_fusion.21), channel_id=1, source_target_pairs={{0,16},{8,24},{16,0},{24,8},{1,17},{9,25},{17,1},{25,9},{2,18},{10... | collective-permute-start | bytes 835592 | tf_op jit(solution)/shard_map/ppermute | solution.py:44
  400.7 25.7 %collective-permute-start.51 = (bf16[4,32,1088]{2,1,0:T(8,128)(2,1)S(1)}, bf16[4,32,1088]{2,1,0:T(8,128)(2,1)S(1)}, u32[]{:S(2)}, u32[]{:S(2)}) collective-permute-start(bf16[4,32,1088]{2,1,0:T(8,128)(2,1)S(1)} %pad_maximum_fusion.21), channel_id=1, source_target_pairs={{0,24},{8,0},{16,8},{24,16},{1,25},{9,1},{17,9},{25,17},{2,26},{10... | collective-permute-start | bytes 835592 | tf_op jit(solution)/shard_map/ppermute | solution.py:44
  403.5 22.9 %collective-permute-start.53 = (bf16[4,32,1088]{2,1,0:T(8,128)(2,1)S(1)}, bf16[4,32,1088]{2,1,0:T(8,128)(2,1)S(1)}, u32[]{:S(2)}, u32[]{:S(2)}) collective-permute-start(bf16[4,32,1088]{2,1,0:T(8,128)(2,1)S(1)} %pad_maximum_fusion.21), channel_id=1, source_target_pairs={{0,8},{8,16},{16,24},{24,0},{1,9},{9,17},{17,25},{25,1},{2,10},{10... | collective-permute-start | bytes 835592 | tf_op jit(solution)/shard_map/ppermute | solution.py:44
  409.2 19.2 %collective-permute-start.58 = (bf16[4,40,1088]{2,1,0:T(8,128)(2,1)S(1)}, bf16[4,40,1088]{2,1,0:T(8,128)(2,1)S(1)}, u32[]{:S(2)}, u32[]{:S(2)}) collective-permute-start(bf16[4,40,1088]{2,1,0:T(8,128)(2,1)S(1)} %pad_maximum_fusion.20), channel_id=1, source_target_pairs={{0,64},{32,96},{64,0},{96,32},{1,65},{33,97},{65,1},{97,33},{2,66}... | collective-permute-start | bytes 1044488 | tf_op jit(solution)/shard_map/ppermute | solution.py:44
  409.6 18.8 %collective-permute-start.57 = (bf16[4,40,1088]{2,1,0:T(8,128)(2,1)S(1)}, bf16[4,40,1088]{2,1,0:T(8,128)(2,1)S(1)}, u32[]{:S(2)}, u32[]{:S(2)}) collective-permute-start(bf16[4,40,1088]{2,1,0:T(8,128)(2,1)S(1)} %pad_maximum_fusion.20), channel_id=1, source_target_pairs={{0,96},{32,0},{64,32},{96,64},{1,97},{33,1},{65,33},{97,65},{2,98}... | collective-permute-start | bytes 1044488 | tf_op jit(solution)/shard_map/ppermute | solution.py:44
  420.1 9.1 %collective-permute-start.59 = (bf16[4,40,1088]{2,1,0:T(8,128)(2,1)S(1)}, bf16[4,40,1088]{2,1,0:T(8,128)(2,1)S(1)}, u32[]{:S(2)}, u32[]{:S(2)}) collective-permute-start(bf16[4,40,1088]{2,1,0:T(8,128)(2,1)S(1)} %pad_maximum_fusion.20), channel_id=1, source_target_pairs={{0,32},{32,64},{64,96},{96,0},{1,33},{33,65},{65,97},{97,1},{2,34}... | collective-permute-start | bytes 1044488 | tf_op jit(solution)/shard_map/ppermute | solution.py:44
  (88 other events, 577.6 us)
Sparse Core Ops, SparseCore 0:
  62.7 53.6 all-gather.2
  182.0 90.9 reduce-scatter.1
  357.2 70.8 all-gather.4
